TPU v7x, 32 devices: a whole 2x2x4 slice. The times are simulated.
32 devices in a mesh: grp: 2 (over y), param: 4 (over z), ex: 4 (over x, core).
Axes of the slice: x: 2, y: 2, z: 4, core: 2. Of those that a mesh axis runs over, the one named last changes fastest.
Arguments:
- activations: bfloat16 [8, 256, 4096], P(('grp', 'ex'), None, 'param'), parts along dimension 0, may hold values from -96 to 96
- backprops: bfloat16 [8, 256, 4096], P(('grp', 'ex'), None, 'param'), parts along dimension 0, may hold values from -96 to 96
- block_counters: int32 [2, 4], P(None, 'param'), may hold values from 0 to 999999
Outputs:
- features: float32 [8, 2048], P(('grp', 'ex'), 'param'), parts along dimension 0
- grad_norm: float32 [8], P(('grp', 'ex')), parts along dimension 0
There are 2 independent parts, one for each index of `grp`. A program takes and returns all parts, laid end to end along the dimension named above; an argument that names none is the same for every part. Nothing has to cross between parts.
All inputs are finite; a program needn't handle non-finite values.
Results may differ from a plain program's by a relative error of at most 0.006.
Values may be sent and summed in bfloat16 or wider, within the bound.
No kernel may reach another device: no remote copies, remote signals or barrier semaphores. Data moves between devices by JAX's collectives and lax.ppermute only.
A program may use at most 64 MiB of HBM per device.

v0:
```python
import jax
import jax.numpy as jnp
from jax import lax
from jax.sharding import PartitionSpec as P

K = 2048


mix_factor = 73244475
epsilon = 1e-06
widest_block = 1024


def scramble(hashed):
    hashed = jnp.bitwise_xor(hashed, lax.shift_right_logical(hashed, jnp.int32(16)))
    hashed = hashed * mix_factor
    hashed = jnp.bitwise_xor(hashed, lax.shift_right_logical(hashed, jnp.int32(16)))
    hashed = hashed * mix_factor
    return jnp.bitwise_xor(hashed, lax.shift_right_logical(hashed, jnp.int32(16)))


def gaussian_block(stream, row_ids, col_ids):
    hashed = stream * 668265261 + row_ids[:, None] * 374761393 + col_ids[None, :] * 1103515245
    hashed = scramble(hashed)
    total_bytes = jnp.bitwise_and(hashed, 255)
    for shift_bits in (8, 16, 24):
        total_bytes = total_bytes + jnp.bitwise_and(
            lax.shift_right_logical(hashed, jnp.int32(shift_bits)), 255
        )
    return ((total_bytes - 510).astype(jnp.float32) * (1.0 / 128.0)).astype(jnp.bfloat16)


def on_device(activations, backprops, block_counters):
    row_block = activations.shape[2]
    proj_cols = lax.iota(jnp.int32, K)
    row_ids = lax.axis_index("param") * row_block + lax.iota(jnp.int32, row_block)
    row_proj = gaussian_block(block_counters[0, 0], row_ids, proj_cols).astype(jnp.float32)
    col_stream = block_counters[1, 0]

    def absorb(carry, acts_rows, part_cols, col_ids):
        running, squares = carry
        grad = jnp.einsum(
            "etr,etw->erw", acts_rows, part_cols, preferred_element_type=jnp.float32
        ).astype(jnp.bfloat16)
        grad_wide = grad.astype(jnp.float32)
        squares = squares + jnp.sum(grad_wide * grad_wide, axis=(1, 2))
        col_proj = gaussian_block(col_stream, col_ids, proj_cols)
        mixed = jnp.einsum("erw,wk->erk", grad, col_proj, preferred_element_type=jnp.float32)
        running = running + jnp.sum(mixed * row_proj[None], axis=1)
        return (running, squares)

    examples_here = activations.shape[0]
    initial = (jnp.zeros((examples_here, K), jnp.float32), jnp.zeros((examples_here,), jnp.float32))
    backs_all = lax.all_gather(backprops, "param", axis=2, tiled=True)
    total_width = backs_all.shape[2]
    step_width = min(total_width, widest_block)

    def one_block(number, inner):
        first = number * step_width
        part_cols = lax.dynamic_slice_in_dim(backs_all, first, step_width, 2)
        return absorb(inner, activations, part_cols, first + lax.iota(jnp.int32, step_width))

    running, squares = lax.fori_loop(0, total_width // step_width, one_block, initial)
    projected = lax.psum_scatter(running, "param", scatter_dimension=1, tiled=True)
    sumsq = lax.psum(squares, "param")
    features = projected * lax.rsqrt(sumsq + epsilon)[:, None]
    return (features, jnp.sqrt(sumsq))


def solution(mesh):
    return jax.shard_map(
        on_device,
        mesh=mesh,
        in_specs=(
            P(("grp", "ex"), None, "param"),
            P(("grp", "ex"), None, "param"),
            P(None, "param"),
        ),
        out_specs=(P(("grp", "ex"), "param"), P(("grp", "ex"))),
        check_vma=False,
    )
```

profile of v0, /device:TPU:0, one launch (start us, length us, event | category | flops | bytes accessed | tf_op | source)
XLA Modules:
  0.0 167.3 jit_solution(10842148868520549854)
XLA Ops:
  7.2 0.0 all-gather.2.cloned.1.call-start
  7.2 0.7 all-gather.2.cloned.1.call-update
  7.9 0.0 reduce-scatter.4.cloned.1.call-start
  8.0 1.3 fusion.30
  10.5 47.7 %all-gather.2.cloned.1.call-done = bf16[1,256,4096]{2,1,0:T(8,128)(2,1)} async-done(((bf16[1,256,1024]{2,1,0:T(8,128)(2,1)}), bf16[1,256,4096]{2,1,0:T(8,128)(2,1)}) %all-gather.2.cloned.1.call-update) | async-done | bytes 2097168 | tf_op jit(solution)/shard_map/all_gather | solution.py:54
  58.2 72.0 %while.18 = (s32[]{:T(128)}, f32[1,2048]{1,0:T(1,128)S(1)}, f32[1]{0:T(128)}, bf16[1,256,4096]{2,1,0:T(8,128)(2,1)}, bf16[1,256,1024]{2,1,0:T(8,128)(2,1)}, /*in...) while((s32[]{:T(128)}, f32[1,2048]{1,0:T(1,128)S(1)}, ...), condition=%wide.region_3.0_spmd.clone, body=%wide.region_0.0_spmd.clone.sunk | while | flops 4938800128 | bytes 5312721 | solution.py:63
  58.3 3.1 %multiply_reduce_fusion.2 = (f32[]{:T(128)}, bf16[1024,1024]{1,0:T(8,128)(2,1)S(1)}) fusion(bf16[1,256,1024]{2,1,0:T(8,128)(2,1)} %get-tuple-element.339, bf16[1,256,4096]{2,1,0:T(8,128)(2,1)} %get-tuple-element.338, s32[]{:T(128)S(6)} %select_n.12), kind=kOutput, calls=%fused_computation.16.clone.1 | convolution fusion | flops 541065216 | bytes 3145736 | tf_op jit(solution)/shard_map/while/body/eval_jaxpr/etr,etw->erw/dot_general | solution.py:42
  62.0 14.2 %fusion.36 = f32[2048]{0:T(1024)S(1)} fusion(bf16[1024,1024]{1,0:T(8,128)(2,1)S(1)} %get-tuple-element.309, s32[2048]{0:T(1024)S(1)} %get-tuple-element.341, s32[1024]{0:T(1024)S(1)} %get-tuple-element.342, s32[2048]{0:T(1024)S(1)} %iota_multiply_fusion.3, s32[1024]{0:T(1024)S(1)} %multiply_add_fusion.3), kind=kOutput, calls=%fused_computation.13.clone.1 | convolution fusion | flops 4397725696 | bytes 2129920 | tf_op jit(solution)/shard_map/while/body/eval_jaxpr/erw,wk->erk/dot_general | solution.py:48
  76.3 3.1 %multiply_reduce_fusion.2 = (f32[]{:T(128)}, bf16[1024,1024]{1,0:T(8,128)(2,1)S(1)}) fusion(bf16[1,256,1024]{2,1,0:T(8,128)(2,1)} %get-tuple-element.339, bf16[1,256,4096]{2,1,0:T(8,128)(2,1)} %get-tuple-element.338, s32[]{:T(128)S(6)} %select_n.12), kind=kOutput, calls=%fused_computation.16.clone.1 | convolution fusion | flops 541065216 | bytes 3145736 | tf_op jit(solution)/shard_map/while/body/eval_jaxpr/etr,etw->erw/dot_general | solution.py:42
  80.0 14.2 %fusion.36 = f32[2048]{0:T(1024)S(1)} fusion(bf16[1024,1024]{1,0:T(8,128)(2,1)S(1)} %get-tuple-element.309, s32[2048]{0:T(1024)S(1)} %get-tuple-element.341, s32[1024]{0:T(1024)S(1)} %get-tuple-element.342, s32[2048]{0:T(1024)S(1)} %iota_multiply_fusion.3, s32[1024]{0:T(1024)S(1)} %multiply_add_fusion.3), kind=kOutput, calls=%fused_computation.13.clone.1 | convolution fusion | flops 4397725696 | bytes 2129920 | tf_op jit(solution)/shard_map/while/body/eval_jaxpr/erw,wk->erk/dot_general | solution.py:48
  94.3 3.1 %multiply_reduce_fusion.2 = (f32[]{:T(128)}, bf16[1024,1024]{1,0:T(8,128)(2,1)S(1)}) fusion(bf16[1,256,1024]{2,1,0:T(8,128)(2,1)} %get-tuple-element.339, bf16[1,256,4096]{2,1,0:T(8,128)(2,1)} %get-tuple-element.338, s32[]{:T(128)S(6)} %select_n.12), kind=kOutput, calls=%fused_computation.16.clone.1 | convolution fusion | flops 541065216 | bytes 3145736 | tf_op jit(solution)/shard_map/while/body/eval_jaxpr/etr,etw->erw/dot_general | solution.py:42
  98.0 14.2 %fusion.36 = f32[2048]{0:T(1024)S(1)} fusion(bf16[1024,1024]{1,0:T(8,128)(2,1)S(1)} %get-tuple-element.309, s32[2048]{0:T(1024)S(1)} %get-tuple-element.341, s32[1024]{0:T(1024)S(1)} %get-tuple-element.342, s32[2048]{0:T(1024)S(1)} %iota_multiply_fusion.3, s32[1024]{0:T(1024)S(1)} %multiply_add_fusion.3), kind=kOutput, calls=%fused_computation.13.clone.1 | convolution fusion | flops 4397725696 | bytes 2129920 | tf_op jit(solution)/shard_map/while/body/eval_jaxpr/erw,wk->erk/dot_general | solution.py:48
  112.3 3.1 %multiply_reduce_fusion.2 = (f32[]{:T(128)}, bf16[1024,1024]{1,0:T(8,128)(2,1)S(1)}) fusion(bf16[1,256,1024]{2,1,0:T(8,128)(2,1)} %get-tuple-element.339, bf16[1,256,4096]{2,1,0:T(8,128)(2,1)} %get-tuple-element.338, s32[]{:T(128)S(6)} %select_n.12), kind=kOutput, calls=%fused_computation.16.clone.1 | convolution fusion | flops 541065216 | bytes 3145736 | tf_op jit(solution)/shard_map/while/body/eval_jaxpr/etr,etw->erw/dot_general | solution.py:42
  116.0 14.2 %fusion.36 = f32[2048]{0:T(1024)S(1)} fusion(bf16[1024,1024]{1,0:T(8,128)(2,1)S(1)} %get-tuple-element.309, s32[2048]{0:T(1024)S(1)} %get-tuple-element.341, s32[1024]{0:T(1024)S(1)} %get-tuple-element.342, s32[2048]{0:T(1024)S(1)} %iota_multiply_fusion.3, s32[1024]{0:T(1024)S(1)} %multiply_add_fusion.3), kind=kOutput, calls=%fused_computation.13.clone.1 | convolution fusion | flops 4397725696 | bytes 2129920 | tf_op jit(solution)/shard_map/while/body/eval_jaxpr/erw,wk->erk/dot_general | solution.py:48
  130.3 1.4 copy.5
  131.6 0.0 reduce-scatter.4.cloned.1.call-update
  131.6 10.6 %psum.7 = f32[1]{0:T(128)} all-reduce(f32[1]{0:T(128)} %get-tuple-element.204), channel_id=1, replica_groups=mesh['grp'=2,'param'=4,'ex'=4] {'param'}, use_global_device_ids=true, to_apply=%region_5.0 | all-reduce | flops 1 | bytes 8 | tf_op jit(solution)/shard_map/psum | solution.py:65
  143.6 14.0 %reduce-scatter.4.cloned.1.call-done = f32[512,1]{1,0:T(8,128)} async-done(((f32[2048,1]{1,0:T(8,128)}), f32[512,1]{1,0:T(8,128)}) %reduce-scatter.4.cloned.1.call-update) | async-done | bytes 2064
  157.7 1.1 copy.6
  158.7 0.6 broadcast_multiply_fusion
  (15 shorter events, 0.2 us)
Async XLA Ops:
  7.2 51.1 %all-gather.2.cloned.1.call-start = ((), (), s32[]{:S(2)}) async-start(), calls=%async_computation.1 | async-start | bytes 2621440 | tf_op jit(solution)/shard_map/all_gather | solution.py:54
  7.9 149.8 %reduce-scatter.4.cloned.1.call-start = ((), (), s32[]{:S(2)}) async-start(), calls=%async_computation.2 | async-start | bytes 1310720
Sparse Core Ops, SparseCore 0:
  9.6 48.6 all-gather.1
  131.8 25.8 reduce-scatter.3
where the time goes:
time: 168 us; the launch traced here: 167 us
  matrix products  69.3 us (41%)
  waiting for transfers between devices  62.4 us (37%)
  between operations  17.8 us (11%)
  blocking collectives  10.6 us (6%)
  local copies, waits for them, and re-layouts  3.74 us (2%)
  loops' own time  2.59 us (2%)
    dot_general x4, matrix products, absorb(): jnp.einsum('erw,wk->erk', grad, col_proj, preferred_element_type=jnp.floa...  56.8 us
    all_gather x1, waiting for transfers between devices, on_device(): backs_all = lax.all_gather(backprops, 'param', axis=2, tiled=True)  47.7 us
    unnamed x3, waiting for transfers between devices  14.7 us
    dot_general x4, matrix products, absorb(): jnp.einsum('etr,etw->erw', acts_rows, part_cols, preferred_element_type=j...  12.5 us
    psum x1, blocking collectives, on_device(): sumsq = lax.psum(squares, 'param')  10.6 us
  transfers between devices with their start and end apart: 2, of which 2 were waited for; matrix products, arithmetic and copies ran while one was open for 1% of the time, Pallas kernels for 0%

commit v1 on v0

v1 whole, which is shorter than its diff:
```python
import functools

import jax
import jax.numpy as jnp
from jax import lax
from jax.experimental import pallas as pl
from jax.experimental.pallas import tpu as pltpu
from jax.sharding import PartitionSpec as P

K = 2048

mix_factor = 73244475
stream_factor = 668265261
row_factor = 374761393
col_factor = 1103515245
epsilon = 1e-06
unscale = 1.0 / (128.0 * 128.0)

tile = 256
sub_rows = 16
sub_cols = 256


def wrapped(number):
    return jnp.int32((number + 2**31) % 2**32 - 2**31)


def scramble(hashed):
    sixteen = jnp.int32(16)
    hashed = jnp.bitwise_xor(hashed, lax.shift_right_logical(hashed, sixteen))
    hashed = hashed * mix_factor
    hashed = jnp.bitwise_xor(hashed, lax.shift_right_logical(hashed, sixteen))
    hashed = hashed * mix_factor
    return jnp.bitwise_xor(hashed, lax.shift_right_logical(hashed, sixteen))


def to_gauss(hashed):
    hashed = scramble(hashed)
    pairs = jnp.int32(0x00FF00FF)
    two_sums = jnp.bitwise_and(hashed, pairs) + jnp.bitwise_and(
        lax.shift_right_logical(hashed, jnp.int32(8)), pairs
    )
    total = lax.shift_right_logical(two_sums * jnp.int32(0x10001), jnp.int32(16))
    return (total - 510).astype(jnp.float32).astype(jnp.bfloat16)


def fill_pattern(pattern_ref):
    shape = pattern_ref.shape
    pattern_ref[...] = (
        lax.broadcasted_iota(jnp.int32, shape, 0) * col_factor
        + lax.broadcasted_iota(jnp.int32, shape, 1) * row_factor
    )


def hash_rows(pattern_ref, out_ref, base, row, width):
    offset = base + (wrapped(row * col_factor) if isinstance(row, int) else row * col_factor)
    for first in range(0, width, sub_cols):
        last = min(first + sub_cols, width)
        out_ref[pl.ds(row, sub_rows), first:last] = to_gauss(pattern_ref[:, first:last] + offset)


def hash_tile(pattern_ref, out_ref, base, width):
    for row in range(0, tile, sub_rows):
        hash_rows(pattern_ref, out_ref, base, row, width)


def dot_nt(lhs, rhs):
    return lax.dot_general(
        lhs, rhs, (((1,), (1,)), ((), ())), preferred_element_type=jnp.float32
    )


def hash_kernel(bases_ref, out_ref, pattern_ref):
    step = pl.program_id(0)

    @pl.when(step == 0)
    def _():
        fill_pattern(pattern_ref)

    base = bases_ref[0] + step * wrapped(tile * col_factor)

    def strip(number, carry):
        row = pl.multiple_of(number * sub_rows, sub_rows)
        hash_rows(pattern_ref, out_ref, base, row, out_ref.shape[1])
        return carry

    lax.fori_loop(0, tile // sub_rows, strip, 0, unroll=4)


def hash_block(base, width, dims):
    return pl.pallas_call(
        hash_kernel,
        grid=(dims // tile,),
        in_specs=[pl.BlockSpec(memory_space=pltpu.SMEM)],
        out_specs=pl.BlockSpec((tile, width), lambda step: (step, 0)),
        out_shape=jax.ShapeDtypeStruct((dims, width), jnp.bfloat16),
        scratch_shapes=[pltpu.VMEM((sub_rows, width), jnp.int32)],
        cost_estimate=pl.CostEstimate(
            flops=18 * dims * width, bytes_accessed=2 * dims * width, transcendentals=0
        ),
        name="hash_block",
    )(base[None])


def early_kernel(blocks, bases_ref, *refs):
    acts = refs[:blocks]
    backs_ref = refs[blocks]
    u_refs = refs[blocks + 1 : 2 * blocks + 1]
    total_ref, gram_a_ref, gram_b_ref = refs[2 * blocks + 1 : 2 * blocks + 4]
    pattern_ref = refs[2 * blocks + 4]
    row_tiles = refs[2 * blocks + 5 : 3 * blocks + 5]
    col_tiles = refs[3 * blocks + 5 :]
    step = pl.program_id(0)
    rows = acts[0].shape[1]
    width = backs_ref.shape[1]
    tokens = gram_a_ref.shape[1]

    def row_base(block, at):
        return bases_ref[2 * block] + at * wrapped(tile * col_factor)

    @pl.when(step == 0)
    def _():
        fill_pattern(pattern_ref)
        hash_tile(pattern_ref, row_tiles[0], row_base(0, 0), rows)
        for e in range(gram_a_ref.shape[0]):
            here = slice(e * tokens, (e + 1) * tokens)
            gram = dot_nt(acts[0][here, :], acts[0][here, :])
            for block in range(1, blocks):
                gram += dot_nt(acts[block][here, :], acts[block][here, :])
            gram_a_ref[e] = gram
            gram_b_ref[e] = dot_nt(backs_ref[here, :], backs_ref[here, :])

    total = None
    for block in range(blocks):
        hash_tile(
            pattern_ref,
            col_tiles[block],
            bases_ref[2 * block + 1] + step * wrapped(tile * col_factor),
            width,
        )
        left = dot_nt(row_tiles[block][...], acts[block][...])
        u_refs[block][...] = left
        following = block + 1
        if following < blocks:
            hash_tile(pattern_ref, row_tiles[following], row_base(following, step), rows)
        else:
            hash_tile(pattern_ref, row_tiles[0], row_base(0, step + 1), rows)
        product = left * dot_nt(col_tiles[block][...], backs_ref[...])
        total = product if total is None else total + product
    total_ref[...] = total


def early(bases, acts, backs, examples, dims):
    blocks = len(acts)
    lanes, rows = acts[0].shape
    width = backs.shape[1]
    tokens = lanes // examples
    whole = lambda array: pl.BlockSpec(array.shape, lambda step: (0, 0))
    by_dims = pl.BlockSpec((tile, lanes), lambda step: (step, 0))
    gram_spec = pl.BlockSpec((examples, tokens, tokens), lambda step: (0, 0, 0))
    gram_shape = jax.ShapeDtypeStruct((examples, tokens, tokens), jnp.float32)
    dims_shape = jax.ShapeDtypeStruct((dims, lanes), jnp.float32)
    hashes = blocks * dims * (rows + width)
    return pl.pallas_call(
        functools.partial(early_kernel, blocks),
        grid=(dims // tile,),
        in_specs=[pl.BlockSpec(memory_space=pltpu.SMEM)]
        + [whole(block) for block in acts]
        + [whole(backs)],
        out_specs=[by_dims] * (blocks + 1) + [gram_spec] * 2,
        out_shape=[dims_shape] * (blocks + 1) + [gram_shape] * 2,
        scratch_shapes=[pltpu.VMEM((sub_rows, max(rows, width)), jnp.int32)]
        + [pltpu.VMEM((tile, rows), jnp.bfloat16)] * blocks
        + [pltpu.VMEM((tile, width), jnp.bfloat16)] * blocks,
        compiler_params=pltpu.CompilerParams(vmem_limit_bytes=40 * 2**20),
        cost_estimate=pl.CostEstimate(
            flops=18 * hashes + 2 * hashes * lanes,
            bytes_accessed=4 * dims * lanes * (blocks + 1),
            transcendentals=0,
        ),
        name="early",
    )(bases, *acts, backs)


def late_kernel(blocks, parts, has_late, place_ref, *refs):
    u_refs = refs[:blocks]
    total_ref, gram_a_ref, gram_b_ref = refs[blocks : blocks + 3]
    refs = refs[blocks + 3 :]
    if has_late:
        backs_ref, col_refs = refs[0], refs[1 : 1 + blocks]
        refs = refs[1 + blocks :]
    outs = refs[:parts]
    step = pl.program_id(0)
    examples, tokens = gram_a_ref.shape[:2]
    part_dims = outs[0].shape[2] - 128

    @pl.when(step == 0)
    def _():
        for e in range(examples):
            gram_b = gram_b_ref[e]
            if has_late:
                here = backs_ref[e * tokens : (e + 1) * tokens, :]
                gram_b = gram_b + dot_nt(here, here)
            both = jnp.sum(gram_a_ref[e] * gram_b)
            for out in outs:
                out[e, :, part_dims:] = jnp.full((1, 128), both, jnp.float32)

    total = total_ref[...]
    if has_late:
        for block in range(blocks):
            total += u_refs[block][...] * dot_nt(col_refs[block][...], backs_ref[...])
    step_dims = min(tile, part_dims)
    for e in range(examples):
        lane_sum = total[:, e * tokens : e * tokens + 128]
        for first in range(128, tokens, 128):
            lane_sum += total[:, e * tokens + first : e * tokens + first + 128]
        across = jnp.sum(lane_sum.T, axis=0, keepdims=True)
        for piece in range(0, tile, step_dims):
            number = (step * tile + piece) // part_dims
            inside = lax.rem(step * tile + piece, part_dims)
            slot = lax.rem(number - place_ref[0] + parts, parts)
            for which, out in enumerate(outs):

                @pl.when(slot == which)
                def _():
                    for begin in range(0, part_dims, step_dims):

                        @pl.when(inside == begin)
                        def _():
                            out[e, :, begin : begin + step_dims] = across[
                                :, piece : piece + step_dims
                            ]


def late(place, us, total, grams, backs, cols, examples, parts):
    blocks = len(us)
    dims, lanes = total.shape
    tokens = lanes // examples
    by_dims = pl.BlockSpec((tile, lanes), lambda step: (step, 0))
    gram_spec = pl.BlockSpec((examples, tokens, tokens), lambda step: (0, 0, 0))
    has_late = backs is not None
    operands = [place, *us, total, *grams]
    specs = [pl.BlockSpec(memory_space=pltpu.SMEM)] + [by_dims] * (blocks + 1) + [gram_spec] * 2
    if has_late:
        width = backs.shape[1]
        operands += [backs, *cols]
        specs += [pl.BlockSpec(backs.shape, lambda step: (0, 0))]
        specs += [pl.BlockSpec((tile, width), lambda step: (step, 0))] * blocks
    message = (examples, 1, dims // parts + 128)
    return pl.pallas_call(
        functools.partial(late_kernel, blocks, parts, has_late),
        grid=(dims // tile,),
        in_specs=specs,
        out_specs=[pl.BlockSpec(message, lambda step: (0, 0, 0))] * parts,
        out_shape=[jax.ShapeDtypeStruct(message, jnp.float32)] * parts,
        compiler_params=pltpu.CompilerParams(vmem_limit_bytes=40 * 2**20),
        name="late",
    )(*operands)


def on_device(parts, activations, backprops, block_counters):
    row_block = activations.shape[2]
    col_block = backprops.shape[2]
    place = lax.axis_index("param")
    acts = activations[0]
    backs = backprops[0]
    counters = block_counters[:, 0]

    def bases_of(streams, place_of, early_at):
        row_start = streams[0] * stream_factor + place_of * wrapped(row_block * row_factor)
        col_start = streams[1] * stream_factor
        return row_start, col_start + early_at * wrapped(col_block * row_factor)

    if parts == 4:
        swap = [(0, 1), (1, 0), (2, 3), (3, 2)]
        other_counters = lax.ppermute(block_counters, "param", swap)[:, 0]
        other_acts = lax.ppermute(acts, "param", swap)
        early_backs = lax.ppermute(backs, "param", [(0, 0), (1, 2), (2, 1), (3, 3)])
        other = jnp.bitwise_xor(place, 1)
        early_at = jnp.array([0, 2, 1, 3], jnp.int32)[place]
        late_at = jnp.array([1, 3, 0, 2], jnp.int32)[place]
        late_step = wrapped(col_block * row_factor)
        own_col = counters[1] * stream_factor
        other_col = other_counters[1] * stream_factor
        own_late = hash_block(own_col + late_at * late_step, col_block, K)
        late_backs = lax.ppermute(backs, "param", [(0, 2), (3, 1), (1, 0), (2, 3)])
        other_late = hash_block(other_col + late_at * late_step, col_block, K)
        bases = jnp.stack(
            [*bases_of(counters, place, early_at), *bases_of(other_counters, other, early_at)]
        )
        results = early(bases, [acts, other_acts], early_backs, 1, K)
        late_cols = [own_late, other_late]
    else:
        every_back = lax.all_gather(backs, "param", axis=1, tiled=True)
        bases = jnp.stack(bases_of(counters, place, 0))
        results = early(bases, [acts], every_back, 1, K)
        late_backs, late_cols = None, None
    *us, total, gram_a, gram_b = results
    messages = late(place[None], us, total, (gram_a, gram_b), late_backs, late_cols, 1, parts)
    summed = messages[0]
    for distance in range(1, parts):
        moves = [(source, (source + distance) % parts) for source in range(parts)]
        summed = summed + lax.ppermute(messages[distance], "param", moves)
    part_dims = K // parts
    sumsq = jnp.maximum(summed[:, 0, part_dims], 0.0)
    features = summed[:, 0, :part_dims] * (lax.rsqrt(sumsq + epsilon) * unscale)[:, None]
    return (features, jnp.sqrt(sumsq))


def solution(mesh):
    return jax.shard_map(
        functools.partial(on_device, mesh.shape["param"]),
        mesh=mesh,
        in_specs=(
            P(("grp", "ex"), None, "param"),
            P(("grp", "ex"), None, "param"),
            P(None, "param"),
        ),
        out_specs=(P(("grp", "ex"), "param"), P(("grp", "ex"))),
        check_vma=False,
    )
```

time: 168 us -> 77.5 us (0.46)
  matrix products: 69.3 us -> 0 us
  waiting for transfers between devices: 62.4 us -> 7.8 us
  Pallas kernels: 0 us -> 43.5 us
  starting transfers between devices: 0.08 us -> 14 us
  between operations: 17.8 us -> 6.3 us
  blocking collectives: 10.6 us -> 0 us
  loops' own time: 2.59 us -> 0 us
    dot_general x8 -> x0, matrix products: 69.3 us -> none  [the longest x4 56.8 us: absorb(): jnp.einsum('erw,wk->erk', grad, col_proj, preferred_element_type=jnp.floa...]
    all_gather x1 -> x0, waiting for transfers between devices: 47.7 us -> none  [on_device(): backs_all = lax.all_gather(backprops, 'param', axis=2, tiled=True)]
    pallas_call x0 -> x4, Pallas kernels: none -> 43.5 us  [the longest x1 23 us: early(): pl.pallas_call(functools.partial(early_kernel, blocks), grid=(dims // til...]
    unnamed x3 -> x0, waiting for transfers between devices: 14.7 us -> none
    ppermute x0 -> x7, starting transfers between devices: none -> 14 us  [the longest x3 5.68 us: on_device(): summed = summed + lax.ppermute(messages[distance], 'param', moves)]
    psum x1 -> x0, blocking collectives: 10.6 us -> none  [on_device(): sumsq = lax.psum(squares, 'param')]
    ppermute x0 -> x7, waiting for transfers between devices: none -> 7.8 us  [the longest x1 5.52 us: on_device(): other_counters = lax.ppermute(block_counters, 'param', swap)[:, 0]]
    another operation x1 -> x0, loops' own time: 2.59 us -> none  [on_device(): lax.fori_loop(0, total_width // step_width, one_block, initial)]
  transfers between devices with their start and end apart: 2 -> 7, of which waited for: 2 -> 3; matrix products, arithmetic and copies ran while one was open for 1% -> 6% of each run, Pallas kernels for 0% -> 46%
where the time goes in v1:
time: 77.5 us; the launch traced here: 77.1 us
  Pallas kernels  43.5 us (56%)
  starting transfers between devices  14 us (18%)
  waiting for transfers between devices  7.8 us (10%)
  between operations  6.3 us (8%)
  local copies, waits for them, and re-layouts  4.89 us (6%)
    pallas_call x1, Pallas kernels, early(): pl.pallas_call(functools.partial(early_kernel, blocks), grid=(dims // til...  23 us
    pallas_call x2, Pallas kernels, hash_block(): pl.pallas_call(hash_kernel, grid=(dims // tile,), in_specs=[pl.BlockSpec(...  12.8 us
    pallas_call x1, Pallas kernels, late(): pl.pallas_call(functools.partial(late_kernel, blocks, parts, has_late), g...  7.7 us
    ppermute x3, starting transfers between devices, on_device(): summed = summed + lax.ppermute(messages[distance], 'param', moves)  5.68 us
    ppermute x1, waiting for transfers between devices, on_device(): other_counters = lax.ppermute(block_counters, 'param', swap)[:, 0]  5.52 us
    ppermute x1, starting transfers between devices, on_device(): other_acts = lax.ppermute(acts, 'param', swap)  3.09 us
    ppermute x1, starting transfers between devices, on_device(): late_backs = lax.ppermute(backs, 'param', [(0, 2), (3, 1), (1, 0), (2, 3)])  2.87 us
    ppermute x3, waiting for transfers between devices, on_device(): summed = summed + lax.ppermute(messages[distance], 'param', moves)  2.28 us
  transfers between devices with their start and end apart: 7, of which 3 were waited for; matrix products, arithmetic and copies ran while one was open for 6% of the time, Pallas kernels for 46%

profile of v1, /device:TPU:0, one launch (start us, length us, event | category | flops | bytes accessed | tf_op | source)
XLA Modules:
  0.0 77.1 jit_solution(15460548144443119846)
XLA Ops:
  0.6 3.1 %collective-permute-start.1 = (bf16[256,1024]{1,0:T(8,128)(2,1)}, bf16[256,1024]{1,0:T(8,128)(2,1)S(1)}, u32[]{:S(2)}, u32[]{:S(2)}) collective-permute-start(bf16[256,1024]{1,0:T(8,128)(2,1)} %bitcast.19), channel_id=1, source_target_pairs={{0,4},{4,0},{8,12},{12,8},{1,5},{5,1},{9,13},{13,9},{2,6},{6,2},{1... | collective-permute-start | bytes 1572872 | tf_op jit(solution)/shard_map/ppermute | solution.py:277
  3.7 1.7 %collective-permute-start.2 = (bf16[256,1024]{1,0:T(8,128)(2,1)}, bf16[256,1024]{1,0:T(8,128)(2,1)S(1)}, u32[]{:S(2)}, u32[]{:S(2)}) collective-permute-start(bf16[256,1024]{1,0:T(8,128)(2,1)} %bitcast.21), channel_id=1, source_target_pairs={{0,0},{4,8},{8,4},{12,12},{1,1},{5,9},{9,5},{13,13},{2,2},{6,10},{... | collective-permute-start | bytes 1572872 | tf_op jit(solution)/shard_map/ppermute | solution.py:278
  5.4 2.9 %collective-permute-start.3 = (bf16[256,1024]{1,0:T(8,128)(2,1)}, bf16[256,1024]{1,0:T(8,128)(2,1)S(1)}, u32[]{:S(2)}, u32[]{:S(2)}) collective-permute-start(bf16[256,1024]{1,0:T(8,128)(2,1)} %bitcast.22), channel_id=1, source_target_pairs={{0,8},{12,4},{4,0},{8,12},{1,9},{13,5},{5,1},{9,13},{2,10},{14,6},... | collective-permute-start | bytes 1572872 | tf_op jit(solution)/shard_map/ppermute | solution.py:286
  8.3 0.6 collective-permute-start
  8.9 1.3 %fusion.1 = (s32[1,1]{0,1:T(1,128)}, s32[1,1]{0,1:T(1,128)}) fusion(s32[2,1]{0,1:T(1,128)} %param.7), kind=kLoop, calls=%fused_computation.4 | loop fusion | bytes 16 | tf_op jit(solution)/shard_map/slice | solution.py:270
  11.5 1.2 %dynamic_slice.6 = s32[1]{0:T(128)} dynamic-slice(s32[4]{0:T(128)} %constant.35.clone, s32[]{:T(128)S(6)} %select_n.4), dynamic_slice_sizes={1} | dynamic-slice | bytes 12 | tf_op jit(solution)/shard_map/dynamic_slice | solution.py:280
  12.8 1.2 %dynamic_slice.7 = s32[1]{0:T(128)} dynamic-slice(s32[4]{0:T(128)} %constant.36.clone, s32[]{:T(128)S(6)} %select_n.4), dynamic_slice_sizes={1} | dynamic-slice | bytes 12 | tf_op jit(solution)/shard_map/dynamic_slice | solution.py:281
  15.2 6.4 %hash_block.2.refs_6_ = bf16[2048,1024]{1,0:T(8,128)(2,1)} custom-call(s32[1]{0:T(128)} %bitcast.13.bases_ref), custom_call_target="tpu_custom_call" | custom-call | flops 37748736 | bytes 4194304 | tf_op jit(solution)/shard_map/hash_block/pallas_call | solution.py:91
  21.6 5.5 %collective-permute-done = s32[2,1]{0,1:T(1,128)S(1)} collective-permute-done((s32[2,1]{0,1:T(1,128)}, s32[2,1]{0,1:T(1,128)S(1)}, u32[]{:S(2)}, u32[]{:S(2)}) %collective-permute-start) | collective-permute-done | bytes 40 | tf_op jit(solution)/shard_map/ppermute | solution.py:276
  27.2 0.6 fusion.2
  28.9 0.0 copy-start.1
  28.9 6.5 %hash_block.3.refs_7_ = bf16[2048,1024]{1,0:T(8,128)(2,1)} custom-call(s32[1]{0:T(128)} %bitcast.14.bases_ref), custom_call_target="tpu_custom_call" | custom-call | flops 37748736 | bytes 4194304 | tf_op jit(solution)/shard_map/hash_block/pallas_call | solution.py:91
  35.4 0.1 pad_add_fusion.bases_ref
  35.5 0.0 collective-permute-done.1.refs_1_
  35.5 0.0 collective-permute-done.2.refs_2_
  35.5 23.0 %early.1 = (f32[2048,256]{1,0:T(8,128)S(1)}, f32[2048,256]{1,0:T(8,128)S(1)}, f32[2048,256]{1,0:T(8,128)S(1)}, f32[1,256,256]{2,1,0:T(8,128)S(1)}, f32[1,256,256]{2,1,0:T(8,128)S(1)}) custom-call(s32[4]{0:T(128)S(1)} %pad_add_fusion.bases_ref, bf16[256,1024]{1,0:T(8,128)(2,1)S(1)} %bitcast.20, bf16[256,1024]{1,0:T(8,128)(2,1)S(1)} %collective-permute-done.1.refs_1_, ...), custom_call_target="tpu_custom_call" | custom-call | flops 4445962240 | bytes 6291456 | tf_op jit(solution)/shard_map/early/pallas_call | solution.py:164
  58.5 7.7 %late.1 = (f32[1,1,640]{2,1,0:T(1,128)S(1)}, f32[1,1,640]{2,1,0:T(1,128)S(1)}, f32[1,1,640]{2,1,0:T(1,128)S(1)}, f32[1,1,640]{2,1,0:T(1,128)S(1)}) custom-call(s32[1]{0:T(128)} %bitcast.place_ref, f32[2048,256]{1,0:T(8,128)S(1)} %get-tuple-element.11.refs_0_, f32[2048,256]{1,0:T(8,128)S(1)} %get-tuple-element.12.refs_1_, ...), custom_call_target="tpu_custom_call" | custom-call | tf_op jit(solution)/shard_map/late/pallas_call | solution.py:250
  66.2 1.7 %collective-permute-start.4 = (f32[1,1,640]{2,1,0:T(1,128)S(1)}, f32[1,1,640]{2,1,0:T(1,128)S(1)}, u32[]{:S(2)}, u32[]{:S(2)}) collective-permute-start(f32[1,1,640]{2,1,0:T(1,128)S(1)} %get-tuple-element.17), channel_id=1, source_target_pairs={{0,4},{4,8},{8,12},{12,0},{1,5},{5,9},{9,13},{13,1},{2,6},{6,10},{... | collective-permute-start | bytes 7688 | tf_op jit(solution)/shard_map/ppermute | solution.py:303
  67.9 2.6 %collective-permute-start.5 = (f32[1,1,640]{2,1,0:T(1,128)S(1)}, f32[1,1,640]{2,1,0:T(1,128)S(1)}, u32[]{:S(2)}, u32[]{:S(2)}) collective-permute-start(f32[1,1,640]{2,1,0:T(1,128)S(1)} %get-tuple-element.18), channel_id=1, source_target_pairs={{0,8},{4,12},{8,0},{12,4},{1,9},{5,13},{9,1},{13,5},{2,10},{6,14},... | collective-permute-start | bytes 7688 | tf_op jit(solution)/shard_map/ppermute | solution.py:303
  70.6 1.3 %collective-permute-start.6 = (f32[1,1,640]{2,1,0:T(1,128)S(1)}, f32[1,1,640]{2,1,0:T(1,128)S(1)}, u32[]{:S(2)}, u32[]{:S(2)}) collective-permute-start(f32[1,1,640]{2,1,0:T(1,128)S(1)} %get-tuple-element.19), channel_id=1, source_target_pairs={{0,12},{4,0},{8,4},{12,8},{1,13},{5,1},{9,5},{13,9},{2,14},{6,2},{... | collective-permute-start | bytes 7688 | tf_op jit(solution)/shard_map/ppermute | solution.py:303
  71.9 0.5 collective-permute-done.5
  72.4 1.7 %collective-permute-done.6 = f32[1,1,640]{2,1,0:T(1,128)S(1)} collective-permute-done((f32[1,1,640]{2,1,0:T(1,128)S(1)}, f32[1,1,640]{2,1,0:T(1,128)S(1)}, u32[]{:S(2)}, u32[]{:S(2)}) %collective-permute-start.6) | collective-permute-done | bytes 2592 | tf_op jit(solution)/shard_map/ppermute | solution.py:303
  74.2 0.5 slice.31
  75.4 0.6 fusion
  (6 shorter events, 0.0 us)
Async XLA Ops:
  0.6 34.8 %collective-permute-start.1 = (bf16[256,1024]{1,0:T(8,128)(2,1)}, bf16[256,1024]{1,0:T(8,128)(2,1)S(1)}, u32[]{:S(2)}, u32[]{:S(2)}) collective-permute-start(bf16[256,1024]{1,0:T(8,128)(2,1)} %bitcast.19), channel_id=1, source_target_pairs={{0,4},{4,0},{8,12},{12,8},{1,5},{5,1},{9,13},{13,9},{2,6},{6,2},{1... | collective-permute-start | bytes 1572872 | tf_op jit(solution)/shard_map/ppermute | solution.py:277
  3.7 31.8 %collective-permute-start.2 = (bf16[256,1024]{1,0:T(8,128)(2,1)}, bf16[256,1024]{1,0:T(8,128)(2,1)S(1)}, u32[]{:S(2)}, u32[]{:S(2)}) collective-permute-start(bf16[256,1024]{1,0:T(8,128)(2,1)} %bitcast.21), channel_id=1, source_target_pairs={{0,0},{4,8},{8,4},{12,12},{1,1},{5,9},{9,5},{13,13},{2,2},{6,10},{... | collective-permute-start | bytes 1572872 | tf_op jit(solution)/shard_map/ppermute | solution.py:278
  5.4 53.1 %collective-permute-start.3 = (bf16[256,1024]{1,0:T(8,128)(2,1)}, bf16[256,1024]{1,0:T(8,128)(2,1)S(1)}, u32[]{:S(2)}, u32[]{:S(2)}) collective-permute-start(bf16[256,1024]{1,0:T(8,128)(2,1)} %bitcast.22), channel_id=1, source_target_pairs={{0,8},{12,4},{4,0},{8,12},{1,9},{13,5},{5,1},{9,13},{2,10},{14,6},... | collective-permute-start | bytes 1572872 | tf_op jit(solution)/shard_map/ppermute | solution.py:286
  8.3 18.9 %collective-permute-start = (s32[2,1]{0,1:T(1,128)}, s32[2,1]{0,1:T(1,128)S(1)}, u32[]{:S(2)}, u32[]{:S(2)}) collective-permute-start(s32[2,1]{0,1:T(1,128)} %param.7), channel_id=1, source_target_pairs={{0,4},{4,0},{8,12},{12,8},{1,5},{5,1},{9,13},{13,9},{2,6},{6,2},{1... | collective-permute-start | bytes 32 | tf_op jit(solution)/shard_map/ppermute | solution.py:276
  28.9 6.6 %copy-start.1 = (bf16[1,256,1024]{2,1,0:T(8,128)(2,1)S(1)}, bf16[1,256,1024]{2,1,0:T(8,128)(2,1)}, u32[]{:S(2)}) copy-start(bf16[1,256,1024]{2,1,0:T(8,128)(2,1)} %param.5) | copy-start | bytes 1572868
  35.5 23.0 %copy-start = (bf16[2048,1024]{1,0:T(8,128)(2,1)S(1)}, bf16[2048,1024]{1,0:T(8,128)(2,1)}, u32[]{:S(2)}) copy-start(bf16[2048,1024]{1,0:T(8,128)(2,1)} %hash_block.2.refs_6_) | copy-start | bytes 12582916
  66.2 5.7 %collective-permute-start.4 = (f32[1,1,640]{2,1,0:T(1,128)S(1)}, f32[1,1,640]{2,1,0:T(1,128)S(1)}, u32[]{:S(2)}, u32[]{:S(2)}) collective-permute-start(f32[1,1,640]{2,1,0:T(1,128)S(1)} %get-tuple-element.17), channel_id=1, source_target_pairs={{0,4},{4,8},{8,12},{12,0},{1,5},{5,9},{9,13},{13,1},{2,6},{6,10},{... | collective-permute-start | bytes 7688 | tf_op jit(solution)/shard_map/ppermute | solution.py:303
  67.9 4.5 %collective-permute-start.5 = (f32[1,1,640]{2,1,0:T(1,128)S(1)}, f32[1,1,640]{2,1,0:T(1,128)S(1)}, u32[]{:S(2)}, u32[]{:S(2)}) collective-permute-start(f32[1,1,640]{2,1,0:T(1,128)S(1)} %get-tuple-element.18), channel_id=1, source_target_pairs={{0,8},{4,12},{8,0},{12,4},{1,9},{5,13},{9,1},{13,5},{2,10},{6,14},... | collective-permute-start | bytes 7688 | tf_op jit(solution)/shard_map/ppermute | solution.py:303
  70.6 3.6 %collective-permute-start.6 = (f32[1,1,640]{2,1,0:T(1,128)S(1)}, f32[1,1,640]{2,1,0:T(1,128)S(1)}, u32[]{:S(2)}, u32[]{:S(2)}) collective-permute-start(f32[1,1,640]{2,1,0:T(1,128)S(1)} %get-tuple-element.19), channel_id=1, source_target_pairs={{0,12},{4,0},{8,4},{12,8},{1,13},{5,1},{9,5},{13,9},{2,14},{6,2},{... | collective-permute-start | bytes 7688 | tf_op jit(solution)/shard_map/ppermute | solution.py:303

commit v2 on v0

v2 whole, which is shorter than its diff:
```python
import functools

import jax
import jax.numpy as jnp
from jax import lax
from jax.experimental import pallas as pl
from jax.experimental.pallas import tpu as pltpu
from jax.sharding import PartitionSpec as P

K = 2048

mix_factor = 73244475
stream_factor = 668265261
row_factor = 374761393
col_factor = 1103515245
epsilon = 1e-06
unscale = 1.0 / (128.0 * 128.0)

tile = 256
sub_rows = 16
sub_cols = 256


def wrapped(number):
    return jnp.int32((number + 2**31) % 2**32 - 2**31)


def scramble(hashed):
    sixteen = jnp.int32(16)
    hashed = jnp.bitwise_xor(hashed, lax.shift_right_logical(hashed, sixteen))
    hashed = hashed * mix_factor
    hashed = jnp.bitwise_xor(hashed, lax.shift_right_logical(hashed, sixteen))
    hashed = hashed * mix_factor
    return jnp.bitwise_xor(hashed, lax.shift_right_logical(hashed, sixteen))


def to_gauss(hashed):
    hashed = scramble(hashed)
    pairs = jnp.int32(0x00FF00FF)
    two_sums = jnp.bitwise_and(hashed, pairs) + jnp.bitwise_and(
        lax.shift_right_logical(hashed, jnp.int32(8)), pairs
    )
    total = lax.shift_right_logical(two_sums * jnp.int32(0x10001), jnp.int32(16))
    return (total - 510).astype(jnp.float32).astype(jnp.bfloat16)


def fill_pattern(pattern_ref):
    shape = pattern_ref.shape
    pattern_ref[...] = (
        lax.broadcasted_iota(jnp.int32, shape, 0) * col_factor
        + lax.broadcasted_iota(jnp.int32, shape, 1) * row_factor
    )


def hash_rows(pattern_ref, out_ref, base, row, width):
    offset = base + (wrapped(row * col_factor) if isinstance(row, int) else row * col_factor)
    for first in range(0, width, sub_cols):
        last = min(first + sub_cols, width)
        out_ref[pl.ds(row, sub_rows), first:last] = to_gauss(pattern_ref[:, first:last] + offset)


def hash_tile(pattern_ref, out_ref, base):
    rows, width = out_ref.shape
    for row in range(0, rows, sub_rows):
        hash_rows(pattern_ref, out_ref, base, row, width)


def dot_nt(lhs, rhs):
    return lax.dot_general(
        lhs, rhs, (((1,), (1,)), ((), ())), preferred_element_type=jnp.float32
    )


def row_base(counters_ref, place, rows):
    return counters_ref[0, 0] * stream_factor + place * wrapped(rows * row_factor)


def col_base(counters_ref, place, columns):
    return counters_ref[1, 0] * stream_factor + place * wrapped(columns * row_factor)


def first_dim(halves, dims):
    if halves == 1:
        return jnp.int32(0)
    return lax.rem(lax.axis_index("ex"), halves) * wrapped(dims * col_factor)


def places(parts):
    place = lax.axis_index("param")
    if parts != 4:
        return place, place, jnp.int32(0), jnp.int32(0)
    early_at = 2 * jnp.bitwise_and(place, 1) + lax.shift_right_logical(place, 1)
    return place, jnp.bitwise_xor(place, 1), early_at, jnp.bitwise_xor(early_at, 1)


def rows_at(step, size):
    return pl.ds(pl.multiple_of(step * size, size), size)


def stream(steps, hashes, uses, beside_first=None):
    hashes[0](0)
    if beside_first is not None:
        beside_first()

    def run(step, last):
        for number, use in enumerate(uses):
            if number + 1 < len(uses):
                hashes[number + 1](step)
            elif not last:
                hashes[0](step + 1)
            use(step)

    def body(step, carry):
        run(step, False)
        return carry

    lax.fori_loop(0, steps - 1, body, 0)
    run(steps - 1, True)


def call(kernel, name, in_smem, operands, outs, scratch, flops, megabytes):
    specs = [pl.BlockSpec(memory_space=pltpu.SMEM)] * in_smem
    specs += [pl.BlockSpec(memory_space=pltpu.VMEM)] * (len(operands) - in_smem)
    return pl.pallas_call(
        kernel,
        in_specs=specs,
        out_specs=[pl.BlockSpec(memory_space=pltpu.VMEM)] * len(outs),
        out_shape=outs,
        scratch_shapes=scratch,
        compiler_params=pltpu.CompilerParams(vmem_limit_bytes=megabytes * 2**20),
        cost_estimate=pl.CostEstimate(flops=flops, bytes_accessed=0, transcendentals=0),
        name=name,
    )(*operands)


def ahead_kernel(parts, halves, is_row, counters_ref, out_ref, pattern_ref):
    _, partner, _, late_at = places(parts)
    dims, columns = out_ref.shape
    fill_pattern(pattern_ref)
    if is_row:
        base = row_base(counters_ref, partner, columns)
    else:
        base = col_base(counters_ref, late_at, columns)
    base += first_dim(halves, dims)

    def strip(number, carry):
        row = pl.multiple_of(number * sub_rows, sub_rows)
        hash_rows(pattern_ref, out_ref, base, row, columns)
        return carry

    lax.fori_loop(0, dims // sub_rows, strip, 0, unroll=4)


def ahead(parts, halves, is_row, counters, columns, dims):
    (block,) = call(
        functools.partial(ahead_kernel, parts, halves, is_row),
        "ahead",
        1,
        [counters],
        [jax.ShapeDtypeStruct((dims, columns), jnp.bfloat16)],
        [pltpu.VMEM((sub_rows, columns), jnp.int32)],
        1000 * dims * columns,
        8,
    )
    return block


def left_kernel(parts, halves, examples, own_ref, *refs):
    acts = refs[:examples]
    u_ref, pattern_ref = refs[examples : examples + 2]
    tiles = refs[examples + 2 :]
    tokens, rows = acts[0].shape
    dims = u_ref.shape[0]
    piece = tiles[0].shape[0]
    fill_pattern(pattern_ref)
    base = row_base(own_ref, places(parts)[0], rows) + first_dim(halves, dims)

    def hash_into(number):
        def run(step):
            offset = step * wrapped(tile * col_factor) + wrapped(number * piece * col_factor)
            hash_tile(pattern_ref, tiles[number], base + offset)

        return run

    def use(number):
        def run(step):
            for e in range(examples):
                u_ref[rows_at(step * len(tiles) + number, piece), e * tokens : (e + 1) * tokens] = (
                    dot_nt(tiles[number][...], acts[e][...])
                )

        return run

    numbers = range(len(tiles))
    stream(dims // tile, [hash_into(n) for n in numbers], [use(n) for n in numbers])


def left(parts, halves, own, acts, dims):
    examples = len(acts)
    tokens, rows = acts[0].shape
    lanes = examples * tokens
    pieces = 2
    (u_own,) = call(
        functools.partial(left_kernel, parts, halves, examples),
        "left",
        1,
        [own, *acts],
        [jax.ShapeDtypeStruct((dims, lanes), jnp.float32)],
        [pltpu.VMEM((sub_rows, rows), jnp.int32)]
        + [pltpu.VMEM((tile // pieces, rows), jnp.bfloat16)] * pieces,
        1000 * dims * rows,
        16,
    )
    return u_own


def middle_kernel(parts, halves, examples, blocks, *refs):
    counters, refs = refs[:blocks], refs[blocks:]
    acts = [refs[b * examples : (b + 1) * examples] for b in range(blocks)]
    refs = refs[blocks * examples :]
    backs, refs = refs[:examples], refs[examples:]
    u_own, refs = refs[0], refs[1:]
    if blocks == 2:
        row_other, u_other, refs = refs[0], refs[1], refs[2:]
    total_ref, gram_a_ref, gram_b_ref, pattern_ref = refs[:4]
    tiles = refs[4:]
    dims = u_own.shape[0]
    tokens, columns = backs[0].shape
    _, _, early_at, _ = places(parts)
    fill_pattern(pattern_ref)

    def grams():
        for e in range(examples):
            gram = None
            for block in acts:
                term = dot_nt(block[e][...], block[e][...])
                gram = term if gram is None else gram + term
            gram_a_ref[e] = gram
            gram_b_ref[e] = dot_nt(backs[e][...], backs[e][...])

    def hash_into(block):
        base = col_base(counters[block], early_at, columns) + first_dim(halves, dims)

        def run(step):
            hash_tile(pattern_ref, tiles[block], base + step * wrapped(tile * col_factor))

        return run

    def use_own(step):
        rows = rows_at(step, tile)
        for e in range(examples):
            here = slice(e * tokens, (e + 1) * tokens)
            total_ref[rows, here] = u_own[rows, here] * dot_nt(tiles[0][...], backs[e][...])

    def use_other(step):
        rows = rows_at(step, tile)
        for e in range(examples):
            here = slice(e * tokens, (e + 1) * tokens)
            u_piece = dot_nt(row_other[rows, :], acts[1][e][...])
            u_other[rows, here] = u_piece
            total_ref[rows, here] += u_piece * dot_nt(tiles[1][...], backs[e][...])

    stream(
        dims // tile, [hash_into(b) for b in range(blocks)], [use_own, use_other][:blocks], grams
    )


def middle(parts, halves, counters, acts, backs, u_own, row_other):
    blocks = len(counters)
    examples = len(backs)
    tokens, columns = backs[0].shape
    dims, lanes = u_own.shape
    gram_shape = jax.ShapeDtypeStruct((examples, tokens, tokens), jnp.float32)
    dims_shape = jax.ShapeDtypeStruct((dims, lanes), jnp.float32)
    operands = [*counters, *[a for block in acts for a in block], *backs, u_own]
    if blocks == 2:
        operands.append(row_other)
    return call(
        functools.partial(middle_kernel, parts, halves, examples, blocks),
        "middle",
        blocks,
        operands,
        [dims_shape] * blocks + [gram_shape] * 2,
        [pltpu.VMEM((sub_rows, columns), jnp.int32)]
        + [pltpu.VMEM((tile, columns), jnp.bfloat16)] * blocks,
        1000 * blocks * dims * columns,
        24,
    )


def late_kernel(parts, halves, examples, blocks, *refs):
    u_refs, refs = refs[:blocks], refs[blocks:]
    total_ref, gram_a_ref, gram_b_ref = refs[:3]
    refs = refs[3:]
    backs = ()
    if blocks:
        backs, refs = refs[:examples], refs[examples:]
        cols, refs = refs[:blocks], refs[blocks:]
    outs = refs
    tokens = gram_a_ref.shape[1]
    dims = total_ref.shape[0]
    part_dims = outs[0].shape[1] - 128
    place = lax.axis_index("param")
    if halves == 2:
        core = lax.rem(lax.axis_index("ex"), 2)

    def send(e, number, columns, values):
        if halves == 1:
            slot = lax.rem(number - place + parts, parts)
        else:
            slot = jnp.bitwise_xor(2 * number + jnp.bitwise_xor(core, e), place)
        for which, out in enumerate(outs):

            @pl.when(slot == which)
            def _():
                out[:, columns] = values

    across = []
    for e in range(examples):
        here = slice(e * tokens, (e + 1) * tokens)
        for step in range(dims // tile):
            rows = slice(step * tile, (step + 1) * tile)
            total = total_ref[rows, here]
            for block in range(blocks):
                total += u_refs[block][rows, here] * dot_nt(cols[block][rows, :], backs[e][...])
            lane_sum = total[:, :128]
            for begin in range(128, tokens, 128):
                lane_sum += total[:, begin : begin + 128]
            across.append(jnp.sum(lane_sum.T, axis=0, keepdims=True))
    for e in range(examples):
        gram_b = gram_b_ref[e]
        if blocks:
            gram_b = gram_b + dot_nt(backs[e][...], backs[e][...])
        both = jnp.full((1, 128), jnp.sum(gram_a_ref[e] * gram_b), jnp.float32)
        for number in range(parts // halves):
            send(e, number, slice(part_dims, part_dims + 128), both)
            step_dims = min(tile, part_dims)
            for begin in range(0, part_dims, step_dims):
                at = number * part_dims + begin
                step, inside = divmod(at, tile)
                values = across[e * (dims // tile) + step][:, inside : inside + step_dims]
                send(e, number, slice(begin, begin + step_dims), values)


def late(parts, halves, us, total, grams, backs, cols):
    blocks = len(cols)
    dims, lanes = total.shape
    examples, tokens = grams[0].shape[:2]
    message = jax.ShapeDtypeStruct((1, dims * halves // parts + 128), jnp.float32)
    return call(
        functools.partial(late_kernel, parts, halves, examples, blocks),
        "late",
        0,
        [*us[:blocks], total, *grams, *backs, *cols],
        [message] * parts,
        [],
        2 * blocks * dims * lanes * 1024,
        24,
    )


def on_device(parts, group, activations, backprops, block_counters):
    columns = backprops.shape[2]
    acts = activations[0]
    backs = backprops[0]
    if parts == 4 and group % 2 == 0:
        swap = [(0, 1), (1, 0), (2, 3), (3, 2)]
        halves = 2
        dims = K // halves

        def with_sibling(array):
            pairs = [(device, device ^ 1) for device in range(group)]
            return [array, lax.ppermute(array, "ex", pairs)]

        other_counters = lax.ppermute(block_counters, "param", swap)
        early_backs = lax.ppermute(backs, "param", [(0, 0), (1, 2), (2, 1), (3, 3)])
        own_pair = with_sibling(acts)
        late_own = ahead(parts, halves, False, block_counters, columns, dims)
        acts, backs, late_own, other_counters = lax.optimization_barrier(
            (acts, backs, late_own, other_counters)
        )
        other_acts = lax.ppermute(acts, "param", swap)
        late_backs = lax.ppermute(backs, "param", [(0, 2), (3, 1), (1, 0), (2, 3)])
        u_own = left(parts, halves, block_counters, own_pair, dims)
        late_other = ahead(parts, halves, False, other_counters, columns, dims)
        other_acts, early_backs, u_own, late_other = lax.optimization_barrier(
            (other_acts, early_backs, u_own, late_other)
        )
        other_pair = with_sibling(other_acts)
        early_pair = with_sibling(early_backs)
        row_other = ahead(parts, halves, True, other_counters, columns, dims)
        u_other, total, *grams = middle(
            parts,
            halves,
            [block_counters, other_counters],
            [own_pair, other_pair],
            early_pair,
            u_own,
            row_other,
        )
        late_pair = with_sibling(late_backs)
        messages = late(
            parts, halves, [u_own, u_other], total, grams, late_pair, [late_own, late_other]
        )
    else:
        halves = 1
        every_back = lax.all_gather(backs, "param", axis=1, tiled=True)
        u_own = left(parts, halves, block_counters, [acts], K)
        total, *grams = middle(
            parts, halves, [block_counters], [[acts]], [every_back], u_own, None
        )
        messages = late(parts, halves, [], total, grams, [], [])
    summed = None
    for number, message in enumerate(messages):
        if halves == 1:
            moves = [(source, (source + number) % parts) for source in range(parts)]
            moved = lax.ppermute(message, "param", moves) if number else message
        else:
            moves = [
                (
                    z * group + chip * 2 + core,
                    (2 * core + (z ^ number) // 2) * group + chip * 2 + (z ^ number) % 2,
                )
                for z in range(parts)
                for chip in range(group // 2)
                for core in range(2)
            ]
            moved = lax.ppermute(message, ("param", "ex"), moves)
        summed = moved if summed is None else summed + moved
    part_dims = K // parts
    sumsq = jnp.maximum(summed[:, part_dims], 0.0)
    features = summed[:, :part_dims] * (lax.rsqrt(sumsq + epsilon) * unscale)[:, None]
    return (features, jnp.sqrt(sumsq))


def solution(mesh):
    return jax.shard_map(
        functools.partial(on_device, mesh.shape["param"], mesh.shape["ex"]),
        mesh=mesh,
        in_specs=(
            P(("grp", "ex"), None, "param"),
            P(("grp", "ex"), None, "param"),
            P(None, "param"),
        ),
        out_specs=(P(("grp", "ex"), "param"), P(("grp", "ex"))),
        check_vma=False,
    )
```

time: 168 us -> 66.4 us (0.40)
  matrix products: 69.3 us -> 0 us
  waiting for transfers between devices: 62.4 us -> 18.7 us
  Pallas kernels: 0 us -> 26.3 us
  starting transfers between devices: 0.08 us -> 16.6 us
  between operations: 17.8 us -> 2.62 us
  blocking collectives: 10.6 us -> 0 us
  loops' own time: 2.59 us -> 0 us
  local copies, waits for them, and re-layouts: 3.74 us -> 1.35 us
    dot_general x8 -> x0, matrix products: 69.3 us -> none  [the longest x4 56.8 us: absorb(): jnp.einsum('erw,wk->erk', grad, col_proj, preferred_element_type=jnp.floa...]
    all_gather x1 -> x0, waiting for transfers between devices: 47.7 us -> none  [on_device(): backs_all = lax.all_gather(backprops, 'param', axis=2, tiled=True)]
    pallas_call x0 -> x6, Pallas kernels: none -> 26.3 us  [call(): pl.pallas_call(kernel, in_specs=specs, out_specs=[pl.BlockSpec(memory_spa...]
    ppermute x0 -> x12, waiting for transfers between devices: none -> 18.7 us  [the longest x1 10.3 us: on_device(): late_backs = lax.ppermute(backs, 'param', [(0, 2), (3, 1), (1, 0), (2, 3)])]
    ppermute x0 -> x12, starting transfers between devices: none -> 16.6 us  [the longest x4 7.97 us: on_device(): moved = lax.ppermute(message, ('param', 'ex'), moves)]
    unnamed x3 -> x0, waiting for transfers between devices: 14.7 us -> none
    psum x1 -> x0, blocking collectives: 10.6 us -> none  [on_device(): sumsq = lax.psum(squares, 'param')]
    another operation x1 -> x0, loops' own time: 2.59 us -> none  [on_device(): lax.fori_loop(0, total_width // step_width, one_block, initial)]
  transfers between devices with their start and end apart: 2 -> 12, of which waited for: 2 -> 4; matrix products, arithmetic and copies ran while one was open for 1% -> 0% of each run, Pallas kernels for 0% -> 34%
where the time goes in v2:
time: 66.4 us; the launch traced here: 66.2 us
  Pallas kernels  26.3 us (40%)
  waiting for transfers between devices  18.7 us (28%)
  starting transfers between devices  16.6 us (25%)
  between operations  2.62 us (4%)
  local copies, waits for them, and re-layouts  1.35 us (2%)
    pallas_call x6, Pallas kernels, call(): pl.pallas_call(kernel, in_specs=specs, out_specs=[pl.BlockSpec(memory_spa...  26.3 us
    ppermute x1, waiting for transfers between devices, on_device(): late_backs = lax.ppermute(backs, 'param', [(0, 2), (3, 1), (1, 0), (2, 3)])  10.3 us
    ppermute x4, starting transfers between devices, on_device(): moved = lax.ppermute(message, ('param', 'ex'), moves)  7.97 us
    ppermute x1, waiting for transfers between devices, on_device(): other_acts = lax.ppermute(acts, 'param', swap)  5.14 us
    ppermute x1, starting transfers between devices, on_device(): other_acts = lax.ppermute(acts, 'param', swap)  3.44 us
    ppermute x4, waiting for transfers between devices, on_device(): moved = lax.ppermute(message, ('param', 'ex'), moves)  3.19 us
    ppermute x1, starting transfers between devices, on_device(): other_counters = lax.ppermute(block_counters, 'param', swap)  3.02 us
    ppermute x1, starting transfers between devices, on_device(): early_backs = lax.ppermute(backs, 'param', [(0, 0), (1, 2), (2, 1), (3, 3)])  1.69 us
  transfers between devices with their start and end apart: 12, of which 4 were waited for; matrix products, arithmetic and copies ran while one was open for 0% of the time, Pallas kernels for 34%

profile of v2, /device:TPU:0, one launch (start us, length us, event | category | flops | bytes accessed | tf_op | source)
XLA Modules:
  0.0 66.2 jit_solution(5288903949801997178)
XLA Ops:
  0.6 0.0 copy-start
  0.6 0.0 copy-start.1
  0.7 0.8 %copy.5.counters_ref.own_ref.refs_0_ = s32[2,1]{1,0:T(2,128)S(1)} copy(s32[2,1]{0,1:T(1,128)} %param.5) | data formatting | bytes 16 | tf_op args[2]
  1.5 3.0 %collective-permute-start = (s32[2,1]{1,0:T(2,128)S(1)}, s32[2,1]{1,0:T(2,128)S(1)}, u32[]{:S(2)}, u32[]{:S(2)}) collective-permute-start(s32[2,1]{1,0:T(2,128)S(1)} %copy.5.counters_ref.own_ref.refs_0_), channel_id=1, source_target_pairs={{0,4},{4,0},{8,12},{12,8},{1,5},{5,1},{9,13},{13,9},{2,6},{6,2},{1... | collective-permute-start | bytes 32 | tf_op jit(solution)/shard_map/ppermute | solution.py:375
  4.5 0.0 collective-permute-start.3
  4.5 1.7 %collective-permute-start.2 = (bf16[256,1024]{1,0:T(8,128)(2,1)}, bf16[256,1024]{1,0:T(8,128)(2,1)S(1)}, u32[]{:S(2)}, u32[]{:S(2)}) collective-permute-start(bf16[256,1024]{1,0:T(8,128)(2,1)} %bitcast.8), channel_id=1, source_target_pairs={{0,0},{4,8},{8,4},{12,12},{1,1},{5,9},{9,5},{13,13},{2,2},{6,10},{... | collective-permute-start | bytes 1572872 | tf_op jit(solution)/shard_map/ppermute | solution.py:376
  6.2 3.1 %ahead.3.refs_7_ = bf16[1024,1024]{1,0:T(8,128)(2,1)S(1)} custom-call(s32[2,1]{1,0:T(2,128)S(1)} %copy.5.counters_ref.own_ref.refs_0_), custom_call_target="tpu_custom_call" | custom-call | flops 1048576000 | tf_op jit(solution)/shard_map/ahead/pallas_call | solution.py:124
  9.3 3.4 %collective-permute-start.1 = (bf16[256,1024]{1,0:T(8,128)(2,1)S(1)}, bf16[256,1024]{1,0:T(8,128)(2,1)S(1)}, u32[]{:S(2)}, u32[]{:S(2)}) collective-permute-start(bf16[256,1024]{1,0:T(8,128)(2,1)S(1)} %bitcast.5), channel_id=1, source_target_pairs={{0,4},{4,0},{8,12},{12,8},{1,5},{5,1},{9,13},{13,9},{2,6},{6,2},{1... | collective-permute-start | bytes 1572872 | tf_op jit(solution)/shard_map/ppermute | solution.py:382
  12.7 3.1 %ahead.4.refs_8_ = bf16[1024,1024]{1,0:T(8,128)(2,1)S(1)} custom-call(s32[2,1]{1,0:T(2,128)S(1)} %collective-permute-done.counters_ref.refs_1_), custom_call_target="tpu_custom_call" | custom-call | flops 1048576000 | tf_op jit(solution)/shard_map/ahead/pallas_call | solution.py:124
  15.8 4.5 %left.1.refs_8_.refs_0_ = f32[1024,512]{1,0:T(8,128)S(1)} custom-call(s32[2,1]{1,0:T(2,128)S(1)} %copy.5.counters_ref.own_ref.refs_0_, bf16[256,1024]{1,0:T(8,128)(2,1)S(1)} %bitcast.6, bf16[256,1024]{1,0:T(8,128)(2,1)S(1)} %collective-permute-done.3.refs_1_.refs_3_), custom_call_target="tpu_custom_call" | custom-call | flops 1048576000 | tf_op jit(solution)/shard_map/left/pallas_call | solution.py:124
  20.3 5.1 %collective-permute-done.1.refs_4_ = bf16[256,1024]{1,0:T(8,128)(2,1)S(1)} collective-permute-done((bf16[256,1024]{1,0:T(8,128)(2,1)S(1)}, bf16[256,1024]{1,0:T(8,128)(2,1)S(1)}, u32[]{:S(2)}, u32[]{:S(2)}) %collective-permute-start.1) | collective-permute-done | bytes 524320 | tf_op jit(solution)/shard_map/ppermute | solution.py:382
  25.4 0.5 collective-permute-start.5
  25.9 10.3 %collective-permute-done.6.refs_5_ = bf16[256,1024]{1,0:T(8,128)(2,1)S(1)} collective-permute-done((bf16[256,1024]{1,0:T(8,128)(2,1)S(1)}, bf16[256,1024]{1,0:T(8,128)(2,1)S(1)}, u32[]{:S(2)}, u32[]{:S(2)}) %collective-permute-start.6) | collective-permute-done | bytes 524320 | tf_op jit(solution)/shard_map/ppermute | solution.py:383
  36.3 3.1 %ahead.5.refs_9_ = bf16[1024,1024]{1,0:T(8,128)(2,1)S(1)} custom-call(s32[2,1]{1,0:T(2,128)S(1)} %collective-permute-done.counters_ref.refs_1_), custom_call_target="tpu_custom_call" | custom-call | flops 1048576000 | tf_op jit(solution)/shard_map/ahead/pallas_call | solution.py:124
  39.4 8.9 %middle.1 = (f32[1024,512]{1,0:T(8,128)S(1)}, f32[1024,512]{1,0:T(8,128)S(1)}, f32[2,256,256]{2,1,0:T(8,128)S(1)}, f32[2,256,256]{2,1,0:T(8,128)S(1)}) custom-call(s32[2,1]{1,0:T(2,128)S(1)} %copy.5.counters_ref.own_ref.refs_0_, s32[2,1]{1,0:T(2,128)S(1)} %collective-permute-done.counters_ref.refs_1_, bf16[256,1024]{1,0:T(8,128)(2,1)S(1)} %bitcast.7, ...), custom_call_target="tpu_custom_call" | custom-call | flops 2097152000 | tf_op jit(solution)/shard_map/middle/pallas_call | solution.py:124
  48.3 3.7 %late.1 = (f32[1,640]{1,0:T(1,128)S(1)}, f32[1,640]{1,0:T(1,128)S(1)}, f32[1,640]{1,0:T(1,128)S(1)}, f32[1,640]{1,0:T(1,128)S(1)}) custom-call(f32[1024,512]{1,0:T(8,128)S(1)} %left.1.refs_8_.refs_0_, f32[1024,512]{1,0:T(8,128)S(1)} %get-tuple-element.23.refs_1_, f32[1024,512]{1,0:T(8,128)S(1)} %get-tuple-element.24.refs_2_, ...), custom_call_target="tpu_custom_call" | custom-call | flops 2147483648 | tf_op jit(solution)/shard_map/late/pallas_call | solution.py:124
  52.0 1.5 %collective-permute-start.10 = (f32[1,640]{1,0:T(1,128)S(1)}, f32[1,640]{1,0:T(1,128)S(1)}, u32[]{:S(2)}, u32[]{:S(2)}) collective-permute-start(f32[1,640]{1,0:T(1,128)S(1)} %get-tuple-element.32), channel_id=1, source_target_pairs={{0,4},{1,12},{2,6},{3,14},{4,5},{5,13},{6,7},{7,15},{8,0},{9,8},{1... | collective-permute-start | bytes 7688 | tf_op jit(solution)/shard_map/ppermute | solution.py:428
  53.6 2.0 %collective-permute-start.11 = (f32[1,640]{1,0:T(1,128)S(1)}, f32[1,640]{1,0:T(1,128)S(1)}, u32[]{:S(2)}, u32[]{:S(2)}) collective-permute-start(f32[1,640]{1,0:T(1,128)S(1)} %get-tuple-element.33), channel_id=1, source_target_pairs={{0,5},{1,13},{2,7},{3,15},{4,4},{5,12},{6,6},{7,14},{8,1},{9,9},{1... | collective-permute-start | bytes 7688 | tf_op jit(solution)/shard_map/ppermute | solution.py:428
  55.6 0.7 collective-permute-start.8
  56.3 3.8 %collective-permute-start.9 = (f32[1,640]{1,0:T(1,128)S(1)}, f32[1,640]{1,0:T(1,128)S(1)}, u32[]{:S(2)}, u32[]{:S(2)}) collective-permute-start(f32[1,640]{1,0:T(1,128)S(1)} %get-tuple-element.31), channel_id=1, source_target_pairs={{0,1},{1,9},{2,3},{3,11},{4,0},{5,8},{6,2},{7,10},{8,5},{9,13},{10... | collective-permute-start | bytes 7688 | tf_op jit(solution)/shard_map/ppermute | solution.py:428
  60.0 0.8 %collective-permute-done.11 = f32[1,640]{1,0:T(1,128)S(1)} collective-permute-done((f32[1,640]{1,0:T(1,128)S(1)}, f32[1,640]{1,0:T(1,128)S(1)}, u32[]{:S(2)}, u32[]{:S(2)}) %collective-permute-start.11) | collective-permute-done | bytes 2592 | tf_op jit(solution)/shard_map/ppermute | solution.py:428
  60.8 2.4 %collective-permute-done.9 = f32[1,640]{1,0:T(1,128)S(1)} collective-permute-done((f32[1,640]{1,0:T(1,128)S(1)}, f32[1,640]{1,0:T(1,128)S(1)}, u32[]{:S(2)}, u32[]{:S(2)}) %collective-permute-start.9) | collective-permute-done | bytes 2592 | tf_op jit(solution)/shard_map/ppermute | solution.py:428
  63.2 0.5 slice.9
  64.5 0.6 slice_multiply_fusion
  (14 shorter events, 0.0 us)
Async XLA Ops:
  0.6 8.6 %copy-start = (bf16[1,256,1024]{2,1,0:T(8,128)(2,1)S(1)}, bf16[1,256,1024]{2,1,0:T(8,128)(2,1)}, u32[]{:S(2)}) copy-start(bf16[1,256,1024]{2,1,0:T(8,128)(2,1)} %param.3) | copy-start | bytes 1572868
  0.6 12.1 %copy-start.1 = (bf16[1,256,1024]{2,1,0:T(8,128)(2,1)S(1)}, bf16[1,256,1024]{2,1,0:T(8,128)(2,1)}, u32[]{:S(2)}) copy-start(bf16[1,256,1024]{2,1,0:T(8,128)(2,1)} %param.4) | copy-start | bytes 1572868
  1.5 7.8 %collective-permute-start = (s32[2,1]{1,0:T(2,128)S(1)}, s32[2,1]{1,0:T(2,128)S(1)}, u32[]{:S(2)}, u32[]{:S(2)}) collective-permute-start(s32[2,1]{1,0:T(2,128)S(1)} %copy.5.counters_ref.own_ref.refs_0_), channel_id=1, source_target_pairs={{0,4},{4,0},{8,12},{12,8},{1,5},{5,1},{9,13},{13,9},{2,6},{6,2},{1... | collective-permute-start | bytes 32 | tf_op jit(solution)/shard_map/ppermute | solution.py:375
  4.5 11.3 %collective-permute-start.3 = (bf16[256,1024]{1,0:T(8,128)(2,1)}, bf16[256,1024]{1,0:T(8,128)(2,1)S(1)}, u32[]{:S(2)}, u32[]{:S(2)}) collective-permute-start(bf16[256,1024]{1,0:T(8,128)(2,1)} %bitcast.4), channel_id=1, source_target_pairs={{0,1},{1,0},{2,3},{3,2},{4,5},{5,4},{6,7},{7,6},{8,9},{9,8},{10,11... | collective-permute-start | bytes 1572872 | tf_op jit(solution)/shard_map/ppermute | solution.py:373
  4.5 15.8 %collective-permute-start.2 = (bf16[256,1024]{1,0:T(8,128)(2,1)}, bf16[256,1024]{1,0:T(8,128)(2,1)S(1)}, u32[]{:S(2)}, u32[]{:S(2)}) collective-permute-start(bf16[256,1024]{1,0:T(8,128)(2,1)} %bitcast.8), channel_id=1, source_target_pairs={{0,0},{4,8},{8,4},{12,12},{1,1},{5,9},{9,5},{13,13},{2,2},{6,10},{... | collective-permute-start | bytes 1572872 | tf_op jit(solution)/shard_map/ppermute | solution.py:376
  9.3 16.1 %collective-permute-start.1 = (bf16[256,1024]{1,0:T(8,128)(2,1)S(1)}, bf16[256,1024]{1,0:T(8,128)(2,1)S(1)}, u32[]{:S(2)}, u32[]{:S(2)}) collective-permute-start(bf16[256,1024]{1,0:T(8,128)(2,1)S(1)} %bitcast.5), channel_id=1, source_target_pairs={{0,4},{4,0},{8,12},{12,8},{1,5},{5,1},{9,13},{13,9},{2,6},{6,2},{1... | collective-permute-start | bytes 1572872 | tf_op jit(solution)/shard_map/ppermute | solution.py:382
  12.7 23.5 %collective-permute-start.6 = (bf16[256,1024]{1,0:T(8,128)(2,1)S(1)}, bf16[256,1024]{1,0:T(8,128)(2,1)S(1)}, u32[]{:S(2)}, u32[]{:S(2)}) collective-permute-start(bf16[256,1024]{1,0:T(8,128)(2,1)S(1)} %bitcast.9), channel_id=1, source_target_pairs={{0,8},{12,4},{4,0},{8,12},{1,9},{13,5},{5,1},{9,13},{2,10},{14,6},... | collective-permute-start | bytes 1572872 | tf_op jit(solution)/shard_map/ppermute | solution.py:383
  25.4 13.9 %collective-permute-start.4 = (bf16[256,1024]{1,0:T(8,128)(2,1)S(1)}, bf16[256,1024]{1,0:T(8,128)(2,1)S(1)}, u32[]{:S(2)}, u32[]{:S(2)}) collective-permute-start(bf16[256,1024]{1,0:T(8,128)(2,1)S(1)} %collective-permute-done.1.refs_4_), channel_id=1, source_target_pairs={{0,1},{1,0},{2,3},{3,2},{4,5},{5,4},{6,7},{7,6},{8,9},{9,8},{10,11... | collective-permute-start | bytes 1572872 | tf_op jit(solution)/shard_map/ppermute | solution.py:373
  25.4 13.9 %collective-permute-start.5 = (bf16[256,1024]{1,0:T(8,128)(2,1)S(1)}, bf16[256,1024]{1,0:T(8,128)(2,1)S(1)}, u32[]{:S(2)}, u32[]{:S(2)}) collective-permute-start(bf16[256,1024]{1,0:T(8,128)(2,1)S(1)} %collective-permute-done.2.refs_6_), channel_id=1, source_target_pairs={{0,1},{1,0},{2,3},{3,2},{4,5},{5,4},{6,7},{7,6},{8,9},{9,8},{10,11... | collective-permute-start | bytes 1572872 | tf_op jit(solution)/shard_map/ppermute | solution.py:373
  36.3 12.0 %collective-permute-start.7 = (bf16[256,1024]{1,0:T(8,128)(2,1)S(1)}, bf16[256,1024]{1,0:T(8,128)(2,1)S(1)}, u32[]{:S(2)}, u32[]{:S(2)}) collective-permute-start(bf16[256,1024]{1,0:T(8,128)(2,1)S(1)} %collective-permute-done.6.refs_5_), channel_id=1, source_target_pairs={{0,1},{1,0},{2,3},{3,2},{4,5},{5,4},{6,7},{7,6},{8,9},{9,8},{10,11... | collective-permute-start | bytes 1572872 | tf_op jit(solution)/shard_map/ppermute | solution.py:373
  52.0 8.0 %collective-permute-start.10 = (f32[1,640]{1,0:T(1,128)S(1)}, f32[1,640]{1,0:T(1,128)S(1)}, u32[]{:S(2)}, u32[]{:S(2)}) collective-permute-start(f32[1,640]{1,0:T(1,128)S(1)} %get-tuple-element.32), channel_id=1, source_target_pairs={{0,4},{1,12},{2,6},{3,14},{4,5},{5,13},{6,7},{7,15},{8,0},{9,8},{1... | collective-permute-start | bytes 7688 | tf_op jit(solution)/shard_map/ppermute | solution.py:428
  53.6 7.3 %collective-permute-start.11 = (f32[1,640]{1,0:T(1,128)S(1)}, f32[1,640]{1,0:T(1,128)S(1)}, u32[]{:S(2)}, u32[]{:S(2)}) collective-permute-start(f32[1,640]{1,0:T(1,128)S(1)} %get-tuple-element.33), channel_id=1, source_target_pairs={{0,5},{1,13},{2,7},{3,15},{4,4},{5,12},{6,6},{7,14},{8,1},{9,9},{1... | collective-permute-start | bytes 7688 | tf_op jit(solution)/shard_map/ppermute | solution.py:428
  55.6 5.2 %collective-permute-start.8 = (f32[1,640]{1,0:T(1,128)S(1)}, f32[1,640]{1,0:T(1,128)S(1)}, u32[]{:S(2)}, u32[]{:S(2)}) collective-permute-start(f32[1,640]{1,0:T(1,128)S(1)} %get-tuple-element.30), channel_id=1, source_target_pairs={{0,0},{1,8},{2,2},{3,10},{4,1},{5,9},{6,3},{7,11},{8,4},{9,12},{10... | collective-permute-start | bytes 7688 | tf_op jit(solution)/shard_map/ppermute | solution.py:428
  56.3 7.0 %collective-permute-start.9 = (f32[1,640]{1,0:T(1,128)S(1)}, f32[1,640]{1,0:T(1,128)S(1)}, u32[]{:S(2)}, u32[]{:S(2)}) collective-permute-start(f32[1,640]{1,0:T(1,128)S(1)} %get-tuple-element.31), channel_id=1, source_target_pairs={{0,1},{1,9},{2,3},{3,11},{4,0},{5,8},{6,2},{7,10},{8,5},{9,13},{10... | collective-permute-start | bytes 7688 | tf_op jit(solution)/shard_map/ppermute | solution.py:428

commit v3 on v2

v3 whole, which is shorter than its diff:
```python
import functools

import jax
import jax.numpy as jnp
from jax import lax
from jax.experimental import pallas as pl
from jax.experimental.pallas import tpu as pltpu
from jax.sharding import PartitionSpec as P

K = 2048

mix_factor = 73244475
stream_factor = 668265261
row_factor = 374761393
col_factor = 1103515245
epsilon = 1e-06
unscale = 1.0 / (128.0 * 128.0)

tile = 256
sub_rows = 16
sub_cols = 256


def wrapped(number):
    return jnp.int32((number + 2**31) % 2**32 - 2**31)


def scramble(hashed):
    sixteen = jnp.int32(16)
    hashed = jnp.bitwise_xor(hashed, lax.shift_right_logical(hashed, sixteen))
    hashed = hashed * mix_factor
    hashed = jnp.bitwise_xor(hashed, lax.shift_right_logical(hashed, sixteen))
    hashed = hashed * mix_factor
    return jnp.bitwise_xor(hashed, lax.shift_right_logical(hashed, sixteen))


def to_gauss(hashed):
    hashed = scramble(hashed)
    pairs = jnp.int32(0x00FF00FF)
    two_sums = jnp.bitwise_and(hashed, pairs) + jnp.bitwise_and(
        lax.shift_right_logical(hashed, jnp.int32(8)), pairs
    )
    total = lax.shift_right_logical(two_sums * jnp.int32(0x10001), jnp.int32(16))
    return (total - 510).astype(jnp.float32).astype(jnp.bfloat16)


def fill_pattern(pattern_ref):
    shape = pattern_ref.shape
    pattern_ref[...] = (
        lax.broadcasted_iota(jnp.int32, shape, 0) * col_factor
        + lax.broadcasted_iota(jnp.int32, shape, 1) * row_factor
    )


def hash_rows(pattern_ref, out_ref, base, row, width):
    offset = base + (wrapped(row * col_factor) if isinstance(row, int) else row * col_factor)
    for first in range(0, width, sub_cols):
        last = min(first + sub_cols, width)
        out_ref[pl.ds(row, sub_rows), first:last] = to_gauss(pattern_ref[:, first:last] + offset)


def hash_tile(pattern_ref, out_ref, base):
    rows, width = out_ref.shape
    for row in range(0, rows, sub_rows):
        hash_rows(pattern_ref, out_ref, base, row, width)


def dot_nt(lhs, rhs):
    return lax.dot_general(
        lhs, rhs, (((1,), (1,)), ((), ())), preferred_element_type=jnp.float32
    )


def counter(source, which):
    if source.dtype == jnp.int32:
        return source[which, 0]
    row = source[source.shape[0] - 16 :, 0:128].astype(jnp.float32)[0:1]
    lane = lax.broadcasted_iota(jnp.int32, row.shape, 1) - 3 * which
    zero = jnp.zeros_like(row)
    value = zero
    for digit in range(3):
        value += jnp.where(lane == digit, row * float(256**digit), zero)
    return jnp.sum(value).astype(jnp.int32)


def row_base(source, place, rows):
    return counter(source, 0) * stream_factor + place * wrapped(rows * row_factor)


def col_base(source, place, columns):
    return counter(source, 1) * stream_factor + place * wrapped(columns * row_factor)


def first_dim(halves, dims):
    if halves == 1:
        return jnp.int32(0)
    return lax.rem(lax.axis_index("ex"), halves) * wrapped(dims * col_factor)


def places(parts):
    place = lax.axis_index("param")
    if parts != 4:
        return place, place, jnp.int32(0), jnp.int32(0)
    early_at = 2 * jnp.bitwise_and(place, 1) + lax.shift_right_logical(place, 1)
    return place, jnp.bitwise_xor(place, 1), early_at, jnp.bitwise_xor(early_at, 1)


def rows_at(step, size):
    return pl.ds(pl.multiple_of(step * size, size), size)


def stream(steps, hash_at, use, beside_first):
    hash_at(0, 0)
    beside_first()

    def body(turn, carry):
        hash_at(2 * turn + 1, 1)
        use(2 * turn, 0)
        hash_at(2 * turn + 2, 0)
        use(2 * turn + 1, 1)
        return carry

    lax.fori_loop(0, steps // 2 - 1, body, 0)
    hash_at(steps - 1, 1)
    use(steps - 2, 0)
    use(steps - 1, 1)


def call(kernel, name, operands, outs, scratch, flops, megabytes):
    spaces = [pltpu.SMEM if array.dtype == jnp.int32 else pltpu.VMEM for array in operands]
    return pl.pallas_call(
        kernel,
        in_specs=[pl.BlockSpec(memory_space=space) for space in spaces],
        out_specs=[pl.BlockSpec(memory_space=pltpu.VMEM)] * len(outs),
        out_shape=outs,
        scratch_shapes=scratch,
        compiler_params=pltpu.CompilerParams(vmem_limit_bytes=megabytes * 2**20),
        cost_estimate=pl.CostEstimate(flops=flops, bytes_accessed=0, transcendentals=0),
        name=name,
    )(*operands)


def floats(*shape):
    return jax.ShapeDtypeStruct(shape, jnp.float32)


def digits_kernel(acts_ref, counters_ref, out_ref):
    tokens, rows = acts_ref.shape
    out_ref[:tokens, :] = acts_ref[...]
    lane = lax.broadcasted_iota(jnp.int32, (16, rows), 1)
    digits = jnp.zeros((16, rows), jnp.int32)
    for which in range(2):
        for digit in range(3):
            value = lax.shift_right_logical(counters_ref[which, 0], jnp.int32(8 * digit))
            digits = jnp.where(lane == 3 * which + digit, jnp.bitwise_and(value, 255), digits)
    out_ref[tokens:, :] = digits.astype(jnp.float32).astype(out_ref.dtype)


def with_digits(acts, counters):
    tokens, rows = acts.shape
    (out,) = call(
        digits_kernel,
        "with_digits",
        [acts, counters],
        [jax.ShapeDtypeStruct((tokens + 16, rows), acts.dtype)],
        [],
        0,
        8,
    )
    return out


def ahead_kernel(parts, halves, is_row, source, out_ref, pattern_ref):
    _, partner, _, late_at = places(parts)
    dims, columns = out_ref.shape
    fill_pattern(pattern_ref)
    if is_row:
        base = row_base(source, partner, columns)
    else:
        base = col_base(source, late_at, columns)
    base += first_dim(halves, dims)

    def strip(number, carry):
        row = pl.multiple_of(number * sub_rows, sub_rows)
        hash_rows(pattern_ref, out_ref, base, row, columns)
        return carry

    lax.fori_loop(0, dims // sub_rows, strip, 0, unroll=4)


def ahead(parts, halves, is_row, source, columns, dims):
    (block,) = call(
        functools.partial(ahead_kernel, parts, halves, is_row),
        "ahead",
        [source],
        [jax.ShapeDtypeStruct((dims, columns), jnp.bfloat16)],
        [pltpu.VMEM((sub_rows, columns), jnp.int32)],
        1000 * dims * columns,
        8,
    )
    return block


def left_kernel(parts, halves, examples, source, *refs):
    acts = refs[:examples]
    u_ref, gram_ref, pattern_ref = refs[examples : examples + 3]
    tiles = refs[examples + 3 :]
    tokens, rows = acts[0].shape
    dims = u_ref.shape[0]
    fill_pattern(pattern_ref)
    base = row_base(source, places(parts)[0], rows) + first_dim(halves, dims)

    def hash_at(step, which):
        hash_tile(pattern_ref, tiles[which], base + step * wrapped(tile * col_factor))

    def grams():
        for e in range(examples):
            gram_ref[e] = dot_nt(acts[e][...], acts[e][...])

    def use(step, which):
        for e in range(examples):
            u_ref[rows_at(step, tile), e * tokens : (e + 1) * tokens] = dot_nt(
                tiles[which][...], acts[e][...]
            )

    stream(dims // tile, hash_at, use, grams)


def left(parts, halves, own, acts, dims):
    examples = len(acts)
    tokens, rows = acts[0].shape
    return call(
        functools.partial(left_kernel, parts, halves, examples),
        "left",
        [own, *acts],
        [floats(dims, examples * tokens), floats(examples, tokens, tokens)],
        [pltpu.VMEM((sub_rows, rows), jnp.int32)] + [pltpu.VMEM((tile, rows), jnp.bfloat16)] * 2,
        1000 * dims * rows,
        16,
    )


def middle_kernel(parts, halves, examples, paired, source, *refs):
    if paired:
        acts, refs = (source, *refs[: examples - 1]), refs[examples - 1 :]
        row_ref, total_in, refs = refs[0], refs[1], refs[2:]
    else:
        u_ref, refs = refs[0], refs[1:]
    backs, refs = refs[:examples], refs[examples:]
    total_ref, gram_ref, refs = refs[0], refs[1], refs[2:]
    if paired:
        u_ref, refs = refs[0], refs[1:]
    pattern_ref, tiles = refs[0], refs[1:]
    dims = total_ref.shape[0]
    tokens, columns = backs[0].shape
    _, _, early_at, _ = places(parts)
    fill_pattern(pattern_ref)
    base = col_base(source, early_at, columns) + first_dim(halves, dims)

    def hash_at(step, which):
        hash_tile(pattern_ref, tiles[which], base + step * wrapped(tile * col_factor))

    def grams():
        for e in range(examples):
            tokens_of = acts[e][:tokens, :] if paired else backs[e][...]
            gram_ref[e] = dot_nt(tokens_of, tokens_of)

    def use(step, which):
        rows = rows_at(step, tile)
        for e in range(examples):
            here = slice(e * tokens, (e + 1) * tokens)
            right = dot_nt(tiles[which][...], backs[e][...])
            if paired:
                u_piece = dot_nt(row_ref[rows, :], acts[e][:tokens, :])
                u_ref[rows, here] = u_piece
                total_ref[rows, here] = total_in[rows, here] + u_piece * right
            else:
                total_ref[rows, here] = u_ref[rows, here] * right

    stream(dims // tile, hash_at, use, grams)


def middle(parts, halves, source, backs, u_own=None, other=None):
    examples = len(backs)
    tokens, columns = backs[0].shape
    if other is None:
        operands = [source, u_own, *backs]
        dims = u_own.shape[0]
        more = []
    else:
        siblings, row_other, total = other
        operands = [source, *siblings, row_other, total, *backs]
        dims = total.shape[0]
        more = [floats(dims, examples * tokens)]
    return call(
        functools.partial(middle_kernel, parts, halves, examples, other is not None),
        "middle",
        operands,
        [floats(dims, examples * tokens), floats(examples, tokens, tokens), *more],
        [pltpu.VMEM((sub_rows, columns), jnp.int32)]
        + [pltpu.VMEM((tile, columns), jnp.bfloat16)] * 2,
        1000 * dims * columns,
        20,
    )


def late_kernel(parts, halves, examples, blocks, *refs):
    u_refs, refs = refs[:blocks], refs[blocks:]
    total_ref, refs = refs[0], refs[1:]
    sides = max(blocks, 1)
    grams_a, grams_b, refs = refs[:sides], refs[sides], refs[sides + 1 :]
    backs = ()
    if blocks:
        backs, refs = refs[:examples], refs[examples:]
        cols, refs = refs[:blocks], refs[blocks:]
    outs = refs
    tokens = grams_b.shape[1]
    dims = total_ref.shape[0]
    part_dims = outs[0].shape[1] - 128
    place = lax.axis_index("param")
    if halves == 2:
        core = lax.rem(lax.axis_index("ex"), 2)

    def send(e, number, columns, values):
        if halves == 1:
            slot = lax.rem(number - place + parts, parts)
        else:
            slot = jnp.bitwise_xor(2 * number + jnp.bitwise_xor(core, e), place)
        for which, out in enumerate(outs):

            @pl.when(slot == which)
            def _():
                out[:, columns] = values

    across = []
    for e in range(examples):
        here = slice(e * tokens, (e + 1) * tokens)
        for step in range(dims // tile):
            rows = slice(step * tile, (step + 1) * tile)
            total = total_ref[rows, here]
            for block in range(blocks):
                total += u_refs[block][rows, here] * dot_nt(cols[block][rows, :], backs[e][...])
            lane_sum = total[:, :128]
            for begin in range(128, tokens, 128):
                lane_sum += total[:, begin : begin + 128]
            across.append(jnp.sum(lane_sum.T, axis=0, keepdims=True))
    for e in range(examples):
        gram_a = grams_a[0][e]
        for more in grams_a[1:]:
            gram_a = gram_a + more[e]
        gram_b = grams_b[e]
        if blocks:
            gram_b = gram_b + dot_nt(backs[e][...], backs[e][...])
        both = jnp.full((1, 128), jnp.sum(gram_a * gram_b), jnp.float32)
        for number in range(parts // halves):
            send(e, number, slice(part_dims, part_dims + 128), both)
            step_dims = min(tile, part_dims)
            for begin in range(0, part_dims, step_dims):
                at = number * part_dims + begin
                step, inside = divmod(at, tile)
                values = across[e * (dims // tile) + step][:, inside : inside + step_dims]
                send(e, number, slice(begin, begin + step_dims), values)


def late(parts, halves, us, total, grams, backs, cols):
    blocks = len(cols)
    dims, lanes = total.shape
    examples, tokens = grams[0].shape[:2]
    message = jax.ShapeDtypeStruct((1, dims * halves // parts + 128), jnp.float32)
    return call(
        functools.partial(late_kernel, parts, halves, examples, blocks),
        "late",
        [*us[:blocks], total, *grams, *backs, *cols],
        [message] * parts,
        [],
        2 * blocks * dims * lanes * 1024,
        24,
    )


def on_device(parts, group, activations, backprops, block_counters):
    columns = backprops.shape[2]
    acts = activations[0]
    backs = backprops[0]
    if parts == 4 and group % 2 == 0:
        swap = [(0, 1), (1, 0), (2, 3), (3, 2)]
        halves = 2
        dims = K // halves

        def with_sibling(array):
            pairs = [(device, device ^ 1) for device in range(group)]
            return [array, lax.ppermute(array, "ex", pairs)]

        other_acts = lax.ppermute(with_digits(acts, block_counters), "param", swap)
        early_backs = lax.ppermute(backs, "param", [(0, 0), (1, 2), (2, 1), (3, 3)])
        own_pair = with_sibling(acts)
        late_own = ahead(parts, halves, False, block_counters, columns, dims)
        late_backs = lax.ppermute(backs, "param", [(0, 2), (3, 1), (1, 0), (2, 3)])
        u_own, gram_own = left(parts, halves, block_counters, own_pair, dims)
        other_acts, u_own, late_own = lax.optimization_barrier((other_acts, u_own, late_own))
        late_other = ahead(parts, halves, False, other_acts, columns, dims)
        row_other = ahead(parts, halves, True, other_acts, columns, dims)
        other_acts, early_backs, late_backs, late_other, row_other = lax.optimization_barrier(
            (other_acts, early_backs, late_backs, late_other, row_other)
        )
        early_pair = with_sibling(early_backs)
        other_pair = with_sibling(other_acts)
        late_pair = with_sibling(late_backs)
        total, gram_early = middle(parts, halves, block_counters, early_pair, u_own=u_own)
        total, gram_other, u_other = middle(
            parts, halves, other_acts, early_pair, other=(other_pair[1:], row_other, total)
        )
        messages = late(
            parts,
            halves,
            [u_own, u_other],
            total,
            [gram_own, gram_other, gram_early],
            late_pair,
            [late_own, late_other],
        )
    else:
        halves = 1
        every_back = lax.all_gather(backs, "param", axis=1, tiled=True)
        u_own, gram_own = left(parts, halves, block_counters, [acts], K)
        total, gram_backs = middle(parts, halves, block_counters, [every_back], u_own=u_own)
        messages = late(parts, halves, [], total, [gram_own, gram_backs], [], [])
    summed = None
    for number, message in enumerate(messages):
        if halves == 1:
            moves = [(source, (source + number) % parts) for source in range(parts)]
            moved = lax.ppermute(message, "param", moves) if number else message
        else:
            moves = [
                (
                    z * group + chip * 2 + core,
                    (2 * core + (z ^ number) // 2) * group + chip * 2 + (z ^ number) % 2,
                )
                for z in range(parts)
                for chip in range(group // 2)
                for core in range(2)
            ]
            moved = lax.ppermute(message, ("param", "ex"), moves)
        summed = moved if summed is None else summed + moved
    part_dims = K // parts
    sumsq = jnp.maximum(summed[:, part_dims], 0.0)
    features = summed[:, :part_dims] * (lax.rsqrt(sumsq + epsilon) * unscale)[:, None]
    return (features, jnp.sqrt(sumsq))


def solution(mesh):
    return jax.shard_map(
        functools.partial(on_device, mesh.shape["param"], mesh.shape["ex"]),
        mesh=mesh,
        in_specs=(
            P(("grp", "ex"), None, "param"),
            P(("grp", "ex"), None, "param"),
            P(None, "param"),
        ),
        out_specs=(P(("grp", "ex"), "param"), P(("grp", "ex"))),
        check_vma=False,
    )
```

time: 66.4 us -> 60.7 us (0.914)
  waiting for transfers between devices: 18.7 us -> 13.8 us
  Pallas kernels: 26.3 us -> 23.4 us
  starting transfers between devices: 16.6 us -> 17.7 us
  local copies, waits for them, and re-layouts: 1.35 us -> 2.3 us
    ppermute x1, waiting for transfers between devices: 10.3 us -> 5.59 us  [on_device(): late_backs = lax.ppermute(backs, 'param', [(0, 2), (3, 1), (1, 0), (2, 3)])]
    ppermute x2 -> x1, starting transfers between devices: 6.46 us -> 2.65 us  [on_device(): other_acts = lax.ppermute(with_digits(acts, block_counters), 'param', swap)]
    pallas_call x6 -> x8, Pallas kernels: 26.3 us -> 23.4 us  [call(): pl.pallas_call(kernel, in_specs=[pl.BlockSpec(memory_space=space) for spa...]
    ppermute x1, starting transfers between devices: 0.01 us -> 2.87 us  [on_device(): late_backs = lax.ppermute(backs, 'param', [(0, 2), (3, 1), (1, 0), (2, 3)])]
    ppermute x2 -> x1, waiting for transfers between devices: 5.14 us -> 2.37 us  [on_device(): other_acts = lax.ppermute(with_digits(acts, block_counters), 'param', swap)]
    ppermute x4, starting transfers between devices: 7.97 us -> 9.45 us  [on_device(): moved = lax.ppermute(message, ('param', 'ex'), moves)]
    ppermute x4, waiting for transfers between devices: 0.01 us -> 1.4 us  [with_sibling(): return [array, lax.ppermute(array, 'ex', pairs)]]
    ppermute x4, waiting for transfers between devices: 3.19 us -> 4.48 us  [on_device(): moved = lax.ppermute(message, ('param', 'ex'), moves)]
  transfers between devices with their start and end apart: 12 -> 11, of which waited for: 4 -> 5; matrix products, arithmetic and copies ran while one was open for 0% -> 1% of each run, Pallas kernels for 34% -> 33%
where the time goes in v3:
time: 60.7 us; the launch traced here: 60.4 us
  Pallas kernels  23.4 us (39%)
  starting transfers between devices  17.7 us (29%)
  waiting for transfers between devices  13.8 us (23%)
  between operations  2.62 us (4%)
  local copies, waits for them, and re-layouts  2.3 us (4%)
    pallas_call x8, Pallas kernels, call(): pl.pallas_call(kernel, in_specs=[pl.BlockSpec(memory_space=space) for spa...  23.4 us
    ppermute x4, starting transfers between devices, on_device(): moved = lax.ppermute(message, ('param', 'ex'), moves)  9.45 us
    ppermute x1, waiting for transfers between devices, on_device(): late_backs = lax.ppermute(backs, 'param', [(0, 2), (3, 1), (1, 0), (2, 3)])  5.59 us
    ppermute x4, waiting for transfers between devices, on_device(): moved = lax.ppermute(message, ('param', 'ex'), moves)  4.48 us
    ppermute x1, starting transfers between devices, on_device(): late_backs = lax.ppermute(backs, 'param', [(0, 2), (3, 1), (1, 0), (2, 3)])  2.87 us
    ppermute x1, starting transfers between devices, on_device(): other_acts = lax.ppermute(with_digits(acts, block_counters), 'param', swap)  2.65 us
    ppermute x1, waiting for transfers between devices, on_device(): other_acts = lax.ppermute(with_digits(acts, block_counters), 'param', swap)  2.37 us
    unnamed x5, local copies, waits for them, and re-layouts  1.79 us
  transfers between devices with their start and end apart: 11, of which 5 were waited for; matrix products, arithmetic and copies ran while one was open for 1% of the time, Pallas kernels for 33%

profile of v3, /device:TPU:0, one launch (start us, length us, event | category | flops | bytes accessed | tf_op | source)
XLA Modules:
  0.0 60.4 jit_solution(17183917430528684746)
XLA Ops:
  0.6 0.5 collective-permute-start.1
  1.1 0.7 %copy.5.counters_ref.source = s32[2,1]{1,0:T(2,128)S(1)} copy(s32[2,1]{0,1:T(1,128)} %param.5) | data formatting | bytes 16 | tf_op args[2]
  1.9 1.0 %copy-done = bf16[1,256,1024]{2,1,0:T(8,128)(2,1)S(1)} copy-done((bf16[1,256,1024]{2,1,0:T(8,128)(2,1)S(1)}, bf16[1,256,1024]{2,1,0:T(8,128)(2,1)}, u32[]{:S(2)}) %copy-start) | copy-done | bytes 524312
  2.9 0.6 with_digits.1
  3.5 2.7 %collective-permute-start = (bf16[272,1024]{1,0:T(8,128)(2,1)S(1)}, bf16[272,1024]{1,0:T(8,128)(2,1)S(1)}, u32[]{:S(2)}, u32[]{:S(2)}) collective-permute-start(bf16[272,1024]{1,0:T(8,128)(2,1)S(1)} %with_digits.1), channel_id=1, source_target_pairs={{0,4},{4,0},{8,12},{12,8},{1,5},{5,1},{9,13},{13,9},{2,6},{6,2},{1... | collective-permute-start | bytes 1671176 | tf_op jit(solution)/shard_map/ppermute | solution.py:394
  6.2 1.7 %collective-permute-start.2 = (bf16[256,1024]{1,0:T(8,128)(2,1)}, bf16[256,1024]{1,0:T(8,128)(2,1)S(1)}, u32[]{:S(2)}, u32[]{:S(2)}) collective-permute-start(bf16[256,1024]{1,0:T(8,128)(2,1)} %bitcast.7), channel_id=1, source_target_pairs={{0,0},{4,8},{8,4},{12,12},{1,1},{5,9},{9,5},{13,13},{2,2},{6,10},{... | collective-permute-start | bytes 1572872 | tf_op jit(solution)/shard_map/ppermute | solution.py:395
  7.9 2.9 %collective-permute-start.3 = (bf16[256,1024]{1,0:T(8,128)(2,1)}, bf16[256,1024]{1,0:T(8,128)(2,1)S(1)}, u32[]{:S(2)}, u32[]{:S(2)}) collective-permute-start(bf16[256,1024]{1,0:T(8,128)(2,1)} %bitcast.8), channel_id=1, source_target_pairs={{0,8},{12,4},{4,0},{8,12},{1,9},{13,5},{5,1},{9,13},{2,10},{14,6},... | collective-permute-start | bytes 1572872 | tf_op jit(solution)/shard_map/ppermute | solution.py:398
  10.7 3.1 %ahead.3.refs_8_ = bf16[1024,1024]{1,0:T(8,128)(2,1)S(1)} custom-call(s32[2,1]{1,0:T(2,128)S(1)} %copy.5.counters_ref.source), custom_call_target="tpu_custom_call" | custom-call | flops 1048576000 | tf_op jit(solution)/shard_map/ahead/pallas_call | solution.py:131
  13.8 3.5 %left.1 = (f32[1024,512]{1,0:T(8,128)S(1)}, f32[2,256,256]{2,1,0:T(8,128)S(1)}) custom-call(s32[2,1]{1,0:T(2,128)S(1)} %copy.5.counters_ref.source, bf16[256,1024]{1,0:T(8,128)(2,1)S(1)} %bitcast.6, bf16[256,1024]{1,0:T(8,128)(2,1)S(1)} %collective-permute-done.1.refs_1_), custom_call_target="tpu_custom_call" | custom-call | flops 1048576000 | tf_op jit(solution)/shard_map/left/pallas_call | solution.py:131
  17.3 2.4 %collective-permute-done.source = bf16[272,1024]{1,0:T(8,128)(2,1)S(1)} collective-permute-done((bf16[272,1024]{1,0:T(8,128)(2,1)S(1)}, bf16[272,1024]{1,0:T(8,128)(2,1)S(1)}, u32[]{:S(2)}, u32[]{:S(2)}) %collective-permute-start) | collective-permute-done | bytes 557088 | tf_op jit(solution)/shard_map/ppermute | solution.py:394
  19.7 2.6 %ahead.4.refs_9_ = bf16[1024,1024]{1,0:T(8,128)(2,1)S(1)} custom-call(bf16[272,1024]{1,0:T(8,128)(2,1)S(1)} %collective-permute-done.source), custom_call_target="tpu_custom_call" | custom-call | flops 1048576000 | tf_op jit(solution)/shard_map/ahead/pallas_call | solution.py:131
  22.3 2.8 %ahead.5.refs_1_ = bf16[1024,1024]{1,0:T(8,128)(2,1)S(1)} custom-call(bf16[272,1024]{1,0:T(8,128)(2,1)S(1)} %collective-permute-done.source), custom_call_target="tpu_custom_call" | custom-call | flops 1048576000 | tf_op jit(solution)/shard_map/ahead/pallas_call | solution.py:131
  25.1 5.6 %collective-permute-done.3.refs_6_ = bf16[256,1024]{1,0:T(8,128)(2,1)S(1)} collective-permute-done((bf16[256,1024]{1,0:T(8,128)(2,1)}, bf16[256,1024]{1,0:T(8,128)(2,1)S(1)}, u32[]{:S(2)}, u32[]{:S(2)}) %collective-permute-start.3) | collective-permute-done | bytes 524320 | tf_op jit(solution)/shard_map/ppermute | solution.py:398
  31.2 1.4 %collective-permute-done.5.refs_2_.refs_4_ = bf16[256,1024]{1,0:T(8,128)(2,1)S(1)} collective-permute-done((bf16[256,1024]{1,0:T(8,128)(2,1)S(1)}, bf16[256,1024]{1,0:T(8,128)(2,1)S(1)}, u32[]{:S(2)}, u32[]{:S(2)}) %collective-permute-start.5) | collective-permute-done | bytes 524320 | tf_op jit(solution)/shard_map/ppermute | solution.py:392
  32.6 3.5 %middle.2 = (f32[1024,512]{1,0:T(8,128)S(1)}, f32[2,256,256]{2,1,0:T(8,128)S(1)}) custom-call(s32[2,1]{1,0:T(2,128)S(1)} %copy.5.counters_ref.source, f32[1024,512]{1,0:T(8,128)S(1)} %get-tuple-element.22.refs_0_, bf16[256,1024]{1,0:T(8,128)(2,1)S(1)} %collective-permute-done.2.refs_1_.refs_3_, bf16[256,1024]{1,0:T(8,128)(2,1)S(1)} %collective-permute-done.5.refs_2_.refs_4_), custom_call_target="tpu_custom_call" | custom-call | flops 1048576000 | tf_op jit(solution)/shard_map/middle/pallas_call | solution.py:131
  36.2 3.7 %middle.3 = (f32[1024,512]{1,0:T(8,128)S(1)}, f32[2,256,256]{2,1,0:T(8,128)S(1)}, f32[1024,512]{1,0:T(8,128)S(1)}) custom-call(bf16[272,1024]{1,0:T(8,128)(2,1)S(1)} %collective-permute-done.source, bf16[272,1024]{1,0:T(8,128)(2,1)S(1)} %collective-permute-done.4.refs_0_, bf16[1024,1024]{1,0:T(8,128)(2,1)S(1)} %ahead.5.refs_1_, ...), custom_call_target="tpu_custom_call" | custom-call | flops 1048576000 | tf_op jit(solution)/shard_map/middle/pallas_call | solution.py:131
  39.9 3.6 %late.1 = (f32[1,640]{1,0:T(1,128)S(1)}, f32[1,640]{1,0:T(1,128)S(1)}, f32[1,640]{1,0:T(1,128)S(1)}, f32[1,640]{1,0:T(1,128)S(1)}) custom-call(f32[1024,512]{1,0:T(8,128)S(1)} %get-tuple-element.22.refs_0_, f32[1024,512]{1,0:T(8,128)S(1)} %get-tuple-element.28.refs_1_, f32[1024,512]{1,0:T(8,128)S(1)} %get-tuple-element.29.refs_2_, ...), custom_call_target="tpu_custom_call" | custom-call | flops 2147483648 | tf_op jit(solution)/shard_map/late/pallas_call | solution.py:131
  43.5 5.9 %collective-permute-start.10 = (f32[1,640]{1,0:T(1,128)S(1)}, f32[1,640]{1,0:T(1,128)S(1)}, u32[]{:S(2)}, u32[]{:S(2)}) collective-permute-start(f32[1,640]{1,0:T(1,128)S(1)} %get-tuple-element.39), channel_id=1, source_target_pairs={{0,5},{1,13},{2,7},{3,15},{4,4},{5,12},{6,6},{7,14},{8,1},{9,9},{1... | collective-permute-start | bytes 7688 | tf_op jit(solution)/shard_map/ppermute | solution.py:443
  49.5 0.7 %collective-permute-start.7 = (f32[1,640]{1,0:T(1,128)S(1)}, f32[1,640]{1,0:T(1,128)S(1)}, u32[]{:S(2)}, u32[]{:S(2)}) collective-permute-start(f32[1,640]{1,0:T(1,128)S(1)} %get-tuple-element.36), channel_id=1, source_target_pairs={{0,0},{1,8},{2,2},{3,10},{4,1},{5,9},{6,3},{7,11},{8,4},{9,12},{10... | collective-permute-start | bytes 7688 | tf_op jit(solution)/shard_map/ppermute | solution.py:443
  50.1 2.9 %collective-permute-start.8 = (f32[1,640]{1,0:T(1,128)S(1)}, f32[1,640]{1,0:T(1,128)S(1)}, u32[]{:S(2)}, u32[]{:S(2)}) collective-permute-start(f32[1,640]{1,0:T(1,128)S(1)} %get-tuple-element.37), channel_id=1, source_target_pairs={{0,1},{1,9},{2,3},{3,11},{4,0},{5,8},{6,2},{7,10},{8,5},{9,13},{10... | collective-permute-start | bytes 7688 | tf_op jit(solution)/shard_map/ppermute | solution.py:443
  53.0 1.2 %collective-permute-done.8 = f32[1,640]{1,0:T(1,128)S(1)} collective-permute-done((f32[1,640]{1,0:T(1,128)S(1)}, f32[1,640]{1,0:T(1,128)S(1)}, u32[]{:S(2)}, u32[]{:S(2)}) %collective-permute-start.8) | collective-permute-done | bytes 2592 | tf_op jit(solution)/shard_map/ppermute | solution.py:443
  54.2 3.2 %collective-permute-done.9 = f32[1,640]{1,0:T(1,128)S(1)} collective-permute-done((f32[1,640]{1,0:T(1,128)S(1)}, f32[1,640]{1,0:T(1,128)S(1)}, u32[]{:S(2)}, u32[]{:S(2)}) %collective-permute-start.9) | collective-permute-done | bytes 2592 | tf_op jit(solution)/shard_map/ppermute | solution.py:443
  57.5 0.5 slice.9
  58.7 0.6 slice_multiply_fusion
  (14 shorter events, 0.5 us)
Async XLA Ops:
  0.6 13.2 %collective-permute-start.1 = (bf16[256,1024]{1,0:T(8,128)(2,1)}, bf16[256,1024]{1,0:T(8,128)(2,1)S(1)}, u32[]{:S(2)}, u32[]{:S(2)}) collective-permute-start(bf16[256,1024]{1,0:T(8,128)(2,1)} %bitcast.4), channel_id=1, source_target_pairs={{0,1},{1,0},{2,3},{3,2},{4,5},{5,4},{6,7},{7,6},{8,9},{9,8},{10,11... | collective-permute-start | bytes 1572872 | tf_op jit(solution)/shard_map/ppermute | solution.py:392
  1.9 1.0 %copy-start = (bf16[1,256,1024]{2,1,0:T(8,128)(2,1)S(1)}, bf16[1,256,1024]{2,1,0:T(8,128)(2,1)}, u32[]{:S(2)}) copy-start(bf16[1,256,1024]{2,1,0:T(8,128)(2,1)} %param.3) | copy-start | bytes 1572868
  3.5 10.3 %copy-start.1 = (bf16[1,256,1024]{2,1,0:T(8,128)(2,1)S(1)}, bf16[1,256,1024]{2,1,0:T(8,128)(2,1)}, u32[]{:S(2)}) copy-start(bf16[1,256,1024]{2,1,0:T(8,128)(2,1)} %param.3) | copy-start | bytes 1572868
  3.5 16.1 %collective-permute-start = (bf16[272,1024]{1,0:T(8,128)(2,1)S(1)}, bf16[272,1024]{1,0:T(8,128)(2,1)S(1)}, u32[]{:S(2)}, u32[]{:S(2)}) collective-permute-start(bf16[272,1024]{1,0:T(8,128)(2,1)S(1)} %with_digits.1), channel_id=1, source_target_pairs={{0,4},{4,0},{8,12},{12,8},{1,5},{5,1},{9,13},{13,9},{2,6},{6,2},{1... | collective-permute-start | bytes 1671176 | tf_op jit(solution)/shard_map/ppermute | solution.py:394
  6.2 18.9 %collective-permute-start.2 = (bf16[256,1024]{1,0:T(8,128)(2,1)}, bf16[256,1024]{1,0:T(8,128)(2,1)S(1)}, u32[]{:S(2)}, u32[]{:S(2)}) collective-permute-start(bf16[256,1024]{1,0:T(8,128)(2,1)} %bitcast.7), channel_id=1, source_target_pairs={{0,0},{4,8},{8,4},{12,12},{1,1},{5,9},{9,5},{13,13},{2,2},{6,10},{... | collective-permute-start | bytes 1572872 | tf_op jit(solution)/shard_map/ppermute | solution.py:395
  7.9 22.8 %collective-permute-start.3 = (bf16[256,1024]{1,0:T(8,128)(2,1)}, bf16[256,1024]{1,0:T(8,128)(2,1)S(1)}, u32[]{:S(2)}, u32[]{:S(2)}) collective-permute-start(bf16[256,1024]{1,0:T(8,128)(2,1)} %bitcast.8), channel_id=1, source_target_pairs={{0,8},{12,4},{4,0},{8,12},{1,9},{13,5},{5,1},{9,13},{2,10},{14,6},... | collective-permute-start | bytes 1572872 | tf_op jit(solution)/shard_map/ppermute | solution.py:398
  30.7 1.9 %collective-permute-start.5 = (bf16[256,1024]{1,0:T(8,128)(2,1)S(1)}, bf16[256,1024]{1,0:T(8,128)(2,1)S(1)}, u32[]{:S(2)}, u32[]{:S(2)}) collective-permute-start(bf16[256,1024]{1,0:T(8,128)(2,1)S(1)} %collective-permute-done.2.refs_1_.refs_3_), channel_id=1, source_target_pairs={{0,1},{1,0},{2,3},{3,2},{4,5},{5,4},{6,7},{7,6},{8,9},{9,8},{10,11... | collective-permute-start | bytes 1572872 | tf_op jit(solution)/shard_map/ppermute | solution.py:392
  30.7 5.5 %collective-permute-start.4 = (bf16[272,1024]{1,0:T(8,128)(2,1)S(1)}, bf16[272,1024]{1,0:T(8,128)(2,1)S(1)}, u32[]{:S(2)}, u32[]{:S(2)}) collective-permute-start(bf16[272,1024]{1,0:T(8,128)(2,1)S(1)} %collective-permute-done.source), channel_id=1, source_target_pairs={{0,1},{1,0},{2,3},{3,2},{4,5},{5,4},{6,7},{7,6},{8,9},{9,8},{10,11... | collective-permute-start | bytes 1671176 | tf_op jit(solution)/shard_map/ppermute | solution.py:392
  31.2 8.7 %collective-permute-start.6 = (bf16[256,1024]{1,0:T(8,128)(2,1)S(1)}, bf16[256,1024]{1,0:T(8,128)(2,1)S(1)}, u32[]{:S(2)}, u32[]{:S(2)}) collective-permute-start(bf16[256,1024]{1,0:T(8,128)(2,1)S(1)} %collective-permute-done.3.refs_6_), channel_id=1, source_target_pairs={{0,1},{1,0},{2,3},{3,2},{4,5},{5,4},{6,7},{7,6},{8,9},{9,8},{10,11... | collective-permute-start | bytes 1572872 | tf_op jit(solution)/shard_map/ppermute | solution.py:392
  43.5 9.5 %collective-permute-start.10 = (f32[1,640]{1,0:T(1,128)S(1)}, f32[1,640]{1,0:T(1,128)S(1)}, u32[]{:S(2)}, u32[]{:S(2)}) collective-permute-start(f32[1,640]{1,0:T(1,128)S(1)} %get-tuple-element.39), channel_id=1, source_target_pairs={{0,5},{1,13},{2,7},{3,15},{4,4},{5,12},{6,6},{7,14},{8,1},{9,9},{1... | collective-permute-start | bytes 7688 | tf_op jit(solution)/shard_map/ppermute | solution.py:443
  49.5 3.5 %collective-permute-start.7 = (f32[1,640]{1,0:T(1,128)S(1)}, f32[1,640]{1,0:T(1,128)S(1)}, u32[]{:S(2)}, u32[]{:S(2)}) collective-permute-start(f32[1,640]{1,0:T(1,128)S(1)} %get-tuple-element.36), channel_id=1, source_target_pairs={{0,0},{1,8},{2,2},{3,10},{4,1},{5,9},{6,3},{7,11},{8,4},{9,12},{10... | collective-permute-start | bytes 7688 | tf_op jit(solution)/shard_map/ppermute | solution.py:443
  50.1 4.1 %collective-permute-start.8 = (f32[1,640]{1,0:T(1,128)S(1)}, f32[1,640]{1,0:T(1,128)S(1)}, u32[]{:S(2)}, u32[]{:S(2)}) collective-permute-start(f32[1,640]{1,0:T(1,128)S(1)} %get-tuple-element.37), channel_id=1, source_target_pairs={{0,1},{1,9},{2,3},{3,11},{4,0},{5,8},{6,2},{7,10},{8,5},{9,13},{10... | collective-permute-start | bytes 7688 | tf_op jit(solution)/shard_map/ppermute | solution.py:443
  53.0 4.5 %collective-permute-start.9 = (f32[1,640]{1,0:T(1,128)S(1)}, f32[1,640]{1,0:T(1,128)S(1)}, u32[]{:S(2)}, u32[]{:S(2)}) collective-permute-start(f32[1,640]{1,0:T(1,128)S(1)} %get-tuple-element.38), channel_id=1, source_target_pairs={{0,4},{1,12},{2,6},{3,14},{4,5},{5,13},{6,7},{7,15},{8,0},{9,8},{1... | collective-permute-start | bytes 7688 | tf_op jit(solution)/shard_map/ppermute | solution.py:443

commit v4 on v3

--- a/solution.py
+++ b/solution.py
@@ -73,7 +73,7 @@
 
 def counter(source, which):
     if source.dtype == jnp.int32:
-        return source[which, 0]
+        return source[which]
     row = source[source.shape[0] - 16 :, 0:128].astype(jnp.float32)[0:1]
     lane = lax.broadcasted_iota(jnp.int32, row.shape, 1) - 3 * which
     zero = jnp.zeros_like(row)
@@ -91,10 +91,15 @@
     return counter(source, 1) * stream_factor + place * wrapped(columns * row_factor)
 
 
+def half():
+    core = lax.rem(lax.axis_index("ex"), 2)
+    return jnp.bitwise_xor(core, lax.shift_right_logical(lax.axis_index("param"), 1))
+
+
 def first_dim(halves, dims):
     if halves == 1:
         return jnp.int32(0)
-    return lax.rem(lax.axis_index("ex"), halves) * wrapped(dims * col_factor)
+    return half() * wrapped(dims * col_factor)
 
 
 def places(parts):
@@ -151,7 +156,7 @@
     digits = jnp.zeros((16, rows), jnp.int32)
     for which in range(2):
         for digit in range(3):
-            value = lax.shift_right_logical(counters_ref[which, 0], jnp.int32(8 * digit))
+            value = lax.shift_right_logical(counters_ref[which], jnp.int32(8 * digit))
             digits = jnp.where(lane == 3 * which + digit, jnp.bitwise_and(value, 255), digits)
     out_ref[tokens:, :] = digits.astype(jnp.float32).astype(out_ref.dtype)
 
@@ -170,35 +175,38 @@
     return out
 
 
-def ahead_kernel(parts, halves, is_row, source, out_ref, pattern_ref):
-    _, partner, _, late_at = places(parts)
-    dims, columns = out_ref.shape
+def ahead_kernel(parts, halves, kinds, sources, *refs):
+    sources_in, outs, pattern_ref = refs[:sources], refs[sources:-1], refs[-1]
+    _, partner, early_at, late_at = places(parts)
+    dims, columns = outs[0].shape
     fill_pattern(pattern_ref)
-    if is_row:
-        base = row_base(source, partner, columns)
-    else:
-        base = col_base(source, late_at, columns)
-    base += first_dim(halves, dims)
+    bases = []
+    for kind, which in kinds:
+        if kind == "row":
+            base = row_base(sources_in[which], partner, columns)
+        else:
+            base = col_base(sources_in[which], early_at if kind == "early" else late_at, columns)
+        bases.append(base + first_dim(halves, dims))
 
     def strip(number, carry):
         row = pl.multiple_of(number * sub_rows, sub_rows)
-        hash_rows(pattern_ref, out_ref, base, row, columns)
+        for base, out_ref in zip(bases, outs):
+            hash_rows(pattern_ref, out_ref, base, row, columns)
         return carry
 
-    lax.fori_loop(0, dims // sub_rows, strip, 0, unroll=4)
-
-
-def ahead(parts, halves, is_row, source, columns, dims):
-    (block,) = call(
-        functools.partial(ahead_kernel, parts, halves, is_row),
+    lax.fori_loop(0, dims // sub_rows, strip, 0, unroll=max(1, 4 // len(kinds)))
+
+
+def ahead(parts, halves, kinds, sources, columns, dims):
+    return call(
+        functools.partial(ahead_kernel, parts, halves, kinds, len(sources)),
         "ahead",
-        [source],
-        [jax.ShapeDtypeStruct((dims, columns), jnp.bfloat16)],
+        sources,
+        [jax.ShapeDtypeStruct((dims, columns), jnp.bfloat16)] * len(kinds),
         [pltpu.VMEM((sub_rows, columns), jnp.int32)],
-        1000 * dims * columns,
+        1000 * dims * columns * len(kinds),
         8,
     )
-    return block
 
 
 def left_kernel(parts, halves, examples, source, *refs):
@@ -240,66 +248,79 @@
     )
 
 
-def middle_kernel(parts, halves, examples, paired, source, *refs):
-    if paired:
-        acts, refs = (source, *refs[: examples - 1]), refs[examples - 1 :]
-        row_ref, total_in, refs = refs[0], refs[1], refs[2:]
-    else:
-        u_ref, refs = refs[0], refs[1:]
+def middle_kernel(parts, halves, examples, source, u_ref, *refs):
     backs, refs = refs[:examples], refs[examples:]
-    total_ref, gram_ref, refs = refs[0], refs[1], refs[2:]
-    if paired:
-        u_ref, refs = refs[0], refs[1:]
-    pattern_ref, tiles = refs[0], refs[1:]
+    total_ref, gram_ref, pattern_ref = refs[:3]
+    tiles = refs[3:]
     dims = total_ref.shape[0]
     tokens, columns = backs[0].shape
-    _, _, early_at, _ = places(parts)
     fill_pattern(pattern_ref)
-    base = col_base(source, early_at, columns) + first_dim(halves, dims)
+    base = col_base(source, places(parts)[2], columns) + first_dim(halves, dims)
 
     def hash_at(step, which):
         hash_tile(pattern_ref, tiles[which], base + step * wrapped(tile * col_factor))
 
     def grams():
         for e in range(examples):
-            tokens_of = acts[e][:tokens, :] if paired else backs[e][...]
-            gram_ref[e] = dot_nt(tokens_of, tokens_of)
+            gram_ref[e] = dot_nt(backs[e][...], backs[e][...])
 
     def use(step, which):
         rows = rows_at(step, tile)
         for e in range(examples):
             here = slice(e * tokens, (e + 1) * tokens)
-            right = dot_nt(tiles[which][...], backs[e][...])
-            if paired:
-                u_piece = dot_nt(row_ref[rows, :], acts[e][:tokens, :])
-                u_ref[rows, here] = u_piece
-                total_ref[rows, here] = total_in[rows, here] + u_piece * right
-            else:
-                total_ref[rows, here] = u_ref[rows, here] * right
+            total_ref[rows, here] = u_ref[rows, here] * dot_nt(tiles[which][...], backs[e][...])
 
     stream(dims // tile, hash_at, use, grams)
 
 
-def middle(parts, halves, source, backs, u_own=None, other=None):
+def middle(parts, halves, source, backs, u_own):
     examples = len(backs)
     tokens, columns = backs[0].shape
-    if other is None:
-        operands = [source, u_own, *backs]
-        dims = u_own.shape[0]
-        more = []
-    else:
-        siblings, row_other, total = other
-        operands = [source, *siblings, row_other, total, *backs]
-        dims = total.shape[0]
-        more = [floats(dims, examples * tokens)]
+    dims = u_own.shape[0]
     return call(
-        functools.partial(middle_kernel, parts, halves, examples, other is not None),
+        functools.partial(middle_kernel, parts, halves, examples),
         "middle",
-        operands,
-        [floats(dims, examples * tokens), floats(examples, tokens, tokens), *more],
+        [source, u_own, *backs],
+        [floats(dims, examples * tokens), floats(examples, tokens, tokens)],
         [pltpu.VMEM((sub_rows, columns), jnp.int32)]
         + [pltpu.VMEM((tile, columns), jnp.bfloat16)] * 2,
         1000 * dims * columns,
+        20,
+    )
+
+
+def products_kernel(examples, u_own, row_other, col_own, col_other, *refs):
+    acts, backs = refs[:examples], refs[examples : 2 * examples]
+    total_ref, u_other, gram_a_ref, gram_b_ref = refs[2 * examples :]
+    tokens = backs[0].shape[0]
+    for e in range(examples):
+        here = slice(e * tokens, (e + 1) * tokens)
+        gram_b_ref[e] = dot_nt(backs[e][...], backs[e][...])
+        for first in range(0, total_ref.shape[0], tile):
+            rows = slice(first, first + tile)
+            total_ref[rows, here] = u_own[rows, here] * dot_nt(col_own[rows, :], backs[e][...])
+    for e in range(examples):
+        here = slice(e * tokens, (e + 1) * tokens)
+        gram_a_ref[e] = dot_nt(acts[e][:tokens, :], acts[e][:tokens, :])
+        for first in range(0, total_ref.shape[0], tile):
+            rows = slice(first, first + tile)
+            u_piece = dot_nt(row_other[rows, :], acts[e][:tokens, :])
+            u_other[rows, here] = u_piece
+            total_ref[rows, here] += u_piece * dot_nt(col_other[rows, :], backs[e][...])
+
+
+def products(u_own, row_other, cols, acts, backs):
+    examples = len(backs)
+    tokens = backs[0].shape[0]
+    dims, lanes = u_own.shape
+    gram = floats(examples, tokens, tokens)
+    return call(
+        functools.partial(products_kernel, examples),
+        "products",
+        [u_own, row_other, *cols, *acts, *backs],
+        [floats(dims, lanes), floats(dims, lanes), gram, gram],
+        [],
+        4000 * dims * lanes,
         20,
     )
 
@@ -318,14 +339,12 @@
     dims = total_ref.shape[0]
     part_dims = outs[0].shape[1] - 128
     place = lax.axis_index("param")
-    if halves == 2:
-        core = lax.rem(lax.axis_index("ex"), 2)
 
     def send(e, number, columns, values):
         if halves == 1:
             slot = lax.rem(number - place + parts, parts)
         else:
-            slot = jnp.bitwise_xor(2 * number + jnp.bitwise_xor(core, e), place)
+            slot = 2 * jnp.bitwise_xor(number, jnp.bitwise_and(place, 1)) + e
         for which, out in enumerate(outs):
 
             @pl.when(slot == which)
@@ -379,7 +398,8 @@
 
 
 def on_device(parts, group, activations, backprops, block_counters):
-    columns = backprops.shape[2]
+    tokens, columns = backprops.shape[1:]
+    counters = block_counters.reshape(2)
     acts = activations[0]
     backs = backprops[0]
     if parts == 4 and group % 2 == 0:
@@ -391,24 +411,30 @@
             pairs = [(device, device ^ 1) for device in range(group)]
             return [array, lax.ppermute(array, "ex", pairs)]
 
-        other_acts = lax.ppermute(with_digits(acts, block_counters), "param", swap)
+        other_acts = lax.ppermute(with_digits(acts, counters), "param", swap)
         early_backs = lax.ppermute(backs, "param", [(0, 0), (1, 2), (2, 1), (3, 3)])
         own_pair = with_sibling(acts)
-        late_own = ahead(parts, halves, False, block_counters, columns, dims)
         late_backs = lax.ppermute(backs, "param", [(0, 2), (3, 1), (1, 0), (2, 3)])
-        u_own, gram_own = left(parts, halves, block_counters, own_pair, dims)
+        (late_own,) = ahead(parts, halves, [("late", 0)], [counters], columns, dims)
+        u_own, gram_own = left(parts, halves, counters, own_pair, dims)
         other_acts, u_own, late_own = lax.optimization_barrier((other_acts, u_own, late_own))
-        late_other = ahead(parts, halves, False, other_acts, columns, dims)
-        row_other = ahead(parts, halves, True, other_acts, columns, dims)
-        other_acts, early_backs, late_backs, late_other, row_other = lax.optimization_barrier(
-            (other_acts, early_backs, late_backs, late_other, row_other)
+        made = ahead(
+            parts,
+            halves,
+            [("early", 0), ("early", 1), ("late", 1), ("row", 1)],
+            [counters, other_acts],
+            columns,
+            dims,
+        )
+        other_acts, early_backs, late_backs, made = lax.optimization_barrier(
+            (other_acts, early_backs, late_backs, made)
         )
         early_pair = with_sibling(early_backs)
         other_pair = with_sibling(other_acts)
         late_pair = with_sibling(late_backs)
-        total, gram_early = middle(parts, halves, block_counters, early_pair, u_own=u_own)
-        total, gram_other, u_other = middle(
-            parts, halves, other_acts, early_pair, other=(other_pair[1:], row_other, total)
+        *early_cols, late_other, row_other = made
+        total, u_other, gram_other, gram_early = products(
+            u_own, row_other, early_cols, other_pair, early_pair
         )
         messages = late(
             parts,
@@ -422,8 +448,8 @@
     else:
         halves = 1
         every_back = lax.all_gather(backs, "param", axis=1, tiled=True)
-        u_own, gram_own = left(parts, halves, block_counters, [acts], K)
-        total, gram_backs = middle(parts, halves, block_counters, [every_back], u_own=u_own)
+        u_own, gram_own = left(parts, halves, counters, [acts], K)
+        total, gram_backs = middle(parts, halves, counters, [every_back], u_own)
         messages = late(parts, halves, [], total, [gram_own, gram_backs], [], [])
     summed = None
     for number, message in enumerate(messages):
@@ -434,7 +460,9 @@
             moves = [
                 (
                     z * group + chip * 2 + core,
-                    (2 * core + (z ^ number) // 2) * group + chip * 2 + (z ^ number) % 2,
+                    (2 * (core ^ z // 2) + (z % 2 ^ number // 2)) * group
+                    + chip * 2
+                    + (core ^ number % 2),
                 )
                 for z in range(parts)
                 for chip in range(group // 2)

time: 60.7 us -> 55.6 us (0.916)
  waiting for transfers between devices: 13.8 us -> 7.84 us
  Pallas kernels: 23.4 us -> 25.5 us
  starting transfers between devices: 17.7 us -> 16.4 us
    ppermute x1, waiting for transfers between devices: 5.59 us -> 0.21 us  [on_device(): late_backs = lax.ppermute(backs, 'param', [(0, 2), (3, 1), (1, 0), (2, 3)])]
    pallas_call x8 -> x6, Pallas kernels: 23.4 us -> 25.5 us  [call(): pl.pallas_call(kernel, in_specs=[pl.BlockSpec(memory_space=space) for spa...]
    ppermute x4, waiting for transfers between devices: 4.48 us -> 3.04 us  [on_device(): moved = lax.ppermute(message, ('param', 'ex'), moves)]
    ppermute x4, starting transfers between devices: 9.45 us -> 8.14 us  [on_device(): moved = lax.ppermute(message, ('param', 'ex'), moves)]
    ppermute x4, waiting for transfers between devices: 1.4 us -> 2.2 us  [with_sibling(): return [array, lax.ppermute(array, 'ex', pairs)]]
    unnamed x5 -> x8, local copies, waits for them, and re-layouts: 1.79 us -> 1.71 us
  transfers between devices with their start and end apart: 11 -> 11, of which waited for: 5 -> 5; matrix products, arithmetic and copies ran while one was open for 1% -> 0% of each run, Pallas kernels for 33% -> 40%
where the time goes in v4:
time: 55.6 us; the launch traced here: 55.1 us
  Pallas kernels  25.5 us (46%)
  starting transfers between devices  16.4 us (29%)
  waiting for transfers between devices  7.84 us (14%)
  between operations  2.61 us (5%)
  local copies, waits for them, and re-layouts  2.22 us (4%)
  other arithmetic  0.59 us (1%)
    pallas_call x6, Pallas kernels, call(): pl.pallas_call(kernel, in_specs=[pl.BlockSpec(memory_space=space) for spa...  25.5 us
    ppermute x4, starting transfers between devices, on_device(): moved = lax.ppermute(message, ('param', 'ex'), moves)  8.14 us
    ppermute x4, waiting for transfers between devices, on_device(): moved = lax.ppermute(message, ('param', 'ex'), moves)  3.04 us
    ppermute x1, starting transfers between devices, on_device(): late_backs = lax.ppermute(backs, 'param', [(0, 2), (3, 1), (1, 0), (2, 3)])  2.87 us
    ppermute x1, starting transfers between devices, on_device(): other_acts = lax.ppermute(with_digits(acts, counters), 'param', swap)  2.65 us
    ppermute x1, waiting for transfers between devices, on_device(): other_acts = lax.ppermute(with_digits(acts, counters), 'param', swap)  2.38 us
    ppermute x4, waiting for transfers between devices, with_sibling(): return [array, lax.ppermute(array, 'ex', pairs)]  2.2 us
    unnamed x8, local copies, waits for them, and re-layouts  1.71 us
  transfers between devices with their start and end apart: 11, of which 5 were waited for; matrix products, arithmetic and copies ran while one was open for 0% of the time, Pallas kernels for 40%

profile of v4, /device:TPU:0, one launch (start us, length us, event | category | flops | bytes accessed | tf_op | source)
XLA Modules:
  0.0 55.1 jit_solution(14284129030453735185)
XLA Ops:
  0.6 0.5 collective-permute-start.1
  1.1 1.0 %copy-done = bf16[1,256,1024]{2,1,0:T(8,128)(2,1)S(1)} copy-done((bf16[1,256,1024]{2,1,0:T(8,128)(2,1)S(1)}, bf16[1,256,1024]{2,1,0:T(8,128)(2,1)}, u32[]{:S(2)}) %copy-start) | copy-done | bytes 524312
  2.2 0.7 %copy-done.2 = s32[2,1]{0,1:T(1,128)S(1)} copy-done((s32[2,1]{0,1:T(1,128)S(1)}, s32[2,1]{0,1:T(1,128)}, u32[]{:S(2)}) %copy-start.2) | copy-done | bytes 32
  2.8 0.6 %with_digits.1 = bf16[272,1024]{1,0:T(8,128)(2,1)S(1)} custom-call(bf16[256,1024]{1,0:T(8,128)(2,1)S(1)} %bitcast.6, s32[2]{0:T(128)S(1)} %bitcast.8), custom_call_target="tpu_custom_call" | custom-call | tf_op jit(solution)/shard_map/with_digits/pallas_call | solution.py:136
  3.5 2.7 %collective-permute-start = (bf16[272,1024]{1,0:T(8,128)(2,1)S(1)}, bf16[272,1024]{1,0:T(8,128)(2,1)S(1)}, u32[]{:S(2)}, u32[]{:S(2)}) collective-permute-start(bf16[272,1024]{1,0:T(8,128)(2,1)S(1)} %with_digits.1), channel_id=1, source_target_pairs={{0,4},{4,0},{8,12},{12,8},{1,5},{5,1},{9,13},{13,9},{2,6},{6,2},{1... | collective-permute-start | bytes 1671176 | tf_op jit(solution)/shard_map/ppermute | solution.py:414
  6.1 1.7 %collective-permute-start.2 = (bf16[256,1024]{1,0:T(8,128)(2,1)}, bf16[256,1024]{1,0:T(8,128)(2,1)S(1)}, u32[]{:S(2)}, u32[]{:S(2)}) collective-permute-start(bf16[256,1024]{1,0:T(8,128)(2,1)} %bitcast.12), channel_id=1, source_target_pairs={{0,0},{4,8},{8,4},{12,12},{1,1},{5,9},{9,5},{13,13},{2,2},{6,10},{... | collective-permute-start | bytes 1572872 | tf_op jit(solution)/shard_map/ppermute | solution.py:415
  7.8 2.9 %collective-permute-start.3 = (bf16[256,1024]{1,0:T(8,128)(2,1)}, bf16[256,1024]{1,0:T(8,128)(2,1)S(1)}, u32[]{:S(2)}, u32[]{:S(2)}) collective-permute-start(bf16[256,1024]{1,0:T(8,128)(2,1)} %bitcast.13), channel_id=1, source_target_pairs={{0,8},{12,4},{4,0},{8,12},{1,9},{13,5},{5,1},{9,13},{2,10},{14,6},... | collective-permute-start | bytes 1572872 | tf_op jit(solution)/shard_map/ppermute | solution.py:417
  10.7 3.0 %ahead.2.refs_8_ = bf16[1024,1024]{1,0:T(8,128)(2,1)S(1)} custom-call(s32[2]{0:T(128)S(1)} %bitcast.9), custom_call_target="tpu_custom_call" | custom-call | flops 1048576000 | tf_op jit(solution)/shard_map/ahead/pallas_call | solution.py:136
  13.8 3.5 %left.1 = (f32[1024,512]{1,0:T(8,128)S(1)}, f32[2,256,256]{2,1,0:T(8,128)S(1)}) custom-call(s32[2]{0:T(128)S(1)} %bitcast.10, bf16[256,1024]{1,0:T(8,128)(2,1)S(1)} %bitcast.7, bf16[256,1024]{1,0:T(8,128)(2,1)S(1)} %collective-permute-done.1.refs_1_), custom_call_target="tpu_custom_call" | custom-call | flops 1048576000 | tf_op jit(solution)/shard_map/left/pallas_call | solution.py:136
  17.2 2.4 %collective-permute-done.refs_1_.refs_0_ = bf16[272,1024]{1,0:T(8,128)(2,1)S(1)} collective-permute-done((bf16[272,1024]{1,0:T(8,128)(2,1)S(1)}, bf16[272,1024]{1,0:T(8,128)(2,1)S(1)}, u32[]{:S(2)}, u32[]{:S(2)}) %collective-permute-start) | collective-permute-done | bytes 557088 | tf_op jit(solution)/shard_map/ppermute | solution.py:414
  19.6 10.8 %ahead.3 = (bf16[1024,1024]{1,0:T(8,128)(2,1)S(1)}, bf16[1024,1024]{1,0:T(8,128)(2,1)S(1)}, bf16[1024,1024]{1,0:T(8,128)(2,1)S(1)}, bf16[1024,1024]{1,0:T(8,128)(2,1)S(1)}) custom-call(s32[2]{0:T(128)S(1)} %bitcast.11, bf16[272,1024]{1,0:T(8,128)(2,1)S(1)} %collective-permute-done.refs_1_.refs_0_), custom_call_target="tpu_custom_call" | custom-call | flops 4194304000 | tf_op jit(solution)/shard_map/ahead/pallas_call | solution.py:136
  30.4 0.2 collective-permute-done.3.refs_6_
  30.6 0.5 collective-permute-start.5
  31.1 2.2 %collective-permute-done.5.refs_3_ = bf16[256,1024]{1,0:T(8,128)(2,1)S(1)} collective-permute-done((bf16[256,1024]{1,0:T(8,128)(2,1)S(1)}, bf16[256,1024]{1,0:T(8,128)(2,1)S(1)}, u32[]{:S(2)}, u32[]{:S(2)}) %collective-permute-start.5) | collective-permute-done | bytes 524320 | tf_op jit(solution)/shard_map/ppermute | solution.py:412
  33.3 4.0 %products.1 = (f32[1024,512]{1,0:T(8,128)S(1)}, f32[1024,512]{1,0:T(8,128)S(1)}, f32[2,256,256]{2,1,0:T(8,128)S(1)}, f32[2,256,256]{2,1,0:T(8,128)S(1)}) custom-call(f32[1024,512]{1,0:T(8,128)S(1)} %get-tuple-element.27.u_own.refs_0_, bf16[1024,1024]{1,0:T(8,128)(2,1)S(1)} %get-tuple-element.33.row_other, bf16[1024,1024]{1,0:T(8,128)(2,1)S(1)} %get-tuple-element.34.col_own, ...), custom_call_target="tpu_custom_call" | custom-call | flops 2097152000 | tf_op jit(solution)/shard_map/products/pallas_call | solution.py:136
  37.3 3.6 %late.1 = (f32[1,640]{1,0:T(1,128)S(1)}, f32[1,640]{1,0:T(1,128)S(1)}, f32[1,640]{1,0:T(1,128)S(1)}, f32[1,640]{1,0:T(1,128)S(1)}) custom-call(f32[1024,512]{1,0:T(8,128)S(1)} %get-tuple-element.27.u_own.refs_0_, f32[1024,512]{1,0:T(8,128)S(1)} %get-tuple-element.38.refs_1_, f32[1024,512]{1,0:T(8,128)S(1)} %get-tuple-element.39.refs_2_, ...), custom_call_target="tpu_custom_call" | custom-call | flops 2147483648 | tf_op jit(solution)/shard_map/late/pallas_call | solution.py:136
  41.0 4.1 %collective-permute-start.10 = (f32[1,640]{1,0:T(1,128)S(1)}, f32[1,640]{1,0:T(1,128)S(1)}, u32[]{:S(2)}, u32[]{:S(2)}) collective-permute-start(f32[1,640]{1,0:T(1,128)S(1)} %get-tuple-element.49), channel_id=1, source_target_pairs={{0,5},{1,12},{2,7},{3,14},{4,1},{5,8},{6,3},{7,10},{8,13},{9,4},{1... | collective-permute-start | bytes 7688 | tf_op jit(solution)/shard_map/ppermute | solution.py:471
  45.0 0.6 %collective-permute-start.7 = (f32[1,640]{1,0:T(1,128)S(1)}, f32[1,640]{1,0:T(1,128)S(1)}, u32[]{:S(2)}, u32[]{:S(2)}) collective-permute-start(f32[1,640]{1,0:T(1,128)S(1)} %get-tuple-element.46), channel_id=1, source_target_pairs={{0,0},{1,9},{2,2},{3,11},{4,4},{5,13},{6,6},{7,15},{8,8},{9,1},{10... | collective-permute-start | bytes 7688 | tf_op jit(solution)/shard_map/ppermute | solution.py:471
  45.7 2.9 %collective-permute-start.8 = (f32[1,640]{1,0:T(1,128)S(1)}, f32[1,640]{1,0:T(1,128)S(1)}, u32[]{:S(2)}, u32[]{:S(2)}) collective-permute-start(f32[1,640]{1,0:T(1,128)S(1)} %get-tuple-element.47), channel_id=1, source_target_pairs={{0,1},{1,8},{2,3},{3,10},{4,5},{5,12},{6,7},{7,14},{8,9},{9,0},{10... | collective-permute-start | bytes 7688 | tf_op jit(solution)/shard_map/ppermute | solution.py:471
  48.6 0.5 collective-permute-start.9
  49.1 1.3 %collective-permute-done.8 = f32[1,640]{1,0:T(1,128)S(1)} collective-permute-done((f32[1,640]{1,0:T(1,128)S(1)}, f32[1,640]{1,0:T(1,128)S(1)}, u32[]{:S(2)}, u32[]{:S(2)}) %collective-permute-start.8) | collective-permute-done | bytes 2592 | tf_op jit(solution)/shard_map/ppermute | solution.py:471
  50.4 1.7 %collective-permute-done.9 = f32[1,640]{1,0:T(1,128)S(1)} collective-permute-done((f32[1,640]{1,0:T(1,128)S(1)}, f32[1,640]{1,0:T(1,128)S(1)}, u32[]{:S(2)}, u32[]{:S(2)}) %collective-permute-start.9) | collective-permute-done | bytes 2592 | tf_op jit(solution)/shard_map/ppermute | solution.py:471
  52.2 0.5 slice.9
  53.4 0.6 %slice_multiply_fusion = f32[1,512]{1,0:T(1,128)} fusion(f32[1,640]{1,0:T(1,128)S(1)} %add_add_fusion, f32[]{:T(128)} %bitcast.3), kind=kLoop, calls=%fused_computation.1 | loop fusion | flops 512 | bytes 4100 | tf_op jit(solution)/shard_map/mul | solution.py:475
  (15 shorter events, 0.0 us)
Async XLA Ops:
  0.6 13.1 %collective-permute-start.1 = (bf16[256,1024]{1,0:T(8,128)(2,1)}, bf16[256,1024]{1,0:T(8,128)(2,1)S(1)}, u32[]{:S(2)}, u32[]{:S(2)}) collective-permute-start(bf16[256,1024]{1,0:T(8,128)(2,1)} %bitcast.5), channel_id=1, source_target_pairs={{0,1},{1,0},{2,3},{3,2},{4,5},{5,4},{6,7},{7,6},{8,9},{9,8},{10,11... | collective-permute-start | bytes 1572872 | tf_op jit(solution)/shard_map/ppermute | solution.py:412
  1.1 1.0 %copy-start = (bf16[1,256,1024]{2,1,0:T(8,128)(2,1)S(1)}, bf16[1,256,1024]{2,1,0:T(8,128)(2,1)}, u32[]{:S(2)}) copy-start(bf16[1,256,1024]{2,1,0:T(8,128)(2,1)} %param.3) | copy-start | bytes 1572868
  2.2 0.7 %copy-start.2 = (s32[2,1]{0,1:T(1,128)S(1)}, s32[2,1]{0,1:T(1,128)}, u32[]{:S(2)}) copy-start(s32[2,1]{0,1:T(1,128)} %param.5) | copy-start | bytes 28
  3.4 10.3 %copy-start.1 = (bf16[1,256,1024]{2,1,0:T(8,128)(2,1)S(1)}, bf16[1,256,1024]{2,1,0:T(8,128)(2,1)}, u32[]{:S(2)}) copy-start(bf16[1,256,1024]{2,1,0:T(8,128)(2,1)} %param.3) | copy-start | bytes 1572868
  3.4 10.3 %copy-start.3 = (s32[2,1]{0,1:T(1,128)S(1)}, s32[2,1]{0,1:T(1,128)}, u32[]{:S(2)}) copy-start(s32[2,1]{0,1:T(1,128)} %param.5) | copy-start | bytes 28
  3.5 16.1 %collective-permute-start = (bf16[272,1024]{1,0:T(8,128)(2,1)S(1)}, bf16[272,1024]{1,0:T(8,128)(2,1)S(1)}, u32[]{:S(2)}, u32[]{:S(2)}) collective-permute-start(bf16[272,1024]{1,0:T(8,128)(2,1)S(1)} %with_digits.1), channel_id=1, source_target_pairs={{0,4},{4,0},{8,12},{12,8},{1,5},{5,1},{9,13},{13,9},{2,6},{6,2},{1... | collective-permute-start | bytes 1671176 | tf_op jit(solution)/shard_map/ppermute | solution.py:414
  6.1 24.3 %collective-permute-start.2 = (bf16[256,1024]{1,0:T(8,128)(2,1)}, bf16[256,1024]{1,0:T(8,128)(2,1)S(1)}, u32[]{:S(2)}, u32[]{:S(2)}) collective-permute-start(bf16[256,1024]{1,0:T(8,128)(2,1)} %bitcast.12), channel_id=1, source_target_pairs={{0,0},{4,8},{8,4},{12,12},{1,1},{5,9},{9,5},{13,13},{2,2},{6,10},{... | collective-permute-start | bytes 1572872 | tf_op jit(solution)/shard_map/ppermute | solution.py:415
  7.8 22.8 %collective-permute-start.3 = (bf16[256,1024]{1,0:T(8,128)(2,1)}, bf16[256,1024]{1,0:T(8,128)(2,1)S(1)}, u32[]{:S(2)}, u32[]{:S(2)}) collective-permute-start(bf16[256,1024]{1,0:T(8,128)(2,1)} %bitcast.13), channel_id=1, source_target_pairs={{0,8},{12,4},{4,0},{8,12},{1,9},{13,5},{5,1},{9,13},{2,10},{14,6},... | collective-permute-start | bytes 1572872 | tf_op jit(solution)/shard_map/ppermute | solution.py:417
  30.6 2.7 %collective-permute-start.4 = (bf16[272,1024]{1,0:T(8,128)(2,1)S(1)}, bf16[272,1024]{1,0:T(8,128)(2,1)S(1)}, u32[]{:S(2)}, u32[]{:S(2)}) collective-permute-start(bf16[272,1024]{1,0:T(8,128)(2,1)S(1)} %collective-permute-done.refs_1_.refs_0_), channel_id=1, source_target_pairs={{0,1},{1,0},{2,3},{3,2},{4,5},{5,4},{6,7},{7,6},{8,9},{9,8},{10,11... | collective-permute-start | bytes 1671176 | tf_op jit(solution)/shard_map/ppermute | solution.py:412
  30.6 2.7 %collective-permute-start.5 = (bf16[256,1024]{1,0:T(8,128)(2,1)S(1)}, bf16[256,1024]{1,0:T(8,128)(2,1)S(1)}, u32[]{:S(2)}, u32[]{:S(2)}) collective-permute-start(bf16[256,1024]{1,0:T(8,128)(2,1)S(1)} %collective-permute-done.2.refs_2_), channel_id=1, source_target_pairs={{0,1},{1,0},{2,3},{3,2},{4,5},{5,4},{6,7},{7,6},{8,9},{9,8},{10,11... | collective-permute-start | bytes 1572872 | tf_op jit(solution)/shard_map/ppermute | solution.py:412
  31.1 6.2 %collective-permute-start.6 = (bf16[256,1024]{1,0:T(8,128)(2,1)S(1)}, bf16[256,1024]{1,0:T(8,128)(2,1)S(1)}, u32[]{:S(2)}, u32[]{:S(2)}) collective-permute-start(bf16[256,1024]{1,0:T(8,128)(2,1)S(1)} %collective-permute-done.3.refs_6_), channel_id=1, source_target_pairs={{0,1},{1,0},{2,3},{3,2},{4,5},{5,4},{6,7},{7,6},{8,9},{9,8},{10,11... | collective-permute-start | bytes 1572872 | tf_op jit(solution)/shard_map/ppermute | solution.py:412
  41.0 8.2 %collective-permute-start.10 = (f32[1,640]{1,0:T(1,128)S(1)}, f32[1,640]{1,0:T(1,128)S(1)}, u32[]{:S(2)}, u32[]{:S(2)}) collective-permute-start(f32[1,640]{1,0:T(1,128)S(1)} %get-tuple-element.49), channel_id=1, source_target_pairs={{0,5},{1,12},{2,7},{3,14},{4,1},{5,8},{6,3},{7,10},{8,13},{9,4},{1... | collective-permute-start | bytes 7688 | tf_op jit(solution)/shard_map/ppermute | solution.py:471
  45.0 4.1 %collective-permute-start.7 = (f32[1,640]{1,0:T(1,128)S(1)}, f32[1,640]{1,0:T(1,128)S(1)}, u32[]{:S(2)}, u32[]{:S(2)}) collective-permute-start(f32[1,640]{1,0:T(1,128)S(1)} %get-tuple-element.46), channel_id=1, source_target_pairs={{0,0},{1,9},{2,2},{3,11},{4,4},{5,13},{6,6},{7,15},{8,8},{9,1},{10... | collective-permute-start | bytes 7688 | tf_op jit(solution)/shard_map/ppermute | solution.py:471
  45.7 4.8 %collective-permute-start.8 = (f32[1,640]{1,0:T(1,128)S(1)}, f32[1,640]{1,0:T(1,128)S(1)}, u32[]{:S(2)}, u32[]{:S(2)}) collective-permute-start(f32[1,640]{1,0:T(1,128)S(1)} %get-tuple-element.47), channel_id=1, source_target_pairs={{0,1},{1,8},{2,3},{3,10},{4,5},{5,12},{6,7},{7,14},{8,9},{9,0},{10... | collective-permute-start | bytes 7688 | tf_op jit(solution)/shard_map/ppermute | solution.py:471
  48.6 3.6 %collective-permute-start.9 = (f32[1,640]{1,0:T(1,128)S(1)}, f32[1,640]{1,0:T(1,128)S(1)}, u32[]{:S(2)}, u32[]{:S(2)}) collective-permute-start(f32[1,640]{1,0:T(1,128)S(1)} %get-tuple-element.48), channel_id=1, source_target_pairs={{0,4},{1,13},{2,6},{3,15},{4,0},{5,9},{6,2},{7,11},{8,12},{9,5},{1... | collective-permute-start | bytes 7688 | tf_op jit(solution)/shard_map/ppermute | solution.py:471

commit v5 on v4

--- a/solution.py
+++ b/solution.py
@@ -289,62 +289,66 @@
     )
 
 
-def products_kernel(examples, u_own, row_other, col_own, col_other, *refs):
-    acts, backs = refs[:examples], refs[examples : 2 * examples]
-    total_ref, u_other, gram_a_ref, gram_b_ref = refs[2 * examples :]
-    tokens = backs[0].shape[0]
-    for e in range(examples):
-        here = slice(e * tokens, (e + 1) * tokens)
-        gram_b_ref[e] = dot_nt(backs[e][...], backs[e][...])
-        for first in range(0, total_ref.shape[0], tile):
-            rows = slice(first, first + tile)
-            total_ref[rows, here] = u_own[rows, here] * dot_nt(col_own[rows, :], backs[e][...])
-    for e in range(examples):
-        here = slice(e * tokens, (e + 1) * tokens)
-        gram_a_ref[e] = dot_nt(acts[e][:tokens, :], acts[e][:tokens, :])
-        for first in range(0, total_ref.shape[0], tile):
-            rows = slice(first, first + tile)
-            u_piece = dot_nt(row_other[rows, :], acts[e][:tokens, :])
-            u_other[rows, here] = u_piece
-            total_ref[rows, here] += u_piece * dot_nt(col_other[rows, :], backs[e][...])
-
-
-def products(u_own, row_other, cols, acts, backs):
-    examples = len(backs)
-    tokens = backs[0].shape[0]
-    dims, lanes = u_own.shape
-    gram = floats(examples, tokens, tokens)
+def example_kernel(which, *refs):
+    u_own, row_other, early_own, early_other, late_own, late_other = refs[:6]
+    acts, early_backs, late_backs, gram_own = refs[6:10]
+    outs = refs[10:]
+    tokens = early_backs.shape[0]
+    dims = row_other.shape[0]
+    part_dims = outs[0].shape[1] - 128
+    here = slice(which * tokens, (which + 1) * tokens)
+    across = []
+    for first in range(0, dims, tile):
+        rows = slice(first, first + tile)
+        right_own = dot_nt(early_own[rows, :], early_backs[...])
+        right_own += dot_nt(late_own[rows, :], late_backs[...])
+        right_other = dot_nt(early_other[rows, :], early_backs[...])
+        right_other += dot_nt(late_other[rows, :], late_backs[...])
+        u_other = dot_nt(row_other[rows, :], acts[:tokens, :])
+        total = u_own[rows, here] * right_own + u_other * right_other
+        lane_sum = total[:, :128]
+        for begin in range(128, tokens, 128):
+            lane_sum += total[:, begin : begin + 128]
+        across.append(jnp.sum(lane_sum.T, axis=0, keepdims=True))
+    gram_a = gram_own[which] + dot_nt(acts[:tokens, :], acts[:tokens, :])
+    gram_b = dot_nt(early_backs[...], early_backs[...]) + dot_nt(late_backs[...], late_backs[...])
+    both = jnp.full((1, 128), jnp.sum(gram_a * gram_b), jnp.float32)
+    low = jnp.bitwise_and(lax.axis_index("param"), 1)
+    for number in range(len(outs)):
+        slot = jnp.bitwise_xor(number, low)
+        for at, out in enumerate(outs):
+
+            @pl.when(slot == at)
+            def _():
+                out[:, part_dims:] = both
+                for begin in range(0, part_dims, tile):
+                    step = (number * part_dims + begin) // tile
+                    out[:, begin : begin + tile] = across[step]
+
+
+def one_example(which, u_own, made, acts, early_backs, late_backs, gram_own, parts):
+    dims = made[0].shape[0]
+    early_own, early_other, late_own, late_other, row_other = made
     return call(
-        functools.partial(products_kernel, examples),
-        "products",
-        [u_own, row_other, *cols, *acts, *backs],
-        [floats(dims, lanes), floats(dims, lanes), gram, gram],
+        functools.partial(example_kernel, which),
+        "one_example",
+        [u_own, row_other, early_own, early_other, late_own, late_other]
+        + [acts, early_backs, late_backs, gram_own],
+        [floats(1, dims * 2 // parts + 128)] * 2,
         [],
-        4000 * dims * lanes,
-        20,
-    )
-
-
-def late_kernel(parts, halves, examples, blocks, *refs):
-    u_refs, refs = refs[:blocks], refs[blocks:]
-    total_ref, refs = refs[0], refs[1:]
-    sides = max(blocks, 1)
-    grams_a, grams_b, refs = refs[:sides], refs[sides], refs[sides + 1 :]
-    backs = ()
-    if blocks:
-        backs, refs = refs[:examples], refs[examples:]
-        cols, refs = refs[:blocks], refs[blocks:]
-    outs = refs
-    tokens = grams_b.shape[1]
+        4 * 10**9,
+        24,
+    )
+
+
+def sums_kernel(parts, examples, total_ref, gram_a_ref, gram_b_ref, *outs):
+    tokens = gram_b_ref.shape[1]
     dims = total_ref.shape[0]
     part_dims = outs[0].shape[1] - 128
     place = lax.axis_index("param")
 
-    def send(e, number, columns, values):
-        if halves == 1:
-            slot = lax.rem(number - place + parts, parts)
-        else:
-            slot = 2 * jnp.bitwise_xor(number, jnp.bitwise_and(place, 1)) + e
+    def send(number, columns, values):
+        slot = lax.rem(number - place + parts, parts)
         for which, out in enumerate(outs):
 
             @pl.when(slot == which)
@@ -352,49 +356,57 @@
                 out[:, columns] = values
 
     across = []
-    for e in range(examples):
-        here = slice(e * tokens, (e + 1) * tokens)
-        for step in range(dims // tile):
-            rows = slice(step * tile, (step + 1) * tile)
-            total = total_ref[rows, here]
-            for block in range(blocks):
-                total += u_refs[block][rows, here] * dot_nt(cols[block][rows, :], backs[e][...])
-            lane_sum = total[:, :128]
-            for begin in range(128, tokens, 128):
-                lane_sum += total[:, begin : begin + 128]
-            across.append(jnp.sum(lane_sum.T, axis=0, keepdims=True))
-    for e in range(examples):
-        gram_a = grams_a[0][e]
-        for more in grams_a[1:]:
-            gram_a = gram_a + more[e]
-        gram_b = grams_b[e]
-        if blocks:
-            gram_b = gram_b + dot_nt(backs[e][...], backs[e][...])
-        both = jnp.full((1, 128), jnp.sum(gram_a * gram_b), jnp.float32)
-        for number in range(parts // halves):
-            send(e, number, slice(part_dims, part_dims + 128), both)
-            step_dims = min(tile, part_dims)
-            for begin in range(0, part_dims, step_dims):
-                at = number * part_dims + begin
-                step, inside = divmod(at, tile)
-                values = across[e * (dims // tile) + step][:, inside : inside + step_dims]
-                send(e, number, slice(begin, begin + step_dims), values)
-
-
-def late(parts, halves, us, total, grams, backs, cols):
-    blocks = len(cols)
-    dims, lanes = total.shape
-    examples, tokens = grams[0].shape[:2]
-    message = jax.ShapeDtypeStruct((1, dims * halves // parts + 128), jnp.float32)
+    for step in range(dims // tile):
+        total = total_ref[step * tile : (step + 1) * tile, :]
+        lane_sum = total[:, :128]
+        for begin in range(128, tokens, 128):
+            lane_sum += total[:, begin : begin + 128]
+        across.append(jnp.sum(lane_sum.T, axis=0, keepdims=True))
+    both = jnp.full((1, 128), jnp.sum(gram_a_ref[0] * gram_b_ref[0]), jnp.float32)
+    step_dims = min(tile, part_dims)
+    for number in range(parts):
+        send(number, slice(part_dims, part_dims + 128), both)
+        for begin in range(0, part_dims, step_dims):
+            step, inside = divmod(number * part_dims + begin, tile)
+            send(number, slice(begin, begin + step_dims), across[step][:, inside : inside + step_dims])
+
+
+def sums(parts, total, gram_a, gram_b):
+    message = floats(1, total.shape[0] // parts + 128)
     return call(
-        functools.partial(late_kernel, parts, halves, examples, blocks),
-        "late",
-        [*us[:blocks], total, *grams, *backs, *cols],
+        functools.partial(sums_kernel, parts, 1),
+        "sums",
+        [total, gram_a, gram_b],
         [message] * parts,
         [],
-        2 * blocks * dims * lanes * 1024,
-        24,
-    )
+        10**9,
+        16,
+    )
+
+
+def finish_kernel(*refs):
+    messages, (features_ref, norm_ref) = refs[:-2], refs[-2:]
+    part_dims = features_ref.shape[1]
+    summed = messages[0][...]
+    for message in messages[1:]:
+        summed += message[...]
+    sumsq = jnp.maximum(summed[:, part_dims : part_dims + 128], 0.0)
+    scale = lax.rsqrt(sumsq + epsilon) * unscale
+    for begin in range(0, part_dims, 128):
+        width = min(128, part_dims - begin)
+        features_ref[:, begin : begin + width] = summed[:, begin : begin + width] * scale[:, :width]
+    norm_ref[0] = jnp.max(jnp.sqrt(sumsq))
+
+
+def finish(messages, part_dims):
+    return pl.pallas_call(
+        finish_kernel,
+        in_specs=[pl.BlockSpec(memory_space=pltpu.VMEM)] * len(messages),
+        out_specs=[pl.BlockSpec(memory_space=space) for space in (pltpu.VMEM, pltpu.SMEM)],
+        out_shape=[floats(1, part_dims), floats(1)],
+        compiler_params=pltpu.CompilerParams(vmem_limit_bytes=4 * 2**20),
+        name="finish",
+    )(*messages)
 
 
 def on_device(parts, group, activations, backprops, block_counters):
@@ -432,30 +444,32 @@
         early_pair = with_sibling(early_backs)
         other_pair = with_sibling(other_acts)
         late_pair = with_sibling(late_backs)
-        *early_cols, late_other, row_other = made
-        total, u_other, gram_other, gram_early = products(
-            u_own, row_other, early_cols, other_pair, early_pair
-        )
-        messages = late(
-            parts,
-            halves,
-            [u_own, u_other],
-            total,
-            [gram_own, gram_other, gram_early],
-            late_pair,
-            [late_own, late_other],
-        )
+        early_own, early_other, late_other, row_other = made
+        made = [early_own, early_other, late_own, late_other, row_other]
+        messages = [None] * parts
+        for which in range(2):
+            messages[which], messages[2 + which] = one_example(
+                which,
+                u_own,
+                made,
+                other_pair[which],
+                early_pair[which],
+                late_pair[which],
+                gram_own,
+                parts,
+            )
+        messages = lax.optimization_barrier(messages)
     else:
         halves = 1
         every_back = lax.all_gather(backs, "param", axis=1, tiled=True)
         u_own, gram_own = left(parts, halves, counters, [acts], K)
         total, gram_backs = middle(parts, halves, counters, [every_back], u_own)
-        messages = late(parts, halves, [], total, [gram_own, gram_backs], [], [])
-    summed = None
+        messages = sums(parts, total, gram_own, gram_backs)
+    received = []
     for number, message in enumerate(messages):
         if halves == 1:
             moves = [(source, (source + number) % parts) for source in range(parts)]
-            moved = lax.ppermute(message, "param", moves) if number else message
+            received.append(lax.ppermute(message, "param", moves) if number else message)
         else:
             moves = [
                 (
@@ -468,12 +482,9 @@
                 for chip in range(group // 2)
                 for core in range(2)
             ]
-            moved = lax.ppermute(message, ("param", "ex"), moves)
-        summed = moved if summed is None else summed + moved
-    part_dims = K // parts
-    sumsq = jnp.maximum(summed[:, part_dims], 0.0)
-    features = summed[:, :part_dims] * (lax.rsqrt(sumsq + epsilon) * unscale)[:, None]
-    return (features, jnp.sqrt(sumsq))
+            received.append(lax.ppermute(message, ("param", "ex"), moves))
+    features, norm = finish(received, K // parts)
+    return (features, norm)
 
 
 def solution(mesh):

time: 55.6 us -> 51.7 us (0.930)
  between operations: 2.61 us -> 0.75 us
  other arithmetic: 0.59 us -> 0 us
    ppermute x4, waiting for transfers between devices: 2.2 us -> 0.01 us  [with_sibling(): return [array, lax.ppermute(array, 'ex', pairs)]]
    ppermute x4, waiting for transfers between devices: 3.04 us -> 4.56 us  [on_device(): received.append(lax.ppermute(message, ('param', 'ex'), moves))]
    pallas_call x0 -> x1, Pallas kernels: none -> 0.65 us  [finish(): pl.pallas_call(finish_kernel, in_specs=[pl.BlockSpec(memory_space=pltpu.V...]
    pallas_call x6, Pallas kernels: 25.5 us -> 24.9 us  [call(): pl.pallas_call(kernel, in_specs=[pl.BlockSpec(memory_space=space) for spa...]
    mul x1 -> x0, other arithmetic: 0.58 us -> none  [on_device(): summed[:, :part_dims] * (lax.rsqrt(sumsq + epsilon) * unscale)[:, None]]
  transfers between devices with their start and end apart: 11 -> 11, of which waited for: 5 -> 5; matrix products, arithmetic and copies ran while one was open for 0% -> 0% of each run, Pallas kernels for 40% -> 42%
where the time goes in v5:
time: 51.7 us; the launch traced here: 51.4 us
  Pallas kernels  25.5 us (49%)
  starting transfers between devices  16 us (31%)
  waiting for transfers between devices  7.45 us (14%)
  local copies, waits for them, and re-layouts  1.71 us (3%)
  between operations  0.75 us (1%)
    pallas_call x6, Pallas kernels, call(): pl.pallas_call(kernel, in_specs=[pl.BlockSpec(memory_space=space) for spa...  24.9 us
    ppermute x4, starting transfers between devices, on_device(): received.append(lax.ppermute(message, ('param', 'ex'), moves))  8.05 us
    ppermute x4, waiting for transfers between devices, on_device(): received.append(lax.ppermute(message, ('param', 'ex'), moves))  4.56 us
    ppermute x1, waiting for transfers between devices, on_device(): other_acts = lax.ppermute(with_digits(acts, counters), 'param', swap)  2.65 us
    ppermute x1, starting transfers between devices, on_device(): other_acts = lax.ppermute(with_digits(acts, counters), 'param', swap)  2.65 us
    ppermute x1, starting transfers between devices, on_device(): late_backs = lax.ppermute(backs, 'param', [(0, 2), (3, 1), (1, 0), (2, 3)])  2.59 us
    unnamed x8, local copies, waits for them, and re-layouts  1.71 us
    ppermute x1, starting transfers between devices, on_device(): early_backs = lax.ppermute(backs, 'param', [(0, 0), (1, 2), (2, 1), (3, 3)])  1.69 us
  transfers between devices with their start and end apart: 11, of which 5 were waited for; matrix products, arithmetic and copies ran while one was open for 0% of the time, Pallas kernels for 42%

profile of v5, /device:TPU:0, one launch (start us, length us, event | category | flops | bytes accessed | tf_op | source)
XLA Modules:
  0.0 51.4 jit_solution(458492177626330748)
XLA Ops:
  0.6 0.5 %collective-permute-start.1 = (bf16[256,1024]{1,0:T(8,128)(2,1)}, bf16[256,1024]{1,0:T(8,128)(2,1)S(1)}, u32[]{:S(2)}, u32[]{:S(2)}) collective-permute-start(bf16[256,1024]{1,0:T(8,128)(2,1)} %bitcast.3), channel_id=1, source_target_pairs={{0,1},{1,0},{2,3},{3,2},{4,5},{5,4},{6,7},{7,6},{8,9},{9,8},{10,11... | collective-permute-start | bytes 1572872 | tf_op jit(solution)/shard_map/ppermute | solution.py:424
  1.1 1.0 %copy-done = bf16[1,256,1024]{2,1,0:T(8,128)(2,1)S(1)} copy-done((bf16[1,256,1024]{2,1,0:T(8,128)(2,1)S(1)}, bf16[1,256,1024]{2,1,0:T(8,128)(2,1)}, u32[]{:S(2)}) %copy-start) | copy-done | bytes 524312
  2.2 0.7 %copy-done.2 = s32[2,1]{0,1:T(1,128)S(1)} copy-done((s32[2,1]{0,1:T(1,128)S(1)}, s32[2,1]{0,1:T(1,128)}, u32[]{:S(2)}) %copy-start.2) | copy-done | bytes 32
  2.8 0.6 %with_digits.1 = bf16[272,1024]{1,0:T(8,128)(2,1)S(1)} custom-call(bf16[256,1024]{1,0:T(8,128)(2,1)S(1)} %bitcast.4, s32[2]{0:T(128)S(1)} %bitcast.6), custom_call_target="tpu_custom_call" | custom-call | tf_op jit(solution)/shard_map/with_digits/pallas_call | solution.py:136
  3.4 0.0 copy-start.1
  3.4 0.0 copy-start.3
  3.5 2.7 %collective-permute-start = (bf16[272,1024]{1,0:T(8,128)(2,1)S(1)}, bf16[272,1024]{1,0:T(8,128)(2,1)S(1)}, u32[]{:S(2)}, u32[]{:S(2)}) collective-permute-start(bf16[272,1024]{1,0:T(8,128)(2,1)S(1)} %with_digits.1), channel_id=1, source_target_pairs={{0,4},{4,0},{8,12},{12,8},{1,5},{5,1},{9,13},{13,9},{2,6},{6,2},{1... | collective-permute-start | bytes 1671176 | tf_op jit(solution)/shard_map/ppermute | solution.py:426
  6.1 2.6 %collective-permute-start.3 = (bf16[256,1024]{1,0:T(8,128)(2,1)}, bf16[256,1024]{1,0:T(8,128)(2,1)S(1)}, u32[]{:S(2)}, u32[]{:S(2)}) collective-permute-start(bf16[256,1024]{1,0:T(8,128)(2,1)} %bitcast.10), channel_id=1, source_target_pairs={{0,8},{12,4},{4,0},{8,12},{1,9},{13,5},{5,1},{9,13},{2,10},{14,6},... | collective-permute-start | bytes 1572872 | tf_op jit(solution)/shard_map/ppermute | solution.py:429
  8.7 1.7 %collective-permute-start.2 = (bf16[256,1024]{1,0:T(8,128)(2,1)}, bf16[256,1024]{1,0:T(8,128)(2,1)S(1)}, u32[]{:S(2)}, u32[]{:S(2)}) collective-permute-start(bf16[256,1024]{1,0:T(8,128)(2,1)} %bitcast.11), channel_id=1, source_target_pairs={{0,0},{4,8},{8,4},{12,12},{1,1},{5,9},{9,5},{13,13},{2,2},{6,10},{... | collective-permute-start | bytes 1572872 | tf_op jit(solution)/shard_map/ppermute | solution.py:427
  10.4 3.0 %ahead.2.refs_4_ = bf16[1024,1024]{1,0:T(8,128)(2,1)S(1)} custom-call(s32[2]{0:T(128)S(1)} %bitcast.7), custom_call_target="tpu_custom_call" | custom-call | flops 1048576000 | tf_op jit(solution)/shard_map/ahead/pallas_call | solution.py:136
  13.5 3.5 %left.1 = (f32[1024,512]{1,0:T(8,128)S(1)}, f32[2,256,256]{2,1,0:T(8,128)S(1)}) custom-call(s32[2]{0:T(128)S(1)} %bitcast.8, bf16[256,1024]{1,0:T(8,128)(2,1)S(1)} %bitcast.5, bf16[256,1024]{1,0:T(8,128)(2,1)S(1)} %collective-permute-done.1.refs_1_), custom_call_target="tpu_custom_call" | custom-call | flops 1048576000 | tf_op jit(solution)/shard_map/left/pallas_call | solution.py:136
  16.9 2.7 %collective-permute-done.refs_1_.refs_6_ = bf16[272,1024]{1,0:T(8,128)(2,1)S(1)} collective-permute-done((bf16[272,1024]{1,0:T(8,128)(2,1)S(1)}, bf16[272,1024]{1,0:T(8,128)(2,1)S(1)}, u32[]{:S(2)}, u32[]{:S(2)}) %collective-permute-start) | collective-permute-done | bytes 557088 | tf_op jit(solution)/shard_map/ppermute | solution.py:426
  19.6 10.8 %ahead.3 = (bf16[1024,1024]{1,0:T(8,128)(2,1)S(1)}, bf16[1024,1024]{1,0:T(8,128)(2,1)S(1)}, bf16[1024,1024]{1,0:T(8,128)(2,1)S(1)}, bf16[1024,1024]{1,0:T(8,128)(2,1)S(1)}) custom-call(s32[2]{0:T(128)S(1)} %bitcast.9, bf16[272,1024]{1,0:T(8,128)(2,1)S(1)} %collective-permute-done.refs_1_.refs_6_), custom_call_target="tpu_custom_call" | custom-call | flops 4194304000 | tf_op jit(solution)/shard_map/ahead/pallas_call | solution.py:136
  30.4 0.2 collective-permute-done.3.refs_8_
  30.6 0.5 collective-permute-start.5
  31.1 3.5 %one_example.2 = (f32[1,640]{1,0:T(1,128)S(1)}, f32[1,640]{1,0:T(1,128)S(1)}) custom-call(f32[1024,512]{1,0:T(8,128)S(1)} %get-tuple-element.27.refs_0_, bf16[1024,1024]{1,0:T(8,128)(2,1)S(1)} %get-tuple-element.33.refs_1_, bf16[1024,1024]{1,0:T(8,128)(2,1)S(1)} %get-tuple-element.34.refs_2_, bf16[1024,1024]{1,0:T(8,128)(2,1)S(1)} %get-tuple-element.35.refs_3_, ...), custom_call_target="tpu_custom_call" | custom-call | flops 4000000000 | tf_op jit(solution)/shard_map/one_example/pallas_call | solution.py:136
  34.7 3.5 %one_example.3 = (f32[1,640]{1,0:T(1,128)S(1)}, f32[1,640]{1,0:T(1,128)S(1)}) custom-call(f32[1024,512]{1,0:T(8,128)S(1)} %get-tuple-element.27.refs_0_, bf16[1024,1024]{1,0:T(8,128)(2,1)S(1)} %get-tuple-element.33.refs_1_, bf16[1024,1024]{1,0:T(8,128)(2,1)S(1)} %get-tuple-element.34.refs_2_, bf16[1024,1024]{1,0:T(8,128)(2,1)S(1)} %get-tuple-element.35.refs_3_, ...), custom_call_target="tpu_custom_call" | custom-call | flops 4000000000 | tf_op jit(solution)/shard_map/one_example/pallas_call | solution.py:136
  38.2 0.7 %collective-permute-start.7 = (f32[1,640]{1,0:T(1,128)S(1)}, f32[1,640]{1,0:T(1,128)S(1)}, u32[]{:S(2)}, u32[]{:S(2)}) collective-permute-start(f32[1,640]{1,0:T(1,128)S(1)} %get-tuple-element.46), channel_id=1, source_target_pairs={{0,0},{1,9},{2,2},{3,11},{4,4},{5,13},{6,6},{7,15},{8,8},{9,1},{10... | collective-permute-start | bytes 7688 | tf_op jit(solution)/shard_map/ppermute | solution.py:485
  38.8 7.1 %collective-permute-start.8 = (f32[1,640]{1,0:T(1,128)S(1)}, f32[1,640]{1,0:T(1,128)S(1)}, u32[]{:S(2)}, u32[]{:S(2)}) collective-permute-start(f32[1,640]{1,0:T(1,128)S(1)} %get-tuple-element.47), channel_id=1, source_target_pairs={{0,1},{1,8},{2,3},{3,10},{4,5},{5,12},{6,7},{7,14},{8,9},{9,0},{10... | collective-permute-start | bytes 7688 | tf_op jit(solution)/shard_map/ppermute | solution.py:485
  46.0 0.3 collective-permute-start.10
  46.2 0.9 %collective-permute-done.8.refs_1_ = f32[1,640]{1,0:T(1,128)S(1)} collective-permute-done((f32[1,640]{1,0:T(1,128)S(1)}, f32[1,640]{1,0:T(1,128)S(1)}, u32[]{:S(2)}, u32[]{:S(2)}) %collective-permute-start.8) | collective-permute-done | bytes 2592 | tf_op jit(solution)/shard_map/ppermute | solution.py:485
  47.1 2.4 %collective-permute-done.9.refs_2_ = f32[1,640]{1,0:T(1,128)S(1)} collective-permute-done((f32[1,640]{1,0:T(1,128)S(1)}, f32[1,640]{1,0:T(1,128)S(1)}, u32[]{:S(2)}, u32[]{:S(2)}) %collective-permute-start.9) | collective-permute-done | bytes 2592 | tf_op jit(solution)/shard_map/ppermute | solution.py:485
  49.5 1.2 %collective-permute-done.10.refs_3_ = f32[1,640]{1,0:T(1,128)S(1)} collective-permute-done((f32[1,640]{1,0:T(1,128)S(1)}, f32[1,640]{1,0:T(1,128)S(1)}, u32[]{:S(2)}, u32[]{:S(2)}) %collective-permute-start.10) | collective-permute-done | bytes 2592 | tf_op jit(solution)/shard_map/ppermute | solution.py:485
  50.8 0.6 %finish.1 = (f32[1,512]{1,0:T(1,128)}, f32[1]{0:T(128)}) custom-call(f32[1,640]{1,0:T(1,128)S(1)} %collective-permute-done.7.refs_0_, f32[1,640]{1,0:T(1,128)S(1)} %collective-permute-done.8.refs_1_, f32[1,640]{1,0:T(1,128)S(1)} %collective-permute-done.9.refs_2_, f32[1,640]{1,0:T(1,128)S(1)} %collective-permute-done.10.refs_3_), custom_call_target="tpu_custom_call" | custom-call | tf_op jit(solution)/shard_map/finish/pallas_call | solution.py:402
  (13 shorter events, 0.0 us)
Async XLA Ops:
  0.6 12.8 %collective-permute-start.1 = (bf16[256,1024]{1,0:T(8,128)(2,1)}, bf16[256,1024]{1,0:T(8,128)(2,1)S(1)}, u32[]{:S(2)}, u32[]{:S(2)}) collective-permute-start(bf16[256,1024]{1,0:T(8,128)(2,1)} %bitcast.3), channel_id=1, source_target_pairs={{0,1},{1,0},{2,3},{3,2},{4,5},{5,4},{6,7},{7,6},{8,9},{9,8},{10,11... | collective-permute-start | bytes 1572872 | tf_op jit(solution)/shard_map/ppermute | solution.py:424
  1.1 1.0 %copy-start = (bf16[1,256,1024]{2,1,0:T(8,128)(2,1)S(1)}, bf16[1,256,1024]{2,1,0:T(8,128)(2,1)}, u32[]{:S(2)}) copy-start(bf16[1,256,1024]{2,1,0:T(8,128)(2,1)} %param.3) | copy-start | bytes 1572868
  2.2 0.7 %copy-start.2 = (s32[2,1]{0,1:T(1,128)S(1)}, s32[2,1]{0,1:T(1,128)}, u32[]{:S(2)}) copy-start(s32[2,1]{0,1:T(1,128)} %param.5) | copy-start | bytes 28
  3.4 10.0 %copy-start.1 = (bf16[1,256,1024]{2,1,0:T(8,128)(2,1)S(1)}, bf16[1,256,1024]{2,1,0:T(8,128)(2,1)}, u32[]{:S(2)}) copy-start(bf16[1,256,1024]{2,1,0:T(8,128)(2,1)} %param.3) | copy-start | bytes 1572868
  3.4 10.0 %copy-start.3 = (s32[2,1]{0,1:T(1,128)S(1)}, s32[2,1]{0,1:T(1,128)}, u32[]{:S(2)}) copy-start(s32[2,1]{0,1:T(1,128)} %param.5) | copy-start | bytes 28
  3.5 16.1 %collective-permute-start = (bf16[272,1024]{1,0:T(8,128)(2,1)S(1)}, bf16[272,1024]{1,0:T(8,128)(2,1)S(1)}, u32[]{:S(2)}, u32[]{:S(2)}) collective-permute-start(bf16[272,1024]{1,0:T(8,128)(2,1)S(1)} %with_digits.1), channel_id=1, source_target_pairs={{0,4},{4,0},{8,12},{12,8},{1,5},{5,1},{9,13},{13,9},{2,6},{6,2},{1... | collective-permute-start | bytes 1671176 | tf_op jit(solution)/shard_map/ppermute | solution.py:426
  6.1 24.5 %collective-permute-start.3 = (bf16[256,1024]{1,0:T(8,128)(2,1)}, bf16[256,1024]{1,0:T(8,128)(2,1)S(1)}, u32[]{:S(2)}, u32[]{:S(2)}) collective-permute-start(bf16[256,1024]{1,0:T(8,128)(2,1)} %bitcast.10), channel_id=1, source_target_pairs={{0,8},{12,4},{4,0},{8,12},{1,9},{13,5},{5,1},{9,13},{2,10},{14,6},... | collective-permute-start | bytes 1572872 | tf_op jit(solution)/shard_map/ppermute | solution.py:429
  8.7 21.9 %collective-permute-start.2 = (bf16[256,1024]{1,0:T(8,128)(2,1)}, bf16[256,1024]{1,0:T(8,128)(2,1)S(1)}, u32[]{:S(2)}, u32[]{:S(2)}) collective-permute-start(bf16[256,1024]{1,0:T(8,128)(2,1)} %bitcast.11), channel_id=1, source_target_pairs={{0,0},{4,8},{8,4},{12,12},{1,1},{5,9},{9,5},{13,13},{2,2},{6,10},{... | collective-permute-start | bytes 1572872 | tf_op jit(solution)/shard_map/ppermute | solution.py:427
  30.6 4.0 %collective-permute-start.4 = (bf16[272,1024]{1,0:T(8,128)(2,1)S(1)}, bf16[272,1024]{1,0:T(8,128)(2,1)S(1)}, u32[]{:S(2)}, u32[]{:S(2)}) collective-permute-start(bf16[272,1024]{1,0:T(8,128)(2,1)S(1)} %collective-permute-done.refs_1_.refs_6_), channel_id=1, source_target_pairs={{0,1},{1,0},{2,3},{3,2},{4,5},{5,4},{6,7},{7,6},{8,9},{9,8},{10,11... | collective-permute-start | bytes 1671176 | tf_op jit(solution)/shard_map/ppermute | solution.py:424
  30.6 4.0 %collective-permute-start.5 = (bf16[256,1024]{1,0:T(8,128)(2,1)S(1)}, bf16[256,1024]{1,0:T(8,128)(2,1)S(1)}, u32[]{:S(2)}, u32[]{:S(2)}) collective-permute-start(bf16[256,1024]{1,0:T(8,128)(2,1)S(1)} %collective-permute-done.2.refs_7_), channel_id=1, source_target_pairs={{0,1},{1,0},{2,3},{3,2},{4,5},{5,4},{6,7},{7,6},{8,9},{9,8},{10,11... | collective-permute-start | bytes 1572872 | tf_op jit(solution)/shard_map/ppermute | solution.py:424
  31.1 3.5 %collective-permute-start.6 = (bf16[256,1024]{1,0:T(8,128)(2,1)S(1)}, bf16[256,1024]{1,0:T(8,128)(2,1)S(1)}, u32[]{:S(2)}, u32[]{:S(2)}) collective-permute-start(bf16[256,1024]{1,0:T(8,128)(2,1)S(1)} %collective-permute-done.3.refs_8_), channel_id=1, source_target_pairs={{0,1},{1,0},{2,3},{3,2},{4,5},{5,4},{6,7},{7,6},{8,9},{9,8},{10,11... | collective-permute-start | bytes 1572872 | tf_op jit(solution)/shard_map/ppermute | solution.py:424
  38.2 8.1 %collective-permute-start.7 = (f32[1,640]{1,0:T(1,128)S(1)}, f32[1,640]{1,0:T(1,128)S(1)}, u32[]{:S(2)}, u32[]{:S(2)}) collective-permute-start(f32[1,640]{1,0:T(1,128)S(1)} %get-tuple-element.46), channel_id=1, source_target_pairs={{0,0},{1,9},{2,2},{3,11},{4,4},{5,13},{6,6},{7,15},{8,8},{9,1},{10... | collective-permute-start | bytes 7688 | tf_op jit(solution)/shard_map/ppermute | solution.py:485
  38.8 8.3 %collective-permute-start.8 = (f32[1,640]{1,0:T(1,128)S(1)}, f32[1,640]{1,0:T(1,128)S(1)}, u32[]{:S(2)}, u32[]{:S(2)}) collective-permute-start(f32[1,640]{1,0:T(1,128)S(1)} %get-tuple-element.47), channel_id=1, source_target_pairs={{0,1},{1,8},{2,3},{3,10},{4,5},{5,12},{6,7},{7,14},{8,9},{9,0},{10... | collective-permute-start | bytes 7688 | tf_op jit(solution)/shard_map/ppermute | solution.py:485
  46.0 3.6 %collective-permute-start.9 = (f32[1,640]{1,0:T(1,128)S(1)}, f32[1,640]{1,0:T(1,128)S(1)}, u32[]{:S(2)}, u32[]{:S(2)}) collective-permute-start(f32[1,640]{1,0:T(1,128)S(1)} %get-tuple-element.48), channel_id=1, source_target_pairs={{0,4},{1,13},{2,6},{3,15},{4,0},{5,9},{6,2},{7,11},{8,12},{9,5},{1... | collective-permute-start | bytes 7688 | tf_op jit(solution)/shard_map/ppermute | solution.py:485
  46.0 4.8 %collective-permute-start.10 = (f32[1,640]{1,0:T(1,128)S(1)}, f32[1,640]{1,0:T(1,128)S(1)}, u32[]{:S(2)}, u32[]{:S(2)}) collective-permute-start(f32[1,640]{1,0:T(1,128)S(1)} %get-tuple-element.49), channel_id=1, source_target_pairs={{0,5},{1,12},{2,7},{3,14},{4,1},{5,8},{6,3},{7,10},{8,13},{9,4},{1... | collective-permute-start | bytes 7688 | tf_op jit(solution)/shard_map/ppermute | solution.py:485

commit v6 on v5

--- a/solution.py
+++ b/solution.py
@@ -289,12 +289,33 @@
     )
 
 
+def partner_kernel(row_other, acts, u_ref, gram_ref):
+    tokens = u_ref.shape[1]
+    for first in range(0, u_ref.shape[0], tile):
+        rows = slice(first, first + tile)
+        u_ref[rows, :] = dot_nt(row_other[rows, :], acts[:tokens, :])
+    gram_ref[...] = dot_nt(acts[:tokens, :], acts[:tokens, :])
+
+
+def partner_left(row_other, acts, tokens):
+    dims = row_other.shape[0]
+    return call(
+        partner_kernel,
+        "partner_left",
+        [row_other, acts],
+        [floats(dims, tokens), floats(tokens, tokens)],
+        [],
+        10**9,
+        12,
+    )
+
+
 def example_kernel(which, *refs):
-    u_own, row_other, early_own, early_other, late_own, late_other = refs[:6]
-    acts, early_backs, late_backs, gram_own = refs[6:10]
+    u_own, early_own, early_other, late_own, late_other = refs[:5]
+    first_other, second_other, early_backs, late_backs, gram_own = refs[5:10]
     outs = refs[10:]
     tokens = early_backs.shape[0]
-    dims = row_other.shape[0]
+    dims = early_own.shape[0]
     part_dims = outs[0].shape[1] - 128
     here = slice(which * tokens, (which + 1) * tokens)
     across = []
@@ -304,13 +325,19 @@
         right_own += dot_nt(late_own[rows, :], late_backs[...])
         right_other = dot_nt(early_other[rows, :], early_backs[...])
         right_other += dot_nt(late_other[rows, :], late_backs[...])
-        u_other = dot_nt(row_other[rows, :], acts[:tokens, :])
+        if which:
+            u_other = dot_nt(first_other[rows, :], second_other[:tokens, :])
+        else:
+            u_other = first_other[rows, :]
         total = u_own[rows, here] * right_own + u_other * right_other
         lane_sum = total[:, :128]
         for begin in range(128, tokens, 128):
             lane_sum += total[:, begin : begin + 128]
         across.append(jnp.sum(lane_sum.T, axis=0, keepdims=True))
-    gram_a = gram_own[which] + dot_nt(acts[:tokens, :], acts[:tokens, :])
+    if which:
+        gram_a = gram_own[which] + dot_nt(second_other[:tokens, :], second_other[:tokens, :])
+    else:
+        gram_a = gram_own[which] + second_other[...]
     gram_b = dot_nt(early_backs[...], early_backs[...]) + dot_nt(late_backs[...], late_backs[...])
     both = jnp.full((1, 128), jnp.sum(gram_a * gram_b), jnp.float32)
     low = jnp.bitwise_and(lax.axis_index("param"), 1)
@@ -326,14 +353,12 @@
                     out[:, begin : begin + tile] = across[step]
 
 
-def one_example(which, u_own, made, acts, early_backs, late_backs, gram_own, parts):
-    dims = made[0].shape[0]
-    early_own, early_other, late_own, late_other, row_other = made
+def one_example(which, u_own, cols, other, early_backs, late_backs, gram_own, parts):
+    dims = cols[0].shape[0]
     return call(
         functools.partial(example_kernel, which),
         "one_example",
-        [u_own, row_other, early_own, early_other, late_own, late_other]
-        + [acts, early_backs, late_backs, gram_own],
+        [u_own, *cols, *other, early_backs, late_backs, gram_own],
         [floats(1, dims * 2 // parts + 128)] * 2,
         [],
         4 * 10**9,
@@ -427,32 +452,37 @@
         early_backs = lax.ppermute(backs, "param", [(0, 0), (1, 2), (2, 1), (3, 3)])
         own_pair = with_sibling(acts)
         late_backs = lax.ppermute(backs, "param", [(0, 2), (3, 1), (1, 0), (2, 3)])
-        (late_own,) = ahead(parts, halves, [("late", 0)], [counters], columns, dims)
+        late_own, early_own = ahead(
+            parts, halves, [("late", 0), ("early", 0)], [counters], columns, dims
+        )
         u_own, gram_own = left(parts, halves, counters, own_pair, dims)
-        other_acts, u_own, late_own = lax.optimization_barrier((other_acts, u_own, late_own))
+        other_acts, u_own, late_own, early_own = lax.optimization_barrier(
+            (other_acts, u_own, late_own, early_own)
+        )
         made = ahead(
             parts,
             halves,
-            [("early", 0), ("early", 1), ("late", 1), ("row", 1)],
-            [counters, other_acts],
+            [("early", 0), ("late", 0), ("row", 0)],
+            [other_acts],
             columns,
             dims,
         )
-        other_acts, early_backs, late_backs, made = lax.optimization_barrier(
-            (other_acts, early_backs, late_backs, made)
+        u_other = partner_left(made[2], other_acts, tokens)
+        other_acts, early_backs, late_backs, made, u_other = lax.optimization_barrier(
+            (other_acts, early_backs, late_backs, made, u_other)
         )
         early_pair = with_sibling(early_backs)
         other_pair = with_sibling(other_acts)
         late_pair = with_sibling(late_backs)
-        early_own, early_other, late_other, row_other = made
-        made = [early_own, early_other, late_own, late_other, row_other]
+        early_other, late_other, row_other = made
+        cols = [early_own, early_other, late_own, late_other]
         messages = [None] * parts
-        for which in range(2):
+        for which, other in enumerate((u_other, [row_other, other_pair[1]])):
             messages[which], messages[2 + which] = one_example(
                 which,
                 u_own,
-                made,
-                other_pair[which],
+                cols,
+                other,
                 early_pair[which],
                 late_pair[which],
                 gram_own,

time: 51.7 us -> 51 us (0.986)
    ppermute x1, waiting for transfers between devices: 2.65 us -> 0.09 us  [on_device(): other_acts = lax.ppermute(with_digits(acts, counters), 'param', swap)]
    ppermute x1, waiting for transfers between devices: 0.23 us -> 2.28 us  [on_device(): late_backs = lax.ppermute(backs, 'param', [(0, 2), (3, 1), (1, 0), (2, 3)])]
    pallas_call x6 -> x7, Pallas kernels: 24.9 us -> 24.7 us  [call(): pl.pallas_call(kernel, in_specs=[pl.BlockSpec(memory_space=space) for spa...]
  transfers between devices with their start and end apart: 11 -> 11, of which waited for: 5 -> 6; matrix products, arithmetic and copies ran while one was open for 0% -> 0% of each run, Pallas kernels for 42% -> 42%
where the time goes in v6:
time: 51 us; the launch traced here: 50.7 us
  Pallas kernels  25.3 us (50%)
  starting transfers between devices  15.9 us (31%)
  waiting for transfers between devices  7.07 us (14%)
  local copies, waits for them, and re-layouts  1.7 us (3%)
  between operations  0.72 us (1%)
    pallas_call x7, Pallas kernels, call(): pl.pallas_call(kernel, in_specs=[pl.BlockSpec(memory_space=space) for spa...  24.7 us
    ppermute x4, starting transfers between devices, on_device(): received.append(lax.ppermute(message, ('param', 'ex'), moves))  7.94 us
    ppermute x4, waiting for transfers between devices, on_device(): received.append(lax.ppermute(message, ('param', 'ex'), moves))  4.56 us
    ppermute x1, starting transfers between devices, on_device(): other_acts = lax.ppermute(with_digits(acts, counters), 'param', swap)  2.65 us
    ppermute x1, starting transfers between devices, on_device(): late_backs = lax.ppermute(backs, 'param', [(0, 2), (3, 1), (1, 0), (2, 3)])  2.59 us
    ppermute x1, waiting for transfers between devices, on_device(): late_backs = lax.ppermute(backs, 'param', [(0, 2), (3, 1), (1, 0), (2, 3)])  2.28 us
    unnamed x8, local copies, waits for them, and re-layouts  1.7 us
    ppermute x1, starting transfers between devices, on_device(): early_backs = lax.ppermute(backs, 'param', [(0, 0), (1, 2), (2, 1), (3, 3)])  1.69 us
  transfers between devices with their start and end apart: 11, of which 6 were waited for; matrix products, arithmetic and copies ran while one was open for 0% of the time, Pallas kernels for 42%

profile of v6, /device:TPU:0, one launch (start us, length us, event | category | flops | bytes accessed | tf_op | source)
XLA Modules:
  0.0 50.7 jit_solution(1506374370107725568)
XLA Ops:
  0.6 0.5 %collective-permute-start.1 = (bf16[256,1024]{1,0:T(8,128)(2,1)}, bf16[256,1024]{1,0:T(8,128)(2,1)S(1)}, u32[]{:S(2)}, u32[]{:S(2)}) collective-permute-start(bf16[256,1024]{1,0:T(8,128)(2,1)} %bitcast.3), channel_id=1, source_target_pairs={{0,1},{1,0},{2,3},{3,2},{4,5},{5,4},{6,7},{7,6},{8,9},{9,8},{10,11... | collective-permute-start | bytes 1572872 | tf_op jit(solution)/shard_map/ppermute | solution.py:449
  1.1 1.0 %copy-done = bf16[1,256,1024]{2,1,0:T(8,128)(2,1)S(1)} copy-done((bf16[1,256,1024]{2,1,0:T(8,128)(2,1)S(1)}, bf16[1,256,1024]{2,1,0:T(8,128)(2,1)}, u32[]{:S(2)}) %copy-start) | copy-done | bytes 524312
  2.2 0.7 %copy-done.2 = s32[2,1]{0,1:T(1,128)S(1)} copy-done((s32[2,1]{0,1:T(1,128)S(1)}, s32[2,1]{0,1:T(1,128)}, u32[]{:S(2)}) %copy-start.2) | copy-done | bytes 32
  2.8 0.6 %with_digits.1 = bf16[272,1024]{1,0:T(8,128)(2,1)S(1)} custom-call(bf16[256,1024]{1,0:T(8,128)(2,1)S(1)} %bitcast.4, s32[2]{0:T(128)S(1)} %bitcast.6), custom_call_target="tpu_custom_call" | custom-call | tf_op jit(solution)/shard_map/with_digits/pallas_call | solution.py:136
  3.4 2.7 %collective-permute-start = (bf16[272,1024]{1,0:T(8,128)(2,1)S(1)}, bf16[272,1024]{1,0:T(8,128)(2,1)S(1)}, u32[]{:S(2)}, u32[]{:S(2)}) collective-permute-start(bf16[272,1024]{1,0:T(8,128)(2,1)S(1)} %with_digits.1), channel_id=1, source_target_pairs={{0,4},{4,0},{8,12},{12,8},{1,5},{5,1},{9,13},{13,9},{2,6},{6,2},{1... | collective-permute-start | bytes 1671176 | tf_op jit(solution)/shard_map/ppermute | solution.py:451
  6.1 2.6 %collective-permute-start.3 = (bf16[256,1024]{1,0:T(8,128)(2,1)}, bf16[256,1024]{1,0:T(8,128)(2,1)S(1)}, u32[]{:S(2)}, u32[]{:S(2)}) collective-permute-start(bf16[256,1024]{1,0:T(8,128)(2,1)} %bitcast.9), channel_id=1, source_target_pairs={{0,8},{12,4},{4,0},{8,12},{1,9},{13,5},{5,1},{9,13},{2,10},{14,6},... | collective-permute-start | bytes 1572872 | tf_op jit(solution)/shard_map/ppermute | solution.py:454
  8.7 1.7 %collective-permute-start.2 = (bf16[256,1024]{1,0:T(8,128)(2,1)}, bf16[256,1024]{1,0:T(8,128)(2,1)S(1)}, u32[]{:S(2)}, u32[]{:S(2)}) collective-permute-start(bf16[256,1024]{1,0:T(8,128)(2,1)} %bitcast.10), channel_id=1, source_target_pairs={{0,0},{4,8},{8,4},{12,12},{1,1},{5,9},{9,5},{13,13},{2,2},{6,10},{... | collective-permute-start | bytes 1572872 | tf_op jit(solution)/shard_map/ppermute | solution.py:452
  10.4 5.6 %ahead.2 = (bf16[1024,1024]{1,0:T(8,128)(2,1)S(1)}, bf16[1024,1024]{1,0:T(8,128)(2,1)S(1)}) custom-call(s32[2]{0:T(128)S(1)} %bitcast.7), custom_call_target="tpu_custom_call" | custom-call | flops 2097152000 | tf_op jit(solution)/shard_map/ahead/pallas_call | solution.py:136
  16.0 3.5 %left.1 = (f32[1024,512]{1,0:T(8,128)S(1)}, f32[2,256,256]{2,1,0:T(8,128)S(1)}) custom-call(s32[2]{0:T(128)S(1)} %bitcast.8, bf16[256,1024]{1,0:T(8,128)(2,1)S(1)} %bitcast.5, bf16[256,1024]{1,0:T(8,128)(2,1)S(1)} %collective-permute-done.1.refs_1_), custom_call_target="tpu_custom_call" | custom-call | flops 1048576000 | tf_op jit(solution)/shard_map/left/pallas_call | solution.py:136
  19.5 0.1 collective-permute-done.refs_0_.acts
  19.6 7.9 %ahead.3 = (bf16[1024,1024]{1,0:T(8,128)(2,1)S(1)}, bf16[1024,1024]{1,0:T(8,128)(2,1)S(1)}, bf16[1024,1024]{1,0:T(8,128)(2,1)S(1)}) custom-call(bf16[272,1024]{1,0:T(8,128)(2,1)S(1)} %collective-permute-done.refs_0_.acts), custom_call_target="tpu_custom_call" | custom-call | flops 3145728000 | tf_op jit(solution)/shard_map/ahead/pallas_call | solution.py:136
  27.4 0.9 %partner_left.1 = (f32[1024,256]{1,0:T(8,128)S(1)}, f32[256,256]{1,0:T(8,128)S(1)}) custom-call(bf16[1024,1024]{1,0:T(8,128)(2,1)S(1)} %get-tuple-element.51.row_other.refs_5_, bf16[272,1024]{1,0:T(8,128)(2,1)S(1)} %collective-permute-done.refs_0_.acts), custom_call_target="tpu_custom_call" | custom-call | flops 1000000000 | tf_op jit(solution)/shard_map/partner_left/pallas_call | solution.py:136
  28.3 2.3 %collective-permute-done.3.refs_8_ = bf16[256,1024]{1,0:T(8,128)(2,1)S(1)} collective-permute-done((bf16[256,1024]{1,0:T(8,128)(2,1)}, bf16[256,1024]{1,0:T(8,128)(2,1)S(1)}, u32[]{:S(2)}, u32[]{:S(2)}) %collective-permute-start.3) | collective-permute-done | bytes 524320 | tf_op jit(solution)/shard_map/ppermute | solution.py:454
  30.6 0.5 %collective-permute-start.5 = (bf16[256,1024]{1,0:T(8,128)(2,1)S(1)}, bf16[256,1024]{1,0:T(8,128)(2,1)S(1)}, u32[]{:S(2)}, u32[]{:S(2)}) collective-permute-start(bf16[256,1024]{1,0:T(8,128)(2,1)S(1)} %collective-permute-done.2.refs_7_), channel_id=1, source_target_pairs={{0,1},{1,0},{2,3},{3,2},{4,5},{5,4},{6,7},{7,6},{8,9},{9,8},{10,11... | collective-permute-start | bytes 1572872 | tf_op jit(solution)/shard_map/ppermute | solution.py:449
  31.1 2.8 %one_example.2 = (f32[1,640]{1,0:T(1,128)S(1)}, f32[1,640]{1,0:T(1,128)S(1)}) custom-call(f32[1024,512]{1,0:T(8,128)S(1)} %get-tuple-element.34.refs_0_, bf16[1024,1024]{1,0:T(8,128)(2,1)S(1)} %get-tuple-element.35.refs_1_, bf16[1024,1024]{1,0:T(8,128)(2,1)S(1)} %get-tuple-element.42.refs_2_, bf16[1024,1024]{1,0:T(8,128)(2,1)S(1)} %get-tuple-element.43.refs_3_, ...), custom_call_target="tpu_custom_call" | custom-call | flops 4000000000 | tf_op jit(solution)/shard_map/one_example/pallas_call | solution.py:136
  33.9 0.1 collective-permute-done.6.refs_8_
  34.1 3.5 %one_example.3 = (f32[1,640]{1,0:T(1,128)S(1)}, f32[1,640]{1,0:T(1,128)S(1)}) custom-call(f32[1024,512]{1,0:T(8,128)S(1)} %get-tuple-element.34.refs_0_, bf16[1024,1024]{1,0:T(8,128)(2,1)S(1)} %get-tuple-element.35.refs_1_, bf16[1024,1024]{1,0:T(8,128)(2,1)S(1)} %get-tuple-element.42.refs_2_, bf16[1024,1024]{1,0:T(8,128)(2,1)S(1)} %get-tuple-element.43.refs_3_, ...), custom_call_target="tpu_custom_call" | custom-call | flops 4000000000 | tf_op jit(solution)/shard_map/one_example/pallas_call | solution.py:136
  37.6 0.7 %collective-permute-start.7 = (f32[1,640]{1,0:T(1,128)S(1)}, f32[1,640]{1,0:T(1,128)S(1)}, u32[]{:S(2)}, u32[]{:S(2)}) collective-permute-start(f32[1,640]{1,0:T(1,128)S(1)} %get-tuple-element.56), channel_id=1, source_target_pairs={{0,0},{1,9},{2,2},{3,11},{4,4},{5,13},{6,6},{7,15},{8,8},{9,1},{10... | collective-permute-start | bytes 7688 | tf_op jit(solution)/shard_map/ppermute | solution.py:515
  38.2 7.0 %collective-permute-start.8 = (f32[1,640]{1,0:T(1,128)S(1)}, f32[1,640]{1,0:T(1,128)S(1)}, u32[]{:S(2)}, u32[]{:S(2)}) collective-permute-start(f32[1,640]{1,0:T(1,128)S(1)} %get-tuple-element.57), channel_id=1, source_target_pairs={{0,1},{1,8},{2,3},{3,10},{4,5},{5,12},{6,7},{7,14},{8,9},{9,0},{10... | collective-permute-start | bytes 7688 | tf_op jit(solution)/shard_map/ppermute | solution.py:515
  45.3 0.3 collective-permute-start.10
  45.5 0.9 %collective-permute-done.8.refs_1_ = f32[1,640]{1,0:T(1,128)S(1)} collective-permute-done((f32[1,640]{1,0:T(1,128)S(1)}, f32[1,640]{1,0:T(1,128)S(1)}, u32[]{:S(2)}, u32[]{:S(2)}) %collective-permute-start.8) | collective-permute-done | bytes 2592 | tf_op jit(solution)/shard_map/ppermute | solution.py:515
  46.4 2.4 %collective-permute-done.9.refs_2_ = f32[1,640]{1,0:T(1,128)S(1)} collective-permute-done((f32[1,640]{1,0:T(1,128)S(1)}, f32[1,640]{1,0:T(1,128)S(1)}, u32[]{:S(2)}, u32[]{:S(2)}) %collective-permute-start.9) | collective-permute-done | bytes 2592 | tf_op jit(solution)/shard_map/ppermute | solution.py:515
  48.9 1.2 %collective-permute-done.10.refs_3_ = f32[1,640]{1,0:T(1,128)S(1)} collective-permute-done((f32[1,640]{1,0:T(1,128)S(1)}, f32[1,640]{1,0:T(1,128)S(1)}, u32[]{:S(2)}, u32[]{:S(2)}) %collective-permute-start.10) | collective-permute-done | bytes 2592 | tf_op jit(solution)/shard_map/ppermute | solution.py:515
  50.1 0.6 %finish.1 = (f32[1,512]{1,0:T(1,128)}, f32[1]{0:T(128)}) custom-call(f32[1,640]{1,0:T(1,128)S(1)} %collective-permute-done.7.refs_0_, f32[1,640]{1,0:T(1,128)S(1)} %collective-permute-done.8.refs_1_, f32[1,640]{1,0:T(1,128)S(1)} %collective-permute-done.9.refs_2_, f32[1,640]{1,0:T(1,128)S(1)} %collective-permute-done.10.refs_3_), custom_call_target="tpu_custom_call" | custom-call | tf_op jit(solution)/shard_map/finish/pallas_call | solution.py:427
  (14 shorter events, 0.0 us)
Async XLA Ops:
  0.6 15.4 %collective-permute-start.1 = (bf16[256,1024]{1,0:T(8,128)(2,1)}, bf16[256,1024]{1,0:T(8,128)(2,1)S(1)}, u32[]{:S(2)}, u32[]{:S(2)}) collective-permute-start(bf16[256,1024]{1,0:T(8,128)(2,1)} %bitcast.3), channel_id=1, source_target_pairs={{0,1},{1,0},{2,3},{3,2},{4,5},{5,4},{6,7},{7,6},{8,9},{9,8},{10,11... | collective-permute-start | bytes 1572872 | tf_op jit(solution)/shard_map/ppermute | solution.py:449
  1.1 1.0 %copy-start = (bf16[1,256,1024]{2,1,0:T(8,128)(2,1)S(1)}, bf16[1,256,1024]{2,1,0:T(8,128)(2,1)}, u32[]{:S(2)}) copy-start(bf16[1,256,1024]{2,1,0:T(8,128)(2,1)} %param.3) | copy-start | bytes 1572868
  2.2 0.7 %copy-start.2 = (s32[2,1]{0,1:T(1,128)S(1)}, s32[2,1]{0,1:T(1,128)}, u32[]{:S(2)}) copy-start(s32[2,1]{0,1:T(1,128)} %param.5) | copy-start | bytes 28
  3.4 16.1 %collective-permute-start = (bf16[272,1024]{1,0:T(8,128)(2,1)S(1)}, bf16[272,1024]{1,0:T(8,128)(2,1)S(1)}, u32[]{:S(2)}, u32[]{:S(2)}) collective-permute-start(bf16[272,1024]{1,0:T(8,128)(2,1)S(1)} %with_digits.1), channel_id=1, source_target_pairs={{0,4},{4,0},{8,12},{12,8},{1,5},{5,1},{9,13},{13,9},{2,6},{6,2},{1... | collective-permute-start | bytes 1671176 | tf_op jit(solution)/shard_map/ppermute | solution.py:451
  6.1 9.9 %copy-start.1 = (bf16[1,256,1024]{2,1,0:T(8,128)(2,1)S(1)}, bf16[1,256,1024]{2,1,0:T(8,128)(2,1)}, u32[]{:S(2)}) copy-start(bf16[1,256,1024]{2,1,0:T(8,128)(2,1)} %param.3) | copy-start | bytes 1572868
  6.1 9.9 %copy-start.3 = (s32[2,1]{0,1:T(1,128)S(1)}, s32[2,1]{0,1:T(1,128)}, u32[]{:S(2)}) copy-start(s32[2,1]{0,1:T(1,128)} %param.5) | copy-start | bytes 28
  6.1 24.5 %collective-permute-start.3 = (bf16[256,1024]{1,0:T(8,128)(2,1)}, bf16[256,1024]{1,0:T(8,128)(2,1)S(1)}, u32[]{:S(2)}, u32[]{:S(2)}) collective-permute-start(bf16[256,1024]{1,0:T(8,128)(2,1)} %bitcast.9), channel_id=1, source_target_pairs={{0,8},{12,4},{4,0},{8,12},{1,9},{13,5},{5,1},{9,13},{2,10},{14,6},... | collective-permute-start | bytes 1572872 | tf_op jit(solution)/shard_map/ppermute | solution.py:454
  8.7 21.9 %collective-permute-start.2 = (bf16[256,1024]{1,0:T(8,128)(2,1)}, bf16[256,1024]{1,0:T(8,128)(2,1)S(1)}, u32[]{:S(2)}, u32[]{:S(2)}) collective-permute-start(bf16[256,1024]{1,0:T(8,128)(2,1)} %bitcast.10), channel_id=1, source_target_pairs={{0,0},{4,8},{8,4},{12,12},{1,1},{5,9},{9,5},{13,13},{2,2},{6,10},{... | collective-permute-start | bytes 1572872 | tf_op jit(solution)/shard_map/ppermute | solution.py:452
  30.6 3.5 %collective-permute-start.4 = (bf16[272,1024]{1,0:T(8,128)(2,1)S(1)}, bf16[272,1024]{1,0:T(8,128)(2,1)S(1)}, u32[]{:S(2)}, u32[]{:S(2)}) collective-permute-start(bf16[272,1024]{1,0:T(8,128)(2,1)S(1)} %collective-permute-done.refs_0_.acts), channel_id=1, source_target_pairs={{0,1},{1,0},{2,3},{3,2},{4,5},{5,4},{6,7},{7,6},{8,9},{9,8},{10,11... | collective-permute-start | bytes 1671176 | tf_op jit(solution)/shard_map/ppermute | solution.py:449
  30.6 3.3 %collective-permute-start.5 = (bf16[256,1024]{1,0:T(8,128)(2,1)S(1)}, bf16[256,1024]{1,0:T(8,128)(2,1)S(1)}, u32[]{:S(2)}, u32[]{:S(2)}) collective-permute-start(bf16[256,1024]{1,0:T(8,128)(2,1)S(1)} %collective-permute-done.2.refs_7_), channel_id=1, source_target_pairs={{0,1},{1,0},{2,3},{3,2},{4,5},{5,4},{6,7},{7,6},{8,9},{9,8},{10,11... | collective-permute-start | bytes 1572872 | tf_op jit(solution)/shard_map/ppermute | solution.py:449
  31.1 2.9 %collective-permute-start.6 = (bf16[256,1024]{1,0:T(8,128)(2,1)S(1)}, bf16[256,1024]{1,0:T(8,128)(2,1)S(1)}, u32[]{:S(2)}, u32[]{:S(2)}) collective-permute-start(bf16[256,1024]{1,0:T(8,128)(2,1)S(1)} %collective-permute-done.3.refs_8_), channel_id=1, source_target_pairs={{0,1},{1,0},{2,3},{3,2},{4,5},{5,4},{6,7},{7,6},{8,9},{9,8},{10,11... | collective-permute-start | bytes 1572872 | tf_op jit(solution)/shard_map/ppermute | solution.py:449
  37.6 8.0 %collective-permute-start.7 = (f32[1,640]{1,0:T(1,128)S(1)}, f32[1,640]{1,0:T(1,128)S(1)}, u32[]{:S(2)}, u32[]{:S(2)}) collective-permute-start(f32[1,640]{1,0:T(1,128)S(1)} %get-tuple-element.56), channel_id=1, source_target_pairs={{0,0},{1,9},{2,2},{3,11},{4,4},{5,13},{6,6},{7,15},{8,8},{9,1},{10... | collective-permute-start | bytes 7688 | tf_op jit(solution)/shard_map/ppermute | solution.py:515
  38.2 8.2 %collective-permute-start.8 = (f32[1,640]{1,0:T(1,128)S(1)}, f32[1,640]{1,0:T(1,128)S(1)}, u32[]{:S(2)}, u32[]{:S(2)}) collective-permute-start(f32[1,640]{1,0:T(1,128)S(1)} %get-tuple-element.57), channel_id=1, source_target_pairs={{0,1},{1,8},{2,3},{3,10},{4,5},{5,12},{6,7},{7,14},{8,9},{9,0},{10... | collective-permute-start | bytes 7688 | tf_op jit(solution)/shard_map/ppermute | solution.py:515
  45.3 3.6 %collective-permute-start.9 = (f32[1,640]{1,0:T(1,128)S(1)}, f32[1,640]{1,0:T(1,128)S(1)}, u32[]{:S(2)}, u32[]{:S(2)}) collective-permute-start(f32[1,640]{1,0:T(1,128)S(1)} %get-tuple-element.58), channel_id=1, source_target_pairs={{0,4},{1,13},{2,6},{3,15},{4,0},{5,9},{6,2},{7,11},{8,12},{9,5},{1... | collective-permute-start | bytes 7688 | tf_op jit(solution)/shard_map/ppermute | solution.py:515
  45.3 4.8 %collective-permute-start.10 = (f32[1,640]{1,0:T(1,128)S(1)}, f32[1,640]{1,0:T(1,128)S(1)}, u32[]{:S(2)}, u32[]{:S(2)}) collective-permute-start(f32[1,640]{1,0:T(1,128)S(1)} %get-tuple-element.59), channel_id=1, source_target_pairs={{0,5},{1,12},{2,7},{3,14},{4,1},{5,8},{6,3},{7,10},{8,13},{9,4},{1... | collective-permute-start | bytes 7688 | tf_op jit(solution)/shard_map/ppermute | solution.py:515

commit v7 on v6

--- a/solution.py
+++ b/solution.py
@@ -448,7 +448,8 @@
             pairs = [(device, device ^ 1) for device in range(group)]
             return [array, lax.ppermute(array, "ex", pairs)]
 
-        other_acts = lax.ppermute(with_digits(acts, counters), "param", swap)
+        payload, acts = lax.optimization_barrier((with_digits(acts, counters), acts))
+        other_acts = lax.ppermute(payload, "param", swap)
         early_backs = lax.ppermute(backs, "param", [(0, 0), (1, 2), (2, 1), (3, 3)])
         own_pair = with_sibling(acts)
         late_backs = lax.ppermute(backs, "param", [(0, 2), (3, 1), (1, 0), (2, 3)])

time: 51 us -> 50.4 us (0.988)
  Pallas kernels: 25.3 us -> 26.4 us
  local copies, waits for them, and re-layouts: 1.7 us -> 0.65 us
  waiting for transfers between devices: 7.07 us -> 6.5 us
    unnamed x8 -> x4, local copies, waits for them, and re-layouts: 1.7 us -> 0.65 us
    pallas_call x7, Pallas kernels: 24.7 us -> 25.7 us  [call(): pl.pallas_call(kernel, in_specs=[pl.BlockSpec(memory_space=space) for spa...]
  transfers between devices with their start and end apart: 11 -> 11, of which waited for: 6 -> 5; matrix products, arithmetic and copies ran while one was open for 0% -> 0% of each run, Pallas kernels for 42% -> 42%
where the time goes in v7:
time: 50.4 us; the launch traced here: 50.2 us
  Pallas kernels  26.4 us (52%)
  starting transfers between devices  15.9 us (32%)
  waiting for transfers between devices  6.5 us (13%)
  between operations  0.72 us (1%)
  local copies, waits for them, and re-layouts  0.65 us (1%)
    pallas_call x7, Pallas kernels, call(): pl.pallas_call(kernel, in_specs=[pl.BlockSpec(memory_space=space) for spa...  25.7 us
    ppermute x4, starting transfers between devices, on_device(): received.append(lax.ppermute(message, ('param', 'ex'), moves))  7.96 us
    ppermute x4, waiting for transfers between devices, on_device(): received.append(lax.ppermute(message, ('param', 'ex'), moves))  4.56 us
    ppermute x1, starting transfers between devices, on_device(): other_acts = lax.ppermute(payload, 'param', swap)  2.65 us
    ppermute x1, starting transfers between devices, on_device(): late_backs = lax.ppermute(backs, 'param', [(0, 2), (3, 1), (1, 0), (2, 3)])  2.59 us
    ppermute x1, waiting for transfers between devices, on_device(): late_backs = lax.ppermute(backs, 'param', [(0, 2), (3, 1), (1, 0), (2, 3)])  1.79 us
    ppermute x1, starting transfers between devices, on_device(): early_backs = lax.ppermute(backs, 'param', [(0, 0), (1, 2), (2, 1), (3, 3)])  1.69 us
    ppermute x4, starting transfers between devices, with_sibling(): return [array, lax.ppermute(array, 'ex', pairs)]  1.03 us
  transfers between devices with their start and end apart: 11, of which 5 were waited for; matrix products, arithmetic and copies ran while one was open for 0% of the time, Pallas kernels for 42%

profile of v7, /device:TPU:0, one launch (start us, length us, event | category | flops | bytes accessed | tf_op | source)
XLA Modules:
  0.0 50.2 jit_solution(109442780166781587)
XLA Ops:
  0.6 0.0 copy-start
  0.6 0.6 %copy-done = s32[2,1]{0,1:T(1,128)S(1)} copy-done((s32[2,1]{0,1:T(1,128)S(1)}, s32[2,1]{0,1:T(1,128)}, u32[]{:S(2)}) %copy-start) | copy-done | bytes 32
  1.3 1.1 %with_digits.1 = bf16[272,1024]{1,0:T(8,128)(2,1)S(1)} custom-call(bf16[256,1024]{1,0:T(8,128)(2,1)} %bitcast.acts_ref.refs_0_, s32[2]{0:T(128)S(1)} %bitcast.3), custom_call_target="tpu_custom_call" | custom-call | tf_op jit(solution)/shard_map/with_digits/pallas_call | solution.py:136
  2.4 0.5 %collective-permute-start.1 = (bf16[256,1024]{1,0:T(8,128)(2,1)}, bf16[256,1024]{1,0:T(8,128)(2,1)S(1)}, u32[]{:S(2)}, u32[]{:S(2)}) collective-permute-start(bf16[256,1024]{1,0:T(8,128)(2,1)} %bitcast.acts_ref.refs_0_), channel_id=1, source_target_pairs={{0,1},{1,0},{2,3},{3,2},{4,5},{5,4},{6,7},{7,6},{8,9},{9,8},{10,11... | collective-permute-start | bytes 1572872 | tf_op jit(solution)/shard_map/ppermute | solution.py:449
  2.9 2.7 %collective-permute-start = (bf16[272,1024]{1,0:T(8,128)(2,1)S(1)}, bf16[272,1024]{1,0:T(8,128)(2,1)S(1)}, u32[]{:S(2)}, u32[]{:S(2)}) collective-permute-start(bf16[272,1024]{1,0:T(8,128)(2,1)S(1)} %with_digits.1), channel_id=1, source_target_pairs={{0,4},{4,0},{8,12},{12,8},{1,5},{5,1},{9,13},{13,9},{2,6},{6,2},{1... | collective-permute-start | bytes 1671176 | tf_op jit(solution)/shard_map/ppermute | solution.py:452
  5.6 2.6 %collective-permute-start.3 = (bf16[256,1024]{1,0:T(8,128)(2,1)}, bf16[256,1024]{1,0:T(8,128)(2,1)S(1)}, u32[]{:S(2)}, u32[]{:S(2)}) collective-permute-start(bf16[256,1024]{1,0:T(8,128)(2,1)} %bitcast.6), channel_id=1, source_target_pairs={{0,8},{12,4},{4,0},{8,12},{1,9},{13,5},{5,1},{9,13},{2,10},{14,6},... | collective-permute-start | bytes 1572872 | tf_op jit(solution)/shard_map/ppermute | solution.py:455
  8.1 1.7 %collective-permute-start.2 = (bf16[256,1024]{1,0:T(8,128)(2,1)}, bf16[256,1024]{1,0:T(8,128)(2,1)S(1)}, u32[]{:S(2)}, u32[]{:S(2)}) collective-permute-start(bf16[256,1024]{1,0:T(8,128)(2,1)} %bitcast.7), channel_id=1, source_target_pairs={{0,0},{4,8},{8,4},{12,12},{1,1},{5,9},{9,5},{13,13},{2,2},{6,10},{... | collective-permute-start | bytes 1572872 | tf_op jit(solution)/shard_map/ppermute | solution.py:453
  9.8 5.6 %ahead.2 = (bf16[1024,1024]{1,0:T(8,128)(2,1)S(1)}, bf16[1024,1024]{1,0:T(8,128)(2,1)S(1)}) custom-call(s32[2]{0:T(128)S(1)} %bitcast.4), custom_call_target="tpu_custom_call" | custom-call | flops 2097152000 | tf_op jit(solution)/shard_map/ahead/pallas_call | solution.py:136
  15.5 4.0 %left.1 = (f32[1024,512]{1,0:T(8,128)S(1)}, f32[2,256,256]{2,1,0:T(8,128)S(1)}) custom-call(s32[2]{0:T(128)S(1)} %bitcast.5, bf16[256,1024]{1,0:T(8,128)(2,1)} %bitcast.acts_ref.refs_0_, bf16[256,1024]{1,0:T(8,128)(2,1)S(1)} %collective-permute-done.1.refs_1_), custom_call_target="tpu_custom_call" | custom-call | flops 1048576000 | tf_op jit(solution)/shard_map/left/pallas_call | solution.py:136
  19.4 7.9 %ahead.3 = (bf16[1024,1024]{1,0:T(8,128)(2,1)S(1)}, bf16[1024,1024]{1,0:T(8,128)(2,1)S(1)}, bf16[1024,1024]{1,0:T(8,128)(2,1)S(1)}) custom-call(bf16[272,1024]{1,0:T(8,128)(2,1)S(1)} %collective-permute-done.refs_0_.acts), custom_call_target="tpu_custom_call" | custom-call | flops 3145728000 | tf_op jit(solution)/shard_map/ahead/pallas_call | solution.py:136
  27.3 0.9 %partner_left.1 = (f32[1024,256]{1,0:T(8,128)S(1)}, f32[256,256]{1,0:T(8,128)S(1)}) custom-call(bf16[1024,1024]{1,0:T(8,128)(2,1)S(1)} %get-tuple-element.55.row_other.refs_5_, bf16[272,1024]{1,0:T(8,128)(2,1)S(1)} %collective-permute-done.refs_0_.acts), custom_call_target="tpu_custom_call" | custom-call | flops 1000000000 | tf_op jit(solution)/shard_map/partner_left/pallas_call | solution.py:136
  28.2 1.8 %collective-permute-done.3.refs_8_ = bf16[256,1024]{1,0:T(8,128)(2,1)S(1)} collective-permute-done((bf16[256,1024]{1,0:T(8,128)(2,1)}, bf16[256,1024]{1,0:T(8,128)(2,1)S(1)}, u32[]{:S(2)}, u32[]{:S(2)}) %collective-permute-start.3) | collective-permute-done | bytes 524320 | tf_op jit(solution)/shard_map/ppermute | solution.py:455
  30.0 0.5 %collective-permute-start.5 = (bf16[256,1024]{1,0:T(8,128)(2,1)S(1)}, bf16[256,1024]{1,0:T(8,128)(2,1)S(1)}, u32[]{:S(2)}, u32[]{:S(2)}) collective-permute-start(bf16[256,1024]{1,0:T(8,128)(2,1)S(1)} %collective-permute-done.2.refs_7_), channel_id=1, source_target_pairs={{0,1},{1,0},{2,3},{3,2},{4,5},{5,4},{6,7},{7,6},{8,9},{9,8},{10,11... | collective-permute-start | bytes 1572872 | tf_op jit(solution)/shard_map/ppermute | solution.py:449
  30.5 0.0 collective-permute-start.6
  30.5 2.8 %one_example.2 = (f32[1,640]{1,0:T(1,128)S(1)}, f32[1,640]{1,0:T(1,128)S(1)}) custom-call(f32[1024,512]{1,0:T(8,128)S(1)} %get-tuple-element.38.refs_0_, bf16[1024,1024]{1,0:T(8,128)(2,1)S(1)} %get-tuple-element.39.refs_1_, bf16[1024,1024]{1,0:T(8,128)(2,1)S(1)} %get-tuple-element.46.refs_2_, bf16[1024,1024]{1,0:T(8,128)(2,1)S(1)} %get-tuple-element.47.refs_3_, ...), custom_call_target="tpu_custom_call" | custom-call | flops 4000000000 | tf_op jit(solution)/shard_map/one_example/pallas_call | solution.py:136
  33.3 0.1 collective-permute-done.6.refs_8_
  33.5 3.5 %one_example.3 = (f32[1,640]{1,0:T(1,128)S(1)}, f32[1,640]{1,0:T(1,128)S(1)}) custom-call(f32[1024,512]{1,0:T(8,128)S(1)} %get-tuple-element.38.refs_0_, bf16[1024,1024]{1,0:T(8,128)(2,1)S(1)} %get-tuple-element.39.refs_1_, bf16[1024,1024]{1,0:T(8,128)(2,1)S(1)} %get-tuple-element.46.refs_2_, bf16[1024,1024]{1,0:T(8,128)(2,1)S(1)} %get-tuple-element.47.refs_3_, ...), custom_call_target="tpu_custom_call" | custom-call | flops 4000000000 | tf_op jit(solution)/shard_map/one_example/pallas_call | solution.py:136
  37.0 0.7 %collective-permute-start.7 = (f32[1,640]{1,0:T(1,128)S(1)}, f32[1,640]{1,0:T(1,128)S(1)}, u32[]{:S(2)}, u32[]{:S(2)}) collective-permute-start(f32[1,640]{1,0:T(1,128)S(1)} %get-tuple-element.60), channel_id=1, source_target_pairs={{0,0},{1,9},{2,2},{3,11},{4,4},{5,13},{6,6},{7,15},{8,8},{9,1},{10... | collective-permute-start | bytes 7688 | tf_op jit(solution)/shard_map/ppermute | solution.py:516
  37.7 7.0 %collective-permute-start.8 = (f32[1,640]{1,0:T(1,128)S(1)}, f32[1,640]{1,0:T(1,128)S(1)}, u32[]{:S(2)}, u32[]{:S(2)}) collective-permute-start(f32[1,640]{1,0:T(1,128)S(1)} %get-tuple-element.61), channel_id=1, source_target_pairs={{0,1},{1,8},{2,3},{3,10},{4,5},{5,12},{6,7},{7,14},{8,9},{9,0},{10... | collective-permute-start | bytes 7688 | tf_op jit(solution)/shard_map/ppermute | solution.py:516
  44.7 0.3 collective-permute-start.10
  45.0 0.9 %collective-permute-done.8.refs_1_ = f32[1,640]{1,0:T(1,128)S(1)} collective-permute-done((f32[1,640]{1,0:T(1,128)S(1)}, f32[1,640]{1,0:T(1,128)S(1)}, u32[]{:S(2)}, u32[]{:S(2)}) %collective-permute-start.8) | collective-permute-done | bytes 2592 | tf_op jit(solution)/shard_map/ppermute | solution.py:516
  45.9 2.4 %collective-permute-done.9.refs_2_ = f32[1,640]{1,0:T(1,128)S(1)} collective-permute-done((f32[1,640]{1,0:T(1,128)S(1)}, f32[1,640]{1,0:T(1,128)S(1)}, u32[]{:S(2)}, u32[]{:S(2)}) %collective-permute-start.9) | collective-permute-done | bytes 2592 | tf_op jit(solution)/shard_map/ppermute | solution.py:516
  48.3 1.2 %collective-permute-done.10.refs_3_ = f32[1,640]{1,0:T(1,128)S(1)} collective-permute-done((f32[1,640]{1,0:T(1,128)S(1)}, f32[1,640]{1,0:T(1,128)S(1)}, u32[]{:S(2)}, u32[]{:S(2)}) %collective-permute-start.10) | collective-permute-done | bytes 2592 | tf_op jit(solution)/shard_map/ppermute | solution.py:516
  49.5 0.6 %finish.1 = (f32[1,512]{1,0:T(1,128)}, f32[1]{0:T(128)}) custom-call(f32[1,640]{1,0:T(1,128)S(1)} %collective-permute-done.7.refs_0_, f32[1,640]{1,0:T(1,128)S(1)} %collective-permute-done.8.refs_1_, f32[1,640]{1,0:T(1,128)S(1)} %collective-permute-done.9.refs_2_, f32[1,640]{1,0:T(1,128)S(1)} %collective-permute-done.10.refs_3_), custom_call_target="tpu_custom_call" | custom-call | tf_op jit(solution)/shard_map/finish/pallas_call | solution.py:427
  (10 shorter events, 0.0 us)
Async XLA Ops:
  0.6 0.7 %copy-start = (s32[2,1]{0,1:T(1,128)S(1)}, s32[2,1]{0,1:T(1,128)}, u32[]{:S(2)}) copy-start(s32[2,1]{0,1:T(1,128)} %param.5) | copy-start | bytes 28
  2.4 13.1 %collective-permute-start.1 = (bf16[256,1024]{1,0:T(8,128)(2,1)}, bf16[256,1024]{1,0:T(8,128)(2,1)S(1)}, u32[]{:S(2)}, u32[]{:S(2)}) collective-permute-start(bf16[256,1024]{1,0:T(8,128)(2,1)} %bitcast.acts_ref.refs_0_), channel_id=1, source_target_pairs={{0,1},{1,0},{2,3},{3,2},{4,5},{5,4},{6,7},{7,6},{8,9},{9,8},{10,11... | collective-permute-start | bytes 1572872 | tf_op jit(solution)/shard_map/ppermute | solution.py:449
  2.9 16.5 %collective-permute-start = (bf16[272,1024]{1,0:T(8,128)(2,1)S(1)}, bf16[272,1024]{1,0:T(8,128)(2,1)S(1)}, u32[]{:S(2)}, u32[]{:S(2)}) collective-permute-start(bf16[272,1024]{1,0:T(8,128)(2,1)S(1)} %with_digits.1), channel_id=1, source_target_pairs={{0,4},{4,0},{8,12},{12,8},{1,5},{5,1},{9,13},{13,9},{2,6},{6,2},{1... | collective-permute-start | bytes 1671176 | tf_op jit(solution)/shard_map/ppermute | solution.py:452
  5.6 9.9 %copy-start.1 = (s32[2,1]{0,1:T(1,128)S(1)}, s32[2,1]{0,1:T(1,128)}, u32[]{:S(2)}) copy-start(s32[2,1]{0,1:T(1,128)} %param.5) | copy-start | bytes 28
  5.6 24.4 %collective-permute-start.3 = (bf16[256,1024]{1,0:T(8,128)(2,1)}, bf16[256,1024]{1,0:T(8,128)(2,1)S(1)}, u32[]{:S(2)}, u32[]{:S(2)}) collective-permute-start(bf16[256,1024]{1,0:T(8,128)(2,1)} %bitcast.6), channel_id=1, source_target_pairs={{0,8},{12,4},{4,0},{8,12},{1,9},{13,5},{5,1},{9,13},{2,10},{14,6},... | collective-permute-start | bytes 1572872 | tf_op jit(solution)/shard_map/ppermute | solution.py:455
  8.1 21.9 %collective-permute-start.2 = (bf16[256,1024]{1,0:T(8,128)(2,1)}, bf16[256,1024]{1,0:T(8,128)(2,1)S(1)}, u32[]{:S(2)}, u32[]{:S(2)}) collective-permute-start(bf16[256,1024]{1,0:T(8,128)(2,1)} %bitcast.7), channel_id=1, source_target_pairs={{0,0},{4,8},{8,4},{12,12},{1,1},{5,9},{9,5},{13,13},{2,2},{6,10},{... | collective-permute-start | bytes 1572872 | tf_op jit(solution)/shard_map/ppermute | solution.py:453
  30.0 3.5 %collective-permute-start.4 = (bf16[272,1024]{1,0:T(8,128)(2,1)S(1)}, bf16[272,1024]{1,0:T(8,128)(2,1)S(1)}, u32[]{:S(2)}, u32[]{:S(2)}) collective-permute-start(bf16[272,1024]{1,0:T(8,128)(2,1)S(1)} %collective-permute-done.refs_0_.acts), channel_id=1, source_target_pairs={{0,1},{1,0},{2,3},{3,2},{4,5},{5,4},{6,7},{7,6},{8,9},{9,8},{10,11... | collective-permute-start | bytes 1671176 | tf_op jit(solution)/shard_map/ppermute | solution.py:449
  30.0 3.3 %collective-permute-start.5 = (bf16[256,1024]{1,0:T(8,128)(2,1)S(1)}, bf16[256,1024]{1,0:T(8,128)(2,1)S(1)}, u32[]{:S(2)}, u32[]{:S(2)}) collective-permute-start(bf16[256,1024]{1,0:T(8,128)(2,1)S(1)} %collective-permute-done.2.refs_7_), channel_id=1, source_target_pairs={{0,1},{1,0},{2,3},{3,2},{4,5},{5,4},{6,7},{7,6},{8,9},{9,8},{10,11... | collective-permute-start | bytes 1572872 | tf_op jit(solution)/shard_map/ppermute | solution.py:449
  30.5 2.9 %collective-permute-start.6 = (bf16[256,1024]{1,0:T(8,128)(2,1)S(1)}, bf16[256,1024]{1,0:T(8,128)(2,1)S(1)}, u32[]{:S(2)}, u32[]{:S(2)}) collective-permute-start(bf16[256,1024]{1,0:T(8,128)(2,1)S(1)} %collective-permute-done.3.refs_8_), channel_id=1, source_target_pairs={{0,1},{1,0},{2,3},{3,2},{4,5},{5,4},{6,7},{7,6},{8,9},{9,8},{10,11... | collective-permute-start | bytes 1572872 | tf_op jit(solution)/shard_map/ppermute | solution.py:449
  37.0 8.0 %collective-permute-start.7 = (f32[1,640]{1,0:T(1,128)S(1)}, f32[1,640]{1,0:T(1,128)S(1)}, u32[]{:S(2)}, u32[]{:S(2)}) collective-permute-start(f32[1,640]{1,0:T(1,128)S(1)} %get-tuple-element.60), channel_id=1, source_target_pairs={{0,0},{1,9},{2,2},{3,11},{4,4},{5,13},{6,6},{7,15},{8,8},{9,1},{10... | collective-permute-start | bytes 7688 | tf_op jit(solution)/shard_map/ppermute | solution.py:516
  37.7 8.2 %collective-permute-start.8 = (f32[1,640]{1,0:T(1,128)S(1)}, f32[1,640]{1,0:T(1,128)S(1)}, u32[]{:S(2)}, u32[]{:S(2)}) collective-permute-start(f32[1,640]{1,0:T(1,128)S(1)} %get-tuple-element.61), channel_id=1, source_target_pairs={{0,1},{1,8},{2,3},{3,10},{4,5},{5,12},{6,7},{7,14},{8,9},{9,0},{10... | collective-permute-start | bytes 7688 | tf_op jit(solution)/shard_map/ppermute | solution.py:516
  44.7 3.6 %collective-permute-start.9 = (f32[1,640]{1,0:T(1,128)S(1)}, f32[1,640]{1,0:T(1,128)S(1)}, u32[]{:S(2)}, u32[]{:S(2)}) collective-permute-start(f32[1,640]{1,0:T(1,128)S(1)} %get-tuple-element.62), channel_id=1, source_target_pairs={{0,4},{1,13},{2,6},{3,15},{4,0},{5,9},{6,2},{7,11},{8,12},{9,5},{1... | collective-permute-start | bytes 7688 | tf_op jit(solution)/shard_map/ppermute | solution.py:516
  44.7 4.8 %collective-permute-start.10 = (f32[1,640]{1,0:T(1,128)S(1)}, f32[1,640]{1,0:T(1,128)S(1)}, u32[]{:S(2)}, u32[]{:S(2)}) collective-permute-start(f32[1,640]{1,0:T(1,128)S(1)} %get-tuple-element.63), channel_id=1, source_target_pairs={{0,5},{1,12},{2,7},{3,14},{4,1},{5,8},{6,3},{7,10},{8,13},{9,4},{1... | collective-permute-start | bytes 7688 | tf_op jit(solution)/shard_map/ppermute | solution.py:516

commit v8 on v7

--- a/solution.py
+++ b/solution.py
@@ -469,11 +469,13 @@
             dims,
         )
         u_other = partner_left(made[2], other_acts, tokens)
-        other_acts, early_backs, late_backs, made, u_other = lax.optimization_barrier(
-            (other_acts, early_backs, late_backs, made, u_other)
+        other_acts, made = lax.optimization_barrier((other_acts, made))
+        other_pair = with_sibling(other_acts)
+        u_other = partner_left(made[2], other_acts, tokens)
+        early_backs, late_backs, u_other = lax.optimization_barrier(
+            (early_backs, late_backs, u_other)
         )
         early_pair = with_sibling(early_backs)
-        other_pair = with_sibling(other_acts)
         late_pair = with_sibling(late_backs)
         early_other, late_other, row_other = made
         cols = [early_own, early_other, late_own, late_other]

time: 50.4 us -> 49.9 us (0.990)
  waiting for transfers between devices: 6.5 us -> 5.87 us
  transfers between devices with their start and end apart: 11 -> 11, of which waited for: 5 -> 4; matrix products, arithmetic and copies ran while one was open for 0% -> 0% of each run, Pallas kernels for 42% -> 43%
where the time goes in v8:
time: 49.9 us; the launch traced here: 49.6 us
  Pallas kernels  26.4 us (53%)
  starting transfers between devices  16 us (32%)
  waiting for transfers between devices  5.87 us (12%)
  between operations  0.75 us (2%)
  local copies, waits for them, and re-layouts  0.65 us (1%)
    pallas_call x7, Pallas kernels, call(): pl.pallas_call(kernel, in_specs=[pl.BlockSpec(memory_space=space) for spa...  25.7 us
    ppermute x4, starting transfers between devices, on_device(): received.append(lax.ppermute(message, ('param', 'ex'), moves))  7.54 us
    ppermute x4, waiting for transfers between devices, on_device(): received.append(lax.ppermute(message, ('param', 'ex'), moves))  4.56 us
    ppermute x1, starting transfers between devices, on_device(): late_backs = lax.ppermute(backs, 'param', [(0, 2), (3, 1), (1, 0), (2, 3)])  2.87 us
    ppermute x1, starting transfers between devices, on_device(): other_acts = lax.ppermute(payload, 'param', swap)  2.65 us
    ppermute x1, starting transfers between devices, on_device(): early_backs = lax.ppermute(backs, 'param', [(0, 0), (1, 2), (2, 1), (3, 3)])  1.82 us
    ppermute x1, waiting for transfers between devices, on_device(): late_backs = lax.ppermute(backs, 'param', [(0, 2), (3, 1), (1, 0), (2, 3)])  1.3 us
    ppermute x4, starting transfers between devices, with_sibling(): return [array, lax.ppermute(array, 'ex', pairs)]  1.1 us
  transfers between devices with their start and end apart: 11, of which 4 were waited for; matrix products, arithmetic and copies ran while one was open for 0% of the time, Pallas kernels for 43%

profile of v8, /device:TPU:0, one launch (start us, length us, event | category | flops | bytes accessed | tf_op | source)
XLA Modules:
  0.0 49.6 jit_solution(4875656719198310908)
XLA Ops:
  0.6 0.0 copy-start
  0.6 0.6 %copy-done = s32[2,1]{0,1:T(1,128)S(1)} copy-done((s32[2,1]{0,1:T(1,128)S(1)}, s32[2,1]{0,1:T(1,128)}, u32[]{:S(2)}) %copy-start) | copy-done | bytes 32
  1.3 1.1 %with_digits.1 = bf16[272,1024]{1,0:T(8,128)(2,1)S(1)} custom-call(bf16[256,1024]{1,0:T(8,128)(2,1)} %bitcast.acts_ref.refs_0_, s32[2]{0:T(128)S(1)} %bitcast.3), custom_call_target="tpu_custom_call" | custom-call | tf_op jit(solution)/shard_map/with_digits/pallas_call | solution.py:136
  2.4 0.5 %collective-permute-start.1 = (bf16[256,1024]{1,0:T(8,128)(2,1)}, bf16[256,1024]{1,0:T(8,128)(2,1)S(1)}, u32[]{:S(2)}, u32[]{:S(2)}) collective-permute-start(bf16[256,1024]{1,0:T(8,128)(2,1)} %bitcast.acts_ref.refs_0_), channel_id=1, source_target_pairs={{0,1},{1,0},{2,3},{3,2},{4,5},{5,4},{6,7},{7,6},{8,9},{9,8},{10,11... | collective-permute-start | bytes 1572872 | tf_op jit(solution)/shard_map/ppermute | solution.py:449
  2.9 2.7 %collective-permute-start = (bf16[272,1024]{1,0:T(8,128)(2,1)S(1)}, bf16[272,1024]{1,0:T(8,128)(2,1)S(1)}, u32[]{:S(2)}, u32[]{:S(2)}) collective-permute-start(bf16[272,1024]{1,0:T(8,128)(2,1)S(1)} %with_digits.1), channel_id=1, source_target_pairs={{0,4},{4,0},{8,12},{12,8},{1,5},{5,1},{9,13},{13,9},{2,6},{6,2},{1... | collective-permute-start | bytes 1671176 | tf_op jit(solution)/shard_map/ppermute | solution.py:452
  5.6 1.8 %collective-permute-start.2 = (bf16[256,1024]{1,0:T(8,128)(2,1)}, bf16[256,1024]{1,0:T(8,128)(2,1)S(1)}, u32[]{:S(2)}, u32[]{:S(2)}) collective-permute-start(bf16[256,1024]{1,0:T(8,128)(2,1)} %bitcast.6), channel_id=1, source_target_pairs={{0,0},{4,8},{8,4},{12,12},{1,1},{5,9},{9,5},{13,13},{2,2},{6,10},{... | collective-permute-start | bytes 1572872 | tf_op jit(solution)/shard_map/ppermute | solution.py:453
  7.4 2.9 %collective-permute-start.3 = (bf16[256,1024]{1,0:T(8,128)(2,1)}, bf16[256,1024]{1,0:T(8,128)(2,1)S(1)}, u32[]{:S(2)}, u32[]{:S(2)}) collective-permute-start(bf16[256,1024]{1,0:T(8,128)(2,1)} %bitcast.7), channel_id=1, source_target_pairs={{0,8},{12,4},{4,0},{8,12},{1,9},{13,5},{5,1},{9,13},{2,10},{14,6},... | collective-permute-start | bytes 1572872 | tf_op jit(solution)/shard_map/ppermute | solution.py:455
  10.2 5.6 %ahead.2 = (bf16[1024,1024]{1,0:T(8,128)(2,1)S(1)}, bf16[1024,1024]{1,0:T(8,128)(2,1)S(1)}) custom-call(s32[2]{0:T(128)S(1)} %bitcast.4), custom_call_target="tpu_custom_call" | custom-call | flops 2097152000 | tf_op jit(solution)/shard_map/ahead/pallas_call | solution.py:136
  15.9 4.0 %left.1 = (f32[1024,512]{1,0:T(8,128)S(1)}, f32[2,256,256]{2,1,0:T(8,128)S(1)}) custom-call(s32[2]{0:T(128)S(1)} %bitcast.5, bf16[256,1024]{1,0:T(8,128)(2,1)} %bitcast.acts_ref.refs_0_, bf16[256,1024]{1,0:T(8,128)(2,1)S(1)} %collective-permute-done.1.refs_1_), custom_call_target="tpu_custom_call" | custom-call | flops 1048576000 | tf_op jit(solution)/shard_map/left/pallas_call | solution.py:136
  19.8 0.0 collective-permute-done.refs_0_.acts
  19.8 7.9 %ahead.3 = (bf16[1024,1024]{1,0:T(8,128)(2,1)S(1)}, bf16[1024,1024]{1,0:T(8,128)(2,1)S(1)}, bf16[1024,1024]{1,0:T(8,128)(2,1)S(1)}) custom-call(bf16[272,1024]{1,0:T(8,128)(2,1)S(1)} %collective-permute-done.refs_0_.acts), custom_call_target="tpu_custom_call" | custom-call | flops 3145728000 | tf_op jit(solution)/shard_map/ahead/pallas_call | solution.py:136
  27.7 0.1 collective-permute-start.4
  27.8 0.9 %partner_left.1 = (f32[1024,256]{1,0:T(8,128)S(1)}, f32[256,256]{1,0:T(8,128)S(1)}) custom-call(bf16[1024,1024]{1,0:T(8,128)(2,1)S(1)} %get-tuple-element.47.row_other.refs_5_, bf16[272,1024]{1,0:T(8,128)(2,1)S(1)} %collective-permute-done.refs_0_.acts), custom_call_target="tpu_custom_call" | custom-call | flops 1000000000 | tf_op jit(solution)/shard_map/partner_left/pallas_call | solution.py:136
  28.7 1.3 %collective-permute-done.3.refs_8_ = bf16[256,1024]{1,0:T(8,128)(2,1)S(1)} collective-permute-done((bf16[256,1024]{1,0:T(8,128)(2,1)}, bf16[256,1024]{1,0:T(8,128)(2,1)S(1)}, u32[]{:S(2)}, u32[]{:S(2)}) %collective-permute-start.3) | collective-permute-done | bytes 524320 | tf_op jit(solution)/shard_map/ppermute | solution.py:455
  30.0 0.5 %collective-permute-start.6 = (bf16[256,1024]{1,0:T(8,128)(2,1)S(1)}, bf16[256,1024]{1,0:T(8,128)(2,1)S(1)}, u32[]{:S(2)}, u32[]{:S(2)}) collective-permute-start(bf16[256,1024]{1,0:T(8,128)(2,1)S(1)} %collective-permute-done.3.refs_8_), channel_id=1, source_target_pairs={{0,1},{1,0},{2,3},{3,2},{4,5},{5,4},{6,7},{7,6},{8,9},{9,8},{10,11... | collective-permute-start | bytes 1572872 | tf_op jit(solution)/shard_map/ppermute | solution.py:449
  30.5 2.8 %one_example.2 = (f32[1,640]{1,0:T(1,128)S(1)}, f32[1,640]{1,0:T(1,128)S(1)}) custom-call(f32[1024,512]{1,0:T(8,128)S(1)} %get-tuple-element.38.refs_0_, bf16[1024,1024]{1,0:T(8,128)(2,1)S(1)} %get-tuple-element.39.refs_1_, bf16[1024,1024]{1,0:T(8,128)(2,1)S(1)} %get-tuple-element.44.refs_2_, bf16[1024,1024]{1,0:T(8,128)(2,1)S(1)} %get-tuple-element.45.refs_3_, ...), custom_call_target="tpu_custom_call" | custom-call | flops 4000000000 | tf_op jit(solution)/shard_map/one_example/pallas_call | solution.py:136
  33.4 3.5 %one_example.3 = (f32[1,640]{1,0:T(1,128)S(1)}, f32[1,640]{1,0:T(1,128)S(1)}) custom-call(f32[1024,512]{1,0:T(8,128)S(1)} %get-tuple-element.38.refs_0_, bf16[1024,1024]{1,0:T(8,128)(2,1)S(1)} %get-tuple-element.39.refs_1_, bf16[1024,1024]{1,0:T(8,128)(2,1)S(1)} %get-tuple-element.44.refs_2_, bf16[1024,1024]{1,0:T(8,128)(2,1)S(1)} %get-tuple-element.45.refs_3_, ...), custom_call_target="tpu_custom_call" | custom-call | flops 4000000000 | tf_op jit(solution)/shard_map/one_example/pallas_call | solution.py:136
  36.9 0.7 %collective-permute-start.7 = (f32[1,640]{1,0:T(1,128)S(1)}, f32[1,640]{1,0:T(1,128)S(1)}, u32[]{:S(2)}, u32[]{:S(2)}) collective-permute-start(f32[1,640]{1,0:T(1,128)S(1)} %get-tuple-element.60), channel_id=1, source_target_pairs={{0,0},{1,9},{2,2},{3,11},{4,4},{5,13},{6,6},{7,15},{8,8},{9,1},{10... | collective-permute-start | bytes 7688 | tf_op jit(solution)/shard_map/ppermute | solution.py:518
  37.5 6.6 %collective-permute-start.8 = (f32[1,640]{1,0:T(1,128)S(1)}, f32[1,640]{1,0:T(1,128)S(1)}, u32[]{:S(2)}, u32[]{:S(2)}) collective-permute-start(f32[1,640]{1,0:T(1,128)S(1)} %get-tuple-element.61), channel_id=1, source_target_pairs={{0,1},{1,8},{2,3},{3,10},{4,5},{5,12},{6,7},{7,14},{8,9},{9,0},{10... | collective-permute-start | bytes 7688 | tf_op jit(solution)/shard_map/ppermute | solution.py:518
  44.2 0.3 collective-permute-start.10
  44.4 0.9 %collective-permute-done.8.refs_1_ = f32[1,640]{1,0:T(1,128)S(1)} collective-permute-done((f32[1,640]{1,0:T(1,128)S(1)}, f32[1,640]{1,0:T(1,128)S(1)}, u32[]{:S(2)}, u32[]{:S(2)}) %collective-permute-start.8) | collective-permute-done | bytes 2592 | tf_op jit(solution)/shard_map/ppermute | solution.py:518
  45.3 2.4 %collective-permute-done.9.refs_2_ = f32[1,640]{1,0:T(1,128)S(1)} collective-permute-done((f32[1,640]{1,0:T(1,128)S(1)}, f32[1,640]{1,0:T(1,128)S(1)}, u32[]{:S(2)}, u32[]{:S(2)}) %collective-permute-start.9) | collective-permute-done | bytes 2592 | tf_op jit(solution)/shard_map/ppermute | solution.py:518
  47.8 1.2 %collective-permute-done.10.refs_3_ = f32[1,640]{1,0:T(1,128)S(1)} collective-permute-done((f32[1,640]{1,0:T(1,128)S(1)}, f32[1,640]{1,0:T(1,128)S(1)}, u32[]{:S(2)}, u32[]{:S(2)}) %collective-permute-start.10) | collective-permute-done | bytes 2592 | tf_op jit(solution)/shard_map/ppermute | solution.py:518
  49.0 0.6 %finish.1 = (f32[1,512]{1,0:T(1,128)}, f32[1]{0:T(128)}) custom-call(f32[1,640]{1,0:T(1,128)S(1)} %collective-permute-done.7.refs_0_, f32[1,640]{1,0:T(1,128)S(1)} %collective-permute-done.8.refs_1_, f32[1,640]{1,0:T(1,128)S(1)} %collective-permute-done.9.refs_2_, f32[1,640]{1,0:T(1,128)S(1)} %collective-permute-done.10.refs_3_), custom_call_target="tpu_custom_call" | custom-call | tf_op jit(solution)/shard_map/finish/pallas_call | solution.py:427
  (10 shorter events, 0.0 us)
Async XLA Ops:
  0.6 0.7 %copy-start = (s32[2,1]{0,1:T(1,128)S(1)}, s32[2,1]{0,1:T(1,128)}, u32[]{:S(2)}) copy-start(s32[2,1]{0,1:T(1,128)} %param.5) | copy-start | bytes 28
  2.4 13.5 %collective-permute-start.1 = (bf16[256,1024]{1,0:T(8,128)(2,1)}, bf16[256,1024]{1,0:T(8,128)(2,1)S(1)}, u32[]{:S(2)}, u32[]{:S(2)}) collective-permute-start(bf16[256,1024]{1,0:T(8,128)(2,1)} %bitcast.acts_ref.refs_0_), channel_id=1, source_target_pairs={{0,1},{1,0},{2,3},{3,2},{4,5},{5,4},{6,7},{7,6},{8,9},{9,8},{10,11... | collective-permute-start | bytes 1572872 | tf_op jit(solution)/shard_map/ppermute | solution.py:449
  2.9 16.9 %collective-permute-start = (bf16[272,1024]{1,0:T(8,128)(2,1)S(1)}, bf16[272,1024]{1,0:T(8,128)(2,1)S(1)}, u32[]{:S(2)}, u32[]{:S(2)}) collective-permute-start(bf16[272,1024]{1,0:T(8,128)(2,1)S(1)} %with_digits.1), channel_id=1, source_target_pairs={{0,4},{4,0},{8,12},{12,8},{1,5},{5,1},{9,13},{13,9},{2,6},{6,2},{1... | collective-permute-start | bytes 1671176 | tf_op jit(solution)/shard_map/ppermute | solution.py:452
  5.6 10.3 %copy-start.1 = (s32[2,1]{0,1:T(1,128)S(1)}, s32[2,1]{0,1:T(1,128)}, u32[]{:S(2)}) copy-start(s32[2,1]{0,1:T(1,128)} %param.5) | copy-start | bytes 28
  5.6 23.1 %collective-permute-start.2 = (bf16[256,1024]{1,0:T(8,128)(2,1)}, bf16[256,1024]{1,0:T(8,128)(2,1)S(1)}, u32[]{:S(2)}, u32[]{:S(2)}) collective-permute-start(bf16[256,1024]{1,0:T(8,128)(2,1)} %bitcast.6), channel_id=1, source_target_pairs={{0,0},{4,8},{8,4},{12,12},{1,1},{5,9},{9,5},{13,13},{2,2},{6,10},{... | collective-permute-start | bytes 1572872 | tf_op jit(solution)/shard_map/ppermute | solution.py:453
  7.4 22.6 %collective-permute-start.3 = (bf16[256,1024]{1,0:T(8,128)(2,1)}, bf16[256,1024]{1,0:T(8,128)(2,1)S(1)}, u32[]{:S(2)}, u32[]{:S(2)}) collective-permute-start(bf16[256,1024]{1,0:T(8,128)(2,1)} %bitcast.7), channel_id=1, source_target_pairs={{0,8},{12,4},{4,0},{8,12},{1,9},{13,5},{5,1},{9,13},{2,10},{14,6},... | collective-permute-start | bytes 1572872 | tf_op jit(solution)/shard_map/ppermute | solution.py:455
  27.7 5.6 %collective-permute-start.4 = (bf16[272,1024]{1,0:T(8,128)(2,1)S(1)}, bf16[272,1024]{1,0:T(8,128)(2,1)S(1)}, u32[]{:S(2)}, u32[]{:S(2)}) collective-permute-start(bf16[272,1024]{1,0:T(8,128)(2,1)S(1)} %collective-permute-done.refs_0_.acts), channel_id=1, source_target_pairs={{0,1},{1,0},{2,3},{3,2},{4,5},{5,4},{6,7},{7,6},{8,9},{9,8},{10,11... | collective-permute-start | bytes 1671176 | tf_op jit(solution)/shard_map/ppermute | solution.py:449
  30.0 3.3 %collective-permute-start.5 = (bf16[256,1024]{1,0:T(8,128)(2,1)S(1)}, bf16[256,1024]{1,0:T(8,128)(2,1)S(1)}, u32[]{:S(2)}, u32[]{:S(2)}) collective-permute-start(bf16[256,1024]{1,0:T(8,128)(2,1)S(1)} %collective-permute-done.2.refs_7_), channel_id=1, source_target_pairs={{0,1},{1,0},{2,3},{3,2},{4,5},{5,4},{6,7},{7,6},{8,9},{9,8},{10,11... | collective-permute-start | bytes 1572872 | tf_op jit(solution)/shard_map/ppermute | solution.py:449
  30.0 3.3 %collective-permute-start.6 = (bf16[256,1024]{1,0:T(8,128)(2,1)S(1)}, bf16[256,1024]{1,0:T(8,128)(2,1)S(1)}, u32[]{:S(2)}, u32[]{:S(2)}) collective-permute-start(bf16[256,1024]{1,0:T(8,128)(2,1)S(1)} %collective-permute-done.3.refs_8_), channel_id=1, source_target_pairs={{0,1},{1,0},{2,3},{3,2},{4,5},{5,4},{6,7},{7,6},{8,9},{9,8},{10,11... | collective-permute-start | bytes 1572872 | tf_op jit(solution)/shard_map/ppermute | solution.py:449
  36.9 7.6 %collective-permute-start.7 = (f32[1,640]{1,0:T(1,128)S(1)}, f32[1,640]{1,0:T(1,128)S(1)}, u32[]{:S(2)}, u32[]{:S(2)}) collective-permute-start(f32[1,640]{1,0:T(1,128)S(1)} %get-tuple-element.60), channel_id=1, source_target_pairs={{0,0},{1,9},{2,2},{3,11},{4,4},{5,13},{6,6},{7,15},{8,8},{9,1},{10... | collective-permute-start | bytes 7688 | tf_op jit(solution)/shard_map/ppermute | solution.py:518
  37.5 7.8 %collective-permute-start.8 = (f32[1,640]{1,0:T(1,128)S(1)}, f32[1,640]{1,0:T(1,128)S(1)}, u32[]{:S(2)}, u32[]{:S(2)}) collective-permute-start(f32[1,640]{1,0:T(1,128)S(1)} %get-tuple-element.61), channel_id=1, source_target_pairs={{0,1},{1,8},{2,3},{3,10},{4,5},{5,12},{6,7},{7,14},{8,9},{9,0},{10... | collective-permute-start | bytes 7688 | tf_op jit(solution)/shard_map/ppermute | solution.py:518
  44.2 3.6 %collective-permute-start.9 = (f32[1,640]{1,0:T(1,128)S(1)}, f32[1,640]{1,0:T(1,128)S(1)}, u32[]{:S(2)}, u32[]{:S(2)}) collective-permute-start(f32[1,640]{1,0:T(1,128)S(1)} %get-tuple-element.62), channel_id=1, source_target_pairs={{0,4},{1,13},{2,6},{3,15},{4,0},{5,9},{6,2},{7,11},{8,12},{9,5},{1... | collective-permute-start | bytes 7688 | tf_op jit(solution)/shard_map/ppermute | solution.py:518
  44.2 4.8 %collective-permute-start.10 = (f32[1,640]{1,0:T(1,128)S(1)}, f32[1,640]{1,0:T(1,128)S(1)}, u32[]{:S(2)}, u32[]{:S(2)}) collective-permute-start(f32[1,640]{1,0:T(1,128)S(1)} %get-tuple-element.63), channel_id=1, source_target_pairs={{0,5},{1,12},{2,7},{3,14},{4,1},{5,8},{6,3},{7,10},{8,13},{9,4},{1... | collective-permute-start | bytes 7688 | tf_op jit(solution)/shard_map/ppermute | solution.py:518
